TPU v7x, 32 devices: a whole 2x2x4 slice. The times are simulated.
32 devices in a mesh: seq: 8 (over y, x, core), head: 4 (over z).
Axes of the slice: x: 2, y: 2, z: 4, core: 2. Of those that a mesh axis runs over, the one named last changes fastest.
Arguments:
- lin_qkv: bfloat16 [2048, 3, 4096], P('seq', None, 'head'), may hold values from -6 to 6
- resid: bfloat16 [2048, 4096], P('seq', 'head'), may hold values from -6 to 6
- w_out: bfloat16 [4096, 4096], P('head'), may hold values from -0.125 to 0.125
- w_qkv: bfloat16 [4096, 3, 4096], P(None, None, 'head'), may hold values from -2 to 2
Outputs:
- hidden: bfloat16 [2048, 4096], P('seq', 'head')
- attended: bfloat16 [2048, 4096], P('seq', 'head')
All inputs are finite; a program needn't handle non-finite values.
Results may differ from a plain program's by a relative error of at most 0.025.
Values may be sent and summed in bfloat16 or wider, within the bound.
No kernel may reach another device: no remote copies, remote signals or barrier semaphores. Data moves between devices by JAX's collectives and lax.ppermute only.
A program may use at most 128 MiB of HBM per device.

v0:
```python
import math

import jax
import jax.numpy as jnp
from jax import lax
from jax.sharding import PartitionSpec as P

D = 4096
HD = 128


def shifted(array, axis, by):
    devices = lax.axis_size(axis)
    pairs = [(i, i + by) for i in range(devices) if 0 <= i + by < devices]
    return lax.ppermute(array, axis, pairs)


def rotary(values, positions):
    half = values.shape[-1] // 2
    freq = 500000.0 ** (-(jnp.arange(half, dtype=jnp.float32) * 2.0 / values.shape[-1]))
    angle = positions.astype(jnp.float32)[:, None] * freq[None, :]
    cosine = jnp.cos(angle)[:, None, :]
    sine = jnp.sin(angle)[:, None, :]
    first = values[..., :half]
    second = values[..., half:]
    return jnp.concatenate(
        [first * cosine - second * sine, second * cosine + first * sine], axis=-1
    )


def local(lin_qkv, resid, w_out, w_qkv):
    tok_rows = lin_qkv.shape[0]
    local_width = lin_qkv.shape[2]
    nheads = local_width // HD
    n_seq = lax.axis_size("seq")
    own_index = lax.axis_index("seq")
    queries = lin_qkv[:, 0].reshape(tok_rows, nheads, HD)
    keys = lin_qkv[:, 1].reshape(tok_rows, nheads, HD)
    values = lin_qkv[:, 2].reshape(tok_rows, nheads, HD)
    own_state = jnp.einsum("thd,the->hde", keys, values, preferred_element_type=jnp.float32)
    piece = lax.all_gather(own_state[None], "seq", axis=0, tiled=True)
    keep = (jnp.arange(piece.shape[0], dtype=jnp.int32) < own_index).astype(jnp.float32)
    before = jnp.sum(piece * keep[:, None, None, None], axis=0)
    before = before.astype(jnp.bfloat16)
    causal = jnp.tril(jnp.ones((tok_rows, tok_rows), dtype=bool))
    scores = jnp.einsum("thd,shd->hts", queries, keys, preferred_element_type=jnp.float32)
    inner = jnp.where(causal[None], scores, 0.0).astype(jnp.bfloat16)
    total = jnp.einsum("hts,shd->thd", inner, values, preferred_element_type=jnp.float32)
    total = total + jnp.einsum("thd,hde->the", queries, before, preferred_element_type=jnp.float32)
    scale = 1.0 / math.sqrt(HD * tok_rows * n_seq)
    lin_out = (total * scale).astype(jnp.bfloat16).reshape(tok_rows, local_width)
    shared = lax.psum_scatter(
        lax.dot_general(
            w_out, lin_out, (((0,), (1,)), ((), ())), preferred_element_type=jnp.float32
        ).astype(jnp.bfloat16),
        "head",
        scatter_dimension=0,
        tiled=True,
    ).astype(jnp.float32)
    mixed_f = resid.astype(jnp.float32) + shared.T
    hidden = mixed_f.astype(jnp.bfloat16)
    flat_w = w_qkv.reshape(w_qkv.shape[0], 3 * local_width)
    squared = lax.psum(jnp.sum(mixed_f * mixed_f, axis=1), "head")
    normed = (mixed_f * lax.rsqrt(squared[:, None] / D + 1e-05)).astype(jnp.bfloat16)
    proj = jnp.dot(
        lax.all_gather(normed, "head", axis=1, tiled=True),
        flat_w,
        preferred_element_type=jnp.float32,
    )
    proj = proj.reshape(tok_rows, 3, nheads, HD)
    positions = own_index * tok_rows + jnp.arange(tok_rows, dtype=jnp.int32)
    query2 = rotary(proj[:, 0], positions).astype(jnp.bfloat16)
    key2 = rotary(proj[:, 1], positions).astype(jnp.bfloat16)
    value2 = proj[:, 2].astype(jnp.bfloat16)
    key_prev, value_prev = shifted((key2, value2), "seq", 1)
    score_scale = 1.0 / math.sqrt(HD)
    all_keys = jnp.concatenate([key_prev, key2], axis=0)
    all_values = jnp.concatenate([value_prev, value2], axis=0)
    logits = (
        jnp.einsum("thd,shd->hts", query2, all_keys, preferred_element_type=jnp.float32)
        * score_scale
    )
    allowed = jnp.concatenate([jnp.full((tok_rows, tok_rows), own_index > 0), causal], axis=1)
    logits = jnp.where(allowed[None], logits, -1e30)
    top = jnp.max(logits, axis=2, keepdims=True)
    expo = jnp.where(allowed[None], jnp.exp(logits - top), 0.0)
    weights = (expo / jnp.sum(expo, axis=2, keepdims=True)).astype(jnp.bfloat16)
    attended = jnp.einsum("hts,shd->thd", weights, all_values, preferred_element_type=jnp.float32)
    return (hidden, attended.astype(jnp.bfloat16).reshape(tok_rows, local_width))


def solution(mesh):
    return jax.shard_map(
        local,
        mesh=mesh,
        in_specs=(P("seq", None, "head"), P("seq", "head"), P("head", None), P(None, None, "head")),
        out_specs=(P("seq", "head"), P("seq", "head")),
        check_vma=False,
    )
```

profile of v0, /device:TPU:4, one launch (start us, length us, event | category | flops | bytes accessed | tf_op | source)
XLA Modules:
  0.0 201.0 jit_solution(18130497831580187959)
XLA Ops:
  7.2 0.0 all-gather.6.cloned.1.call-start
  7.2 1.5 fusion.37
  8.7 0.2 copy.53
  8.9 0.2 copy.36
  9.1 1.1 fusion.39
  10.2 0.0 all-gather.6.cloned.1.call-update
  10.2 0.0 reduce-scatter.2.cloned.1.call-start
  10.3 0.2 copy.52
  10.5 37.7 %all-gather.6.cloned.1.call-done = f32[64,128,128]{2,1,0:T(8,128)} async-done(((f32[8,128,128]{2,1,0:T(8,128)}), f32[64,128,128]{2,1,0:T(8,128)}) %all-gather.6.cloned.1.call-update) | async-done | bytes 4194320 | tf_op jit(solution)/shard_map/all_gather | solution.py:41
  48.3 2.7 %multiply_reduce_fusion = bf16[8,128,128]{2,1,0:T(8,128)(2,1)S(1)} fusion(f32[8,8,128,128]{3,2,1,0:T(8,128)} %bitcast.55, f32[8]{0:T(128)S(1)} %compare_convert_fusion), kind=kLoop, calls=%fused_computation.6 | loop fusion | flops 1966080 | bytes 4456480 | tf_op jit(solution)/shard_map/reduce_sum | solution.py:43
  50.9 0.4 convolution_bitcast_fusion
  51.3 0.8 fusion.13
  52.1 0.0 copy-start.1
  52.1 7.2 %fusion.1 = bf16[4096,256]{0,1:T(8,128)(2,1)} fusion(bf16[256,1024]{0,1:T(8,128)(2,1)S(1)} %bitcast.62, bf16[1024,4096]{1,0:T(8,128)(2,1)} %param.6), kind=kOutput, calls=%fused_computation.2 | convolution fusion | flops 2148532224 | bytes 11010048 | tf_op jit(solution)/shard_map/dot_general | solution.py:53
  59.3 0.0 reduce-scatter.2.cloned.1.call-update
  59.3 0.0 all-gather.4.cloned.1.call-start
  59.3 44.1 %reduce-scatter.2.cloned.1.call-done = bf16[1024,256]{0,1:T(8,128)(2,1)} async-done(((bf16[4096,256]{0,1:T(8,128)(2,1)}), bf16[1024,256]{0,1:T(8,128)(2,1)}) %reduce-scatter.2.cloned.1.call-update) | async-done | bytes 524304 | tf_op jit(solution)/shard_map/reduce_scatter | solution.py:52
  103.5 0.0 copy-done.1
  103.5 1.3 multiply_reduce_fusion.1
  104.8 10.0 %psum.7 = f32[256]{0:T(256)S(1)} all-reduce(f32[256]{0:T(256)S(1)} %multiply_reduce_fusion.1), channel_id=1, replica_groups=mesh['seq'=8,'head'=4] {'head'}, use_global_device_ids=true, to_apply=%region_3.4 | all-reduce | flops 256 | bytes 2048 | tf_op jit(solution)/shard_map/psum | solution.py:63
  114.8 2.2 %multiply_convert_fusion = (bf16[256,1024]{1,0:T(8,128)(2,1)}, bf16[256,1024]{1,0:T(8,128)(2,1)}) fusion(bf16[1024,256]{0,1:T(8,128)(2,1)} %reduce-scatter.2.cloned.1.call-done, bf16[256,1024]{1,0:T(8,128)(2,1)S(1)} %copy-done.1, f32[256]{0:T(256)S(1)} %add_rsqrt_fusion), kind=kLoop, calls=%fused_computation.35 | loop fusion | flops 1572864 | bytes 2098176 | tf_op jit(solution)/shard_map/convert_element_type | solution.py:64
  117.0 0.0 all-gather.4.cloned.1.call-update
  117.0 33.4 %copy.40 = bf16[4096,3,1024]{0,2,1:T(8,128)(2,1)} copy(bf16[4096,3,1024]{2,0,1:T(8,128)(2,1)} %param.7) | data formatting | bytes 50331648 | tf_op args[3]
  150.5 0.3 multiply_cosine_fusion
  150.8 10.5 %all-gather.4.cloned.1.call-done = bf16[256,4096]{1,0:T(8,128)(2,1)} async-done(((bf16[256,1024]{1,0:T(8,128)(2,1)}), bf16[256,4096]{1,0:T(8,128)(2,1)}) %all-gather.4.cloned.1.call-update) | async-done | bytes 2097168 | tf_op jit(solution)/shard_map/all_gather | solution.py:66
  161.2 12.5 %fusion.3 = f32[256,3,8,128]{0,3,2,1:T(8,128)S(1)} fusion(bf16[3,8,128,4096]{3,2,1,0:T(8,128)(2,1)} %bitcast.54, bf16[256,4096]{1,0:T(8,128)(2,1)} %all-gather.4.cloned.1.call-done), kind=kOutput, calls=%fused_computation.8 | convolution fusion | flops 6442450944 | bytes 30408704 | tf_op jit(solution)/shard_map/dot_general | solution.py:65
  173.8 0.0 copy-start
  173.8 0.1 slice_bitcast_fusion.1
  174.0 0.3 subtract_convert_fusion.1
  174.3 1.1 copy-done
  175.5 1.9 collective-permute-start.1
  177.4 1.3 fusion.27
  178.7 3.6 %collective-permute-start = (bf16[256,8,128]{0,2,1:T(8,128)(2,1)S(1)}, bf16[256,8,128]{0,2,1:T(8,128)(2,1)S(1)}, u32[]{:S(2)}, u32[]{:S(2)}) collective-permute-start(bf16[256,8,128]{0,2,1:T(8,128)(2,1)S(1)} %fusion.27), channel_id=1, source_target_pairs={{0,4},{4,8},{8,12},{12,16},{16,20},{20,24},{24,28},{1,5},{5,9},{9,... | collective-permute-start | bytes 1572872 | tf_op jit(solution)/shard_map/ppermute | solution.py:15
  182.4 4.5 %collective-permute-done.1 = bf16[256,8,128]{0,2,1:T(8,128)(2,1)S(1)} collective-permute-done((bf16[256,8,128]{0,2,1:T(8,128)(2,1)S(1)}, bf16[256,8,128]{0,2,1:T(8,128)(2,1)S(1)}, u32[]{:S(2)}, u32[]{:S(2)}) %collective-permute-start.1) | collective-permute-done | bytes 524320 | tf_op jit(solution)/shard_map/ppermute | solution.py:15
  186.8 0.8 fusion.18
  187.6 2.4 %fusion.38 = (f32[8,256]{1,0:T(8,128)S(1)}, f32[8,256,512]{2,1,0:T(8,128)S(1)}) fusion(f32[8,256,512]{2,1,0:T(8,128)S(1)} %fusion.18, pred[256,512]{1,0:T(8,128)(4,1)S(1)} %concatenate.18), kind=kOutput, calls=%fused_computation.63 | output fusion | flops 7340543 | bytes 8527872 | tf_op jit(solution)/shard_map/sub | solution.py:86
  190.0 2.5 %collective-permute-done = bf16[256,8,128]{0,2,1:T(8,128)(2,1)S(1)} collective-permute-done((bf16[256,8,128]{0,2,1:T(8,128)(2,1)S(1)}, bf16[256,8,128]{0,2,1:T(8,128)(2,1)S(1)}, u32[]{:S(2)}, u32[]{:S(2)}) %collective-permute-start) | collective-permute-done | bytes 524320 | tf_op jit(solution)/shard_map/ppermute | solution.py:15
  192.5 1.0 fusion.14
  193.4 1.0 copy.43
  (7 shorter events, 0.1 us)
Async XLA Ops:
  7.2 41.1 %all-gather.6.cloned.1.call-start = ((), (), s32[]{:S(2)}) async-start(), calls=%async_computation.3 | async-start | bytes 4718592 | tf_op jit(solution)/shard_map/all_gather | solution.py:41
  10.2 93.2 %reduce-scatter.2.cloned.1.call-start = ((), (), s32[]{:S(2)}) async-start(), calls=%async_computation.1 | async-start | bytes 2621440 | tf_op jit(solution)/shard_map/reduce_scatter | solution.py:52
  52.1 51.4 %copy-start.1 = (bf16[256,1024]{1,0:T(8,128)(2,1)S(1)}, bf16[256,1024]{1,0:T(8,128)(2,1)}, u32[]{:S(2)}) copy-start(bf16[256,1024]{1,0:T(8,128)(2,1)} %param.5) | copy-start | bytes 1572868
  59.3 102.0 %all-gather.4.cloned.1.call-start = ((), (), s32[]{:S(2)}) async-start(), calls=%async_computation.2 | async-start | bytes 2621440 | tf_op jit(solution)/shard_map/all_gather | solution.py:66
  173.8 1.7 copy-start
  175.5 11.4 %collective-permute-start.1 = (bf16[256,8,128]{0,2,1:T(8,128)(2,1)S(1)}, bf16[256,8,128]{0,2,1:T(8,128)(2,1)S(1)}, u32[]{:S(2)}, u32[]{:S(2)}) collective-permute-start(bf16[256,8,128]{0,2,1:T(8,128)(2,1)S(1)} %pad_maximum_fusion), channel_id=1, source_target_pairs={{0,4},{4,8},{8,12},{12,16},{16,20},{20,24},{24,28},{1,5},{5,9},{9,... | collective-permute-start | bytes 1572872 | tf_op jit(solution)/shard_map/ppermute | solution.py:15
  178.7 13.8 %collective-permute-start = (bf16[256,8,128]{0,2,1:T(8,128)(2,1)S(1)}, bf16[256,8,128]{0,2,1:T(8,128)(2,1)S(1)}, u32[]{:S(2)}, u32[]{:S(2)}) collective-permute-start(bf16[256,8,128]{0,2,1:T(8,128)(2,1)S(1)} %fusion.27), channel_id=1, source_target_pairs={{0,4},{4,8},{8,12},{12,16},{16,20},{20,24},{24,28},{1,5},{5,9},{9,... | collective-permute-start | bytes 1572872 | tf_op jit(solution)/shard_map/ppermute | solution.py:15
Sparse Core Ops, SparseCore 0:
  10.5 37.7 all-gather.5
  59.4 44.0 reduce-scatter.1
  117.1 44.0 all-gather.3
where the time goes:
time: 202 us; the launch traced here: 201 us
  waiting for transfers between devices  99.3 us (49%)
  local copies, waits for them, and re-layouts  39.1 us (19%)
  matrix products  23.6 us (12%)
  between operations  13.9 us (7%)
  blocking collectives  10 us (5%)
  other arithmetic  9.29 us (5%)
  starting transfers between devices  5.68 us (3%)
    reduce_scatter x1, waiting for transfers between devices, local(): lax.psum_scatter(lax.dot_general(w_out, lin_out, (((0,), (1,)), ((), ()))...  44.1 us
    all_gather x1, waiting for transfers between devices, local(): piece = lax.all_gather(own_state[None], 'seq', axis=0, tiled=True)  37.7 us
    unnamed x8, local copies, waits for them, and re-layouts  36 us
    dot_general x1, matrix products, local(): jnp.dot(lax.all_gather(normed, 'head', axis=1, tiled=True), flat_w, prefe...  12.5 us
    all_gather x1, waiting for transfers between devices, local(): lax.all_gather(normed, 'head', axis=1, tiled=True)  10.5 us
    psum x1, blocking collectives, local(): squared = lax.psum(jnp.sum(mixed_f * mixed_f, axis=1), 'head')  10 us
    dot_general x1, matrix products, local(): lax.dot_general(w_out, lin_out, (((0,), (1,)), ((), ())), preferred_eleme...  7.16 us
    ppermute x2, waiting for transfers between devices, shifted(): return lax.ppermute(array, axis, pairs)  6.94 us
  transfers between devices with their start and end apart: 5, of which 5 were waited for; matrix products, arithmetic and copies ran while one was open for 19% of the time, Pallas kernels for 0%

commit v1 on v0

--- a/solution.py
+++ b/solution.py
@@ -1,18 +1,31 @@
+import functools
 import math
 
 import jax
 import jax.numpy as jnp
 from jax import lax
+from jax.experimental import pallas as pl
+from jax.experimental.pallas import tpu as pltpu
 from jax.sharding import PartitionSpec as P
 
 D = 4096
 HD = 128
+BF16 = jnp.bfloat16
+F32 = jnp.float32
+NEG = -1e30
+
+PAIR = [(0, 1), (1, 0), (2, 3), (3, 2)]
+CROSS = [(0, 3), (3, 0), (1, 2), (2, 1)]
 
 
 def shifted(array, axis, by):
     devices = lax.axis_size(axis)
     pairs = [(i, i + by) for i in range(devices) if 0 <= i + by < devices]
     return lax.ppermute(array, axis, pairs)
+
+
+def swapped(array, axis, bits):
+    return lax.ppermute(array, axis, [(i, i ^ bits) for i in range(lax.axis_size(axis))])
 
 
 def rotary(values, positions):
@@ -28,7 +41,7 @@
     )
 
 
-def local(lin_qkv, resid, w_out, w_qkv):
+def general(lin_qkv, resid, w_out, w_qkv):
     tok_rows = lin_qkv.shape[0]
     local_width = lin_qkv.shape[2]
     nheads = local_width // HD
@@ -89,9 +102,293 @@
     return (hidden, attended.astype(jnp.bfloat16).reshape(tok_rows, local_width))
 
 
+def dot(a, b):
+    return jnp.dot(a, b, preferred_element_type=F32)
+
+
+def dot_nt(a, b):
+    return lax.dot_general(a, b, (((1,), (1,)), ((), ())), preferred_element_type=F32)
+
+
+def dot_tn(a, b):
+    return lax.dot_general(a, b, (((0,), (0,)), ((), ())), preferred_element_type=F32)
+
+
+def head_at(index):
+    return pl.ds(pl.multiple_of(index * HD, HD), HD)
+
+
+def call(body, grid, ins, in_specs, outs, out_specs, scalars=None, scratch=(), vmem=32, flops=0, moved=0):
+    return pl.pallas_call(
+        body,
+        grid_spec=pltpu.PrefetchScalarGridSpec(
+            num_scalar_prefetch=1,
+            grid=grid,
+            in_specs=in_specs,
+            out_specs=out_specs,
+            scratch_shapes=scratch,
+        ),
+        out_shape=outs,
+        compiler_params=pltpu.CompilerParams(vmem_limit_bytes=vmem * 2**20),
+        cost_estimate=pl.CostEstimate(flops=flops, bytes_accessed=moved, transcendentals=0),
+    )(scalars, *ins)
+
+
+def whole(shape):
+    return pl.BlockSpec(shape, lambda *_: (0,) * len(shape))
+
+
+def part(index, rows, width):
+    return pl.BlockSpec((None, rows, width), lambda *_: (index, 0, 0))
+
+
+def state_body(s_ref, k_ref, v_ref, send_ref, keep_ref):
+    core = s_ref[0]
+    count = send_ref.shape[0]
+    for j in range(count):
+        for ref, group in ((send_ref, 1 - core), (keep_ref, core)):
+            at = head_at(group * count + j)
+            ref[j] = dot_tn(k_ref[:, at], v_ref[:, at]).astype(BF16)
+
+
+def intra_body(s_ref, q_ref, k_ref, v_ref, o_ref):
+    rows = q_ref.shape[0]
+    ahead = lax.broadcasted_iota(jnp.int32, (rows, rows), 1) > lax.broadcasted_iota(
+        jnp.int32, (rows, rows), 0
+    )
+    for h in range(q_ref.shape[1] // HD):
+        at = slice(h * HD, (h + 1) * HD)
+        scores = dot_nt(q_ref[:, at], k_ref[:, at])
+        inner = jnp.where(ahead, 0.0, scores).astype(BF16)
+        o_ref[:, at] = dot(inner, v_ref[:, at])
+
+
+def send_body(scale, s_ref, q_ref, intra_ref, own_ref, other_ref, w_ref, lin_ref, a_ref, b_ref):
+    core = s_ref[0]
+    count = own_ref.shape[0]
+
+    @pl.when(pl.program_id(0) == 0)
+    def _():
+        for j in range(count):
+            for ref, group in ((own_ref, core), (other_ref, 1 - core)):
+                at = head_at(group * count + j)
+                total = intra_ref[:, at] + dot(q_ref[:, at], ref[j])
+                lin_ref[:, at] = (total * scale).astype(BF16)
+
+    half = a_ref.shape[0]
+    product = dot(lin_ref[...], w_ref[...]).astype(BF16)
+    a_ref[...] = product[:half]
+    b_ref[...] = product[half:]
+
+
+def mine_body(per, s_ref, lin_ref, w_ref, r_ref, a_ref, b_ref):
+    own = s_ref[4 + pl.program_id(0) // per] == s_ref[1]
+    half = a_ref.shape[0]
+    product = dot(lin_ref[...], w_ref[...])
+    product = product + jnp.where(own, r_ref[...].astype(F32), 0.0)
+    product = product.astype(BF16)
+    a_ref[...] = product[:half]
+    b_ref[...] = product[half:]
+
+
+def first_body(s_ref, x_ref, w_ref, acc_ref):
+    j, k = pl.program_id(0), pl.program_id(1)
+
+    @pl.when(k == 0)
+    def _():
+        acc_ref[...] = dot(x_ref[...], w_ref[...])
+
+    @pl.when(k > 0)
+    def _():
+        acc_ref[...] += dot(x_ref[...], w_ref[...])
+
+
+def second_body(s_ref, x_ref, w_ref, in_ref, t_ref, o_ref, cos_ref, sin_ref, out_ref, acc, inv):
+    j, k = pl.program_id(0), pl.program_id(1)
+
+    @pl.when((j == 0) & (k == 0))
+    def _():
+        t = t_ref[...].astype(F32)
+        o = o_ref[...].astype(F32)
+        total = jnp.sum(t * t + o * o, axis=1, keepdims=True)
+        inv[...] = jnp.broadcast_to(lax.rsqrt(total / D + 1e-05), inv.shape)
+
+    @pl.when(k == 0)
+    def _():
+        acc[...] = in_ref[...] + dot(x_ref[...], w_ref[...])
+
+    @pl.when(k == pl.num_programs(1) - 1)
+    def _():
+        cos, sin = cos_ref[...], sin_ref[...]
+        for h in range(acc.shape[1] // HD):
+            at = slice(h * HD, (h + 1) * HD)
+            value = (acc[:, at] + dot(x_ref[...], w_ref[:, at])) * inv[...]
+            turned = value * cos + pltpu.roll(value, HD // 2, 1) * sin
+            out_ref[:, at] = jnp.where(j == 1, value, turned).astype(BF16)
+
+
+def attend_body(s_ref, qa_ref, qb_ref, a_ref, b_ref, pa_ref, pb_ref, out_ref):
+    has_prev = s_ref[6] > 0
+    half = qa_ref.shape[0]
+    rows = 2 * half
+    row = lax.broadcasted_iota(jnp.int32, (rows, 2 * rows), 0)
+    col = lax.broadcasted_iota(jnp.int32, (rows, 2 * rows), 1)
+    allowed = ((col < rows) & has_prev) | ((col >= rows) & (col - rows <= row))
+    for h in range(qa_ref.shape[1] // HD):
+        at = slice(h * HD, (h + 1) * HD)
+        queries = jnp.concatenate([qa_ref[:, at], qb_ref[:, at]], axis=0)
+        keys = jnp.concatenate([r[0, :, at] for r in (pa_ref, pb_ref, a_ref, b_ref)], axis=0)
+        values = jnp.concatenate([r[1, :, at] for r in (pa_ref, pb_ref, a_ref, b_ref)], axis=0)
+        logits = dot_nt(queries, keys) * (1.0 / math.sqrt(HD))
+        logits = jnp.where(allowed, logits, NEG)
+        top = jnp.max(logits, axis=1, keepdims=True)
+        expo = jnp.where(allowed, jnp.exp(logits - top), 0.0)
+        weights = (expo / jnp.sum(expo, axis=1, keepdims=True)).astype(BF16)
+        out_ref[:, at] = dot(weights, values).astype(BF16)
+
+
+def tuned(lin_qkv, resid, w_out, w_qkv):
+    rows, _, width = lin_qkv.shape
+    nheads = width // HD
+    half = rows // 2
+    group = nheads // 2
+    full = w_out.shape[1]
+    seq = lax.axis_index("seq").astype(jnp.int32)
+    z = lax.axis_index("head").astype(jnp.int32)
+    core = seq % 2
+    edge = (z == 0) | (z == 3)
+    order = jnp.where(edge, jnp.array([1, 2, 0, 3], jnp.int32), jnp.array([0, 3, 1, 2], jnp.int32))
+    scalars = jnp.concatenate([jnp.stack([core, z]), order, jnp.stack([seq, z // 2])])
+
+    qkv = jnp.transpose(lin_qkv, (1, 0, 2))
+    wqkv = jnp.transpose(w_qkv, (1, 0, 2))
+    heads = lambda n: jax.ShapeDtypeStruct((n, HD, HD), BF16)
+    q_spec, k_spec, v_spec = (part(i, rows, width) for i in range(3))
+
+    with jax.named_scope("state"):
+        send, keep = call(
+            state_body, (1,), (qkv, qkv), [k_spec, v_spec],
+            (heads(group), heads(group)), (whole((group, HD, HD)),) * 2,
+            scalars, flops=2 * rows * width * HD, moved=4 * rows * width,
+        )
+        other = swapped(send, "seq", 1)
+        chip_total = (keep.astype(F32) + other.astype(F32)).astype(BF16)
+        by_x = swapped(chip_total, "seq", 2)
+        by_y = swapped(chip_total, "seq", 4)
+        by_xy = swapped(chip_total, "seq", 6)
+    with jax.named_scope("intra"):
+        intra = call(
+            intra_body, (1,), (qkv, qkv, qkv), [q_spec, k_spec, v_spec],
+            jax.ShapeDtypeStruct((rows, width), F32), whole((rows, width)),
+            scalars, flops=4 * rows * rows * width, moved=10 * rows * width,
+        )
+    with jax.named_scope("prefix"):
+        x_bit = ((seq // 2) % 2).astype(F32)
+        y_bit = (seq // 4).astype(F32)
+        chips = (
+            by_x.astype(F32) * x_bit + by_y.astype(F32) * y_bit + by_xy.astype(F32) * y_bit
+        )
+        low = chips.astype(BF16)
+        first_core = jnp.where(core == 0, keep, other)
+        high = (chips + first_core.astype(F32)).astype(BF16)
+        own_prefix = jnp.where(core == 0, low, high)
+        other_prefix = swapped(jnp.where(core == 0, high, low), "seq", 1)
+
+    scale = 1.0 / math.sqrt(HD * rows * lax.axis_size("seq"))
+    block = width // 2
+    per = width // block
+    w_at = lambda base: pl.BlockSpec(
+        (width, block), lambda i, s: (0, s[base + i // per] * per + i % per)
+    )
+    half_out = pl.BlockSpec((half, block), lambda i, s: (0, i))
+    halves = jax.ShapeDtypeStruct((half, full // 2), BF16)
+    with jax.named_scope("partials"):
+        lin_out, send_a, send_b = call(
+            functools.partial(send_body, scale), (2 * per,),
+            (qkv, intra, own_prefix, other_prefix, w_out),
+            [q_spec, whole((rows, width)), whole((group, HD, HD)), whole((group, HD, HD)), w_at(2)],
+            (jax.ShapeDtypeStruct((rows, width), BF16), halves, halves),
+            (whole((rows, width)), half_out, half_out),
+            scalars, flops=rows * width * full, moved=width * full,
+        )
+        got_a = lax.ppermute(send_a, "head", PAIR)
+        mine_a, mine_b = call(
+            functools.partial(mine_body, per), (2 * per,), (lin_out, w_out, resid),
+            [whole((rows, width)), w_at(4), pl.BlockSpec((rows, block), lambda i, s: (0, i % per))],
+            (halves, halves), (half_out, half_out),
+            scalars, flops=rows * width * full, moved=width * full,
+        )
+
+    positions = seq * rows + jnp.arange(rows, dtype=jnp.int32)
+    freq = 500000.0 ** (-(jnp.arange(HD // 2, dtype=F32) * 2.0 / HD))
+    angle = positions.astype(F32)[:, None] * freq[None, :]
+    cosine, sine = jnp.cos(angle), jnp.sin(angle)
+    cos2 = jnp.concatenate([cosine, cosine], axis=1)
+    sin2 = jnp.concatenate([-sine, sine], axis=1)
+
+    def w_rows(base):
+        return pl.BlockSpec(
+            (None, width, width), lambda j, k, s: ((j + 1) % 3, s[base + k], 0)
+        )
+
+    x_spec = pl.BlockSpec((half, width), lambda j, k, s: (0, k))
+    acc_spec = pl.BlockSpec((None, half, width), lambda j, k, s: (j, 0, 0))
+
+    def own_part(total):
+        return call(
+            first_body, (3, 2), (total, wqkv), [x_spec, w_rows(4)],
+            jax.ShapeDtypeStruct((3, half, width), F32), acc_spec,
+            scalars, flops=half * full * 3 * width, moved=3 * width * full,
+        )
+
+    def rest(total, got, acc, index):
+        turn = pl.BlockSpec((half, HD), lambda *_: (index, 0))
+        return call(
+            second_body, (3, 2), (got, wqkv, acc, total, got, cos2, sin2),
+            [x_spec, w_rows(2), acc_spec, whole((half, full // 2)), whole((half, full // 2)), turn, turn],
+            jax.ShapeDtypeStruct((3, half, width), BF16), acc_spec,
+            scalars, scratch=(pltpu.VMEM((half, width), F32), pltpu.VMEM((half, HD), F32)),
+            flops=half * full * 3 * width, moved=3 * width * full,
+        )
+
+    def add(a, b):
+        return (a.astype(F32) + b.astype(F32)).astype(BF16)
+
+    with jax.named_scope("mix"):
+        send_b, got_a = lax.optimization_barrier((send_b, got_a))
+        got_b = lax.ppermute(send_b, "head", PAIR)
+        sum_a = add(mine_a, got_a)
+        far_a = lax.ppermute(sum_a, "head", CROSS)
+        sum_b = add(mine_b, got_b)
+        far_b = lax.ppermute(sum_b, "head", CROSS)
+        total_a = add(sum_a, far_a)
+        rest_a = lax.ppermute(total_a, "head", PAIR)
+        total_b = add(sum_b, far_b)
+        rest_b = lax.ppermute(total_b, "head", PAIR)
+    with jax.named_scope("project_a"):
+        kvq_a = rest(total_a, rest_a, own_part(total_a), 0)
+        prev_a = shifted(kvq_a[:2], "seq", 1)
+    with jax.named_scope("project_b"):
+        kvq_b = rest(total_b, rest_b, own_part(total_b), 1)
+        prev_b = shifted(kvq_b[:2], "seq", 1)
+    hidden = jnp.concatenate([total_a, total_b], axis=0)
+    hidden = jnp.where(z < 2, hidden[:, :width], hidden[:, width:])
+    with jax.named_scope("attend"):
+        kv = whole((2, half, width))
+        q2 = part(2, half, width)
+        attended = call(
+            attend_body, (1,), (kvq_a, kvq_b, kvq_a, kvq_b, prev_a, prev_b),
+            [q2, q2, kv, kv, kv, kv],
+            jax.ShapeDtypeStruct((rows, width), BF16), whole((rows, width)),
+            scalars, flops=8 * rows * rows * width, moved=12 * rows * width,
+        )
+    return hidden, attended
+
+
 def solution(mesh):
+    line = mesh.shape["seq"] == 8 and mesh.shape["head"] == 4
     return jax.shard_map(
-        local,
+        tuned if line else general,
         mesh=mesh,
         in_specs=(P("seq", None, "head"), P("seq", "head"), P("head", None), P(None, None, "head")),
         out_specs=(P("seq", "head"), P("seq", "head")),

time: 202 us -> 150 us (0.74)
  waiting for transfers between devices: 99.3 us -> 30.7 us
  starting transfers between devices: 5.68 us -> 55.7 us
  Pallas kernels: 0 us -> 49.6 us
  local copies, waits for them, and re-layouts: 39.1 us -> 9.93 us
  matrix products: 23.6 us -> 0 us
  between operations: 13.9 us -> 0.84 us
  blocking collectives: 10 us -> 0 us
  other arithmetic: 9.29 us -> 3.04 us
    ppermute x0 -> x11, starting transfers between devices: none -> 50.8 us  [the longest x1 19.7 us: tuned(): far_b = lax.ppermute(sum_b, 'head', CROSS)]
    pallas_call x0 -> x9, Pallas kernels: none -> 49.6 us  [call(): pl.pallas_call(body, grid_spec=pltpu.PrefetchScalarGridSpec(num_scalar_pr...]
    all_gather x2 -> x0, waiting for transfers between devices: 48.2 us -> none  [the longest x1 37.7 us: local(): piece = lax.all_gather(own_state[None], 'seq', axis=0, tiled=True)]
    reduce_scatter x1 -> x0, waiting for transfers between devices: 44.1 us -> none  [local(): lax.psum_scatter(lax.dot_general(w_out, lin_out, (((0,), (1,)), ((), ()))...]
    unnamed x8 -> x10, local copies, waits for them, and re-layouts: 36 us -> 8.18 us
    dot_general x7 -> x0, matrix products: 23.6 us -> none  [the longest x1 12.5 us: local(): jnp.dot(lax.all_gather(normed, 'head', axis=1, tiled=True), flat_w, prefe...]
    ppermute x0 -> x11, waiting for transfers between devices: none -> 22.9 us  [the longest x1 12.6 us: tuned(): got_a = lax.ppermute(send_a, 'head', PAIR)]
    psum x1 -> x0, blocking collectives: 10 us -> none  [local(): squared = lax.psum(jnp.sum(mixed_f * mixed_f, axis=1), 'head')]
  transfers between devices with their start and end apart: 5 -> 13, of which waited for: 5 -> 7; matrix products, arithmetic and copies ran while one was open for 19% -> 3% of each run, Pallas kernels for 0% -> 26%
where the time goes in v1:
time: 150 us
  starting transfers between devices  55.7 us (37%)
  Pallas kernels  49.6 us (33%)
  waiting for transfers between devices  30.7 us (20%)
  local copies, waits for them, and re-layouts  9.93 us (7%)
  other arithmetic  3.04 us (2%)
    pallas_call x9, Pallas kernels, call(): pl.pallas_call(body, grid_spec=pltpu.PrefetchScalarGridSpec(num_scalar_pr...  49.6 us
    ppermute x1, starting transfers between devices, tuned(): far_b = lax.ppermute(sum_b, 'head', CROSS)  19.7 us
    ppermute x1, waiting for transfers between devices, tuned(): got_a = lax.ppermute(send_a, 'head', PAIR)  12.6 us
    ppermute x1, starting transfers between devices, tuned(): rest_a = lax.ppermute(total_a, 'head', PAIR)  12.3 us
    ppermute x1, starting transfers between devices, tuned(): rest_b = lax.ppermute(total_b, 'head', PAIR)  9.39 us
    unnamed x10, local copies, waits for them, and re-layouts  8.18 us
    ppermute x2, waiting for transfers between devices, shifted(): return lax.ppermute(array, axis, pairs)  7.72 us
    ppermute x5, waiting for transfers between devices, swapped(): lax.ppermute(array, axis, [(i, i ^ bits) for i in range(lax.axis_size(axi...  6.94 us
  transfers between devices with their start and end apart: 13, of which 7 were waited for; matrix products, arithmetic and copies ran while one was open for 3% of the time, Pallas kernels for 26%

profile of v1, /device:TPU:4, one launch (start us, length us, event | category | flops | bytes accessed | tf_op | source)
XLA Modules:
  0.0 149.8 jit_solution(9102625240027599297)
XLA Ops:
  0.7 0.7 broadcast_select_fusion.2
  1.3 0.1 concatenate.12.s_ref
  1.4 1.4 copy-done
  2.8 1.0 state.1
  3.8 0.1 collective-permute-start
  3.9 1.3 collective-permute-done
  5.3 1.5 collective-permute-start.3
  6.8 1.5 %collective-permute-start.2 = (bf16[4,128,128]{2,1,0:T(8,128)(2,1)S(1)}, bf16[4,128,128]{2,1,0:T(8,128)(2,1)S(1)}, u32[]{:S(2)}, u32[]{:S(2)}) collective-permute-start(bf16[4,128,128]{2,1,0:T(8,128)(2,1)S(1)} %add_convert_fusion.5), channel_id=1, source_target_pairs={{0,16},{4,20},{8,24},{12,28},{16,0},{20,4},{24,8},{28,12},{1,17},{... | collective-permute-start | bytes 393224 | tf_op jit(solution)/shard_map/state/ppermute | solution.py:28
  8.3 0.5 collective-permute-start.1
  8.9 1.5 intra.1.intra_ref
  10.3 2.3 %collective-permute-done.3 = bf16[4,128,128]{2,1,0:T(8,128)(2,1)S(1)} collective-permute-done((bf16[4,128,128]{2,1,0:T(8,128)(2,1)S(1)}, bf16[4,128,128]{2,1,0:T(8,128)(2,1)S(1)}, u32[]{:S(2)}, u32[]{:S(2)}) %collective-permute-start.3) | collective-permute-done | bytes 131104 | tf_op jit(solution)/shard_map/state/ppermute | solution.py:28
  12.6 2.0 %collective-permute-done.2 = bf16[4,128,128]{2,1,0:T(8,128)(2,1)S(1)} collective-permute-done((bf16[4,128,128]{2,1,0:T(8,128)(2,1)S(1)}, bf16[4,128,128]{2,1,0:T(8,128)(2,1)S(1)}, u32[]{:S(2)}, u32[]{:S(2)}) %collective-permute-start.2) | collective-permute-done | bytes 131104 | tf_op jit(solution)/shard_map/state/ppermute | solution.py:28
  14.6 0.1 broadcast_select_fusion
  14.8 0.1 collective-permute-start.4
  14.9 1.3 collective-permute-done.4.other_ref
  16.2 3.4 %copy-done.2 = bf16[1024,4096]{1,0:T(8,128)(2,1)S(1)} copy-done((bf16[1024,4096]{1,0:T(8,128)(2,1)S(1)}, bf16[1024,4096]{1,0:T(8,128)(2,1)}, u32[]{:S(2)}) %copy-start.2) | copy-done | bytes 8388632
  19.6 3.8 %partials.2 = (bf16[256,1024]{1,0:T(8,128)(2,1)S(1)}, bf16[128,2048]{1,0:T(8,128)(2,1)}, bf16[128,2048]{1,0:T(8,128)(2,1)S(1)}) custom-call(s32[8]{0:T(128)S(1)} %concatenate.12.s_ref, bf16[3,256,1024]{2,1,0:T(8,128)(2,1)S(1)} %bitcast.11, f32[256,1024]{1,0:T(8,128)S(1)} %intra.1.intra_ref, bf16[4,128,128]{2,1,0:T(8,128)(2,1)S(1)} %broadcast_select_fusion.1.own_ref, ...), custom_call_target="tpu_custom_call" | custom-call | flops 1073741824 | bytes 4194304 | tf_op jit(solution)/shard_map/partials/pallas_call | solution.py:122
  23.4 1.6 %collective-permute-start.5 = (bf16[128,2048]{1,0:T(8,128)(2,1)}, bf16[128,2048]{1,0:T(8,128)(2,1)S(1)}, u32[]{:S(2)}, u32[]{:S(2)}) collective-permute-start(bf16[128,2048]{1,0:T(8,128)(2,1)} %get-tuple-element.16), channel_id=1, source_target_pairs={{0,1},{1,0},{2,3},{3,2},{4,5},{5,4},{6,7},{7,6},{8,9},{9,8},{10,11... | collective-permute-start | bytes 1572872 | tf_op jit(solution)/shard_map/partials/ppermute | solution.py:314
  25.0 12.6 %collective-permute-done.5 = bf16[128,2048]{1,0:T(8,128)(2,1)S(1)} collective-permute-done((bf16[128,2048]{1,0:T(8,128)(2,1)}, bf16[128,2048]{1,0:T(8,128)(2,1)S(1)}, u32[]{:S(2)}, u32[]{:S(2)}) %collective-permute-start.5) | collective-permute-done | bytes 524320 | tf_op jit(solution)/shard_map/partials/ppermute | solution.py:314
  37.6 1.6 %collective-permute-start.7 = (bf16[128,2048]{1,0:T(8,128)(2,1)S(1)}, bf16[128,2048]{1,0:T(8,128)(2,1)S(1)}, u32[]{:S(2)}, u32[]{:S(2)}) collective-permute-start(bf16[128,2048]{1,0:T(8,128)(2,1)S(1)} %get-tuple-element.19), channel_id=1, source_target_pairs={{0,1},{1,0},{2,3},{3,2},{4,5},{5,4},{6,7},{7,6},{8,9},{9,8},{10,11... | collective-permute-start | bytes 1572872 | tf_op jit(solution)/shard_map/mix/ppermute | solution.py:359
  39.2 3.4 %copy-done.3 = bf16[1024,4096]{1,0:T(8,128)(2,1)S(1)} copy-done((bf16[1024,4096]{1,0:T(8,128)(2,1)S(1)}, bf16[1024,4096]{1,0:T(8,128)(2,1)}, u32[]{:S(2)}) %copy-start.3) | copy-done | bytes 8388632
  42.6 2.9 %partials.3 = (bf16[128,2048]{1,0:T(8,128)(2,1)S(1)}, bf16[128,2048]{1,0:T(8,128)(2,1)S(1)}) custom-call(s32[8]{0:T(128)S(1)} %concatenate.12.s_ref, bf16[256,1024]{1,0:T(8,128)(2,1)S(1)} %get-tuple-element.13.lin_ref, bf16[1024,4096]{1,0:T(8,128)(2,1)S(1)} %copy-done.3, bf16[256,1024]{1,0:T(8,128)(2,1)S(1)} %copy-done.4), custom_call_target="tpu_custom_call" | custom-call | flops 1073741824 | bytes 4194304 | tf_op jit(solution)/shard_map/partials/pallas_call | solution.py:122
  45.5 0.1 add_convert_fusion.3
  45.6 2.5 %collective-permute-start.6 = (bf16[128,2048]{1,0:T(8,128)(2,1)S(1)}, bf16[128,2048]{1,0:T(8,128)(2,1)S(1)}, u32[]{:S(2)}, u32[]{:S(2)}) collective-permute-start(bf16[128,2048]{1,0:T(8,128)(2,1)S(1)} %add_convert_fusion.3), channel_id=1, source_target_pairs={{0,3},{3,0},{1,2},{2,1},{4,7},{7,4},{5,6},{6,5},{8,11},{11,8},{9,1... | collective-permute-start | bytes 1572872 | tf_op jit(solution)/shard_map/mix/ppermute | solution.py:361
  48.2 3.4 %collective-permute-done.7 = bf16[128,2048]{1,0:T(8,128)(2,1)S(1)} collective-permute-done((bf16[128,2048]{1,0:T(8,128)(2,1)S(1)}, bf16[128,2048]{1,0:T(8,128)(2,1)S(1)}, u32[]{:S(2)}, u32[]{:S(2)}) %collective-permute-start.7) | collective-permute-done | bytes 524320 | tf_op jit(solution)/shard_map/mix/ppermute | solution.py:359
  51.6 0.1 add_convert_fusion.1
  51.7 19.7 %collective-permute-start.8 = (bf16[128,2048]{1,0:T(8,128)(2,1)S(1)}, bf16[128,2048]{1,0:T(8,128)(2,1)S(1)}, u32[]{:S(2)}, u32[]{:S(2)}) collective-permute-start(bf16[128,2048]{1,0:T(8,128)(2,1)S(1)} %add_convert_fusion.1), channel_id=1, source_target_pairs={{0,3},{3,0},{1,2},{2,1},{4,7},{7,4},{5,6},{6,5},{8,11},{11,8},{9,1... | collective-permute-start | bytes 1572872 | tf_op jit(solution)/shard_map/mix/ppermute | solution.py:363
  71.4 0.5 fusion.3
  71.9 0.0 collective-permute-done.6
  71.9 0.1 add_convert_fusion.2.x_ref.t_ref
  72.1 12.3 %collective-permute-start.9 = (bf16[128,2048]{1,0:T(8,128)(2,1)S(1)}, bf16[128,2048]{1,0:T(8,128)(2,1)S(1)}, u32[]{:S(2)}, u32[]{:S(2)}) collective-permute-start(bf16[128,2048]{1,0:T(8,128)(2,1)S(1)} %add_convert_fusion.2.x_ref.t_ref), channel_id=1, source_target_pairs={{0,1},{1,0},{2,3},{3,2},{4,5},{5,4},{6,7},{7,6},{8,9},{9,8},{10,11... | collective-permute-start | bytes 1572872 | tf_op jit(solution)/shard_map/mix/ppermute | solution.py:365
  84.4 0.0 collective-permute-done.8
  84.4 0.1 add_convert_fusion.x_ref.t_ref
  84.5 9.4 %collective-permute-start.10 = (bf16[128,2048]{1,0:T(8,128)(2,1)S(1)}, bf16[128,2048]{1,0:T(8,128)(2,1)S(1)}, u32[]{:S(2)}, u32[]{:S(2)}) collective-permute-start(bf16[128,2048]{1,0:T(8,128)(2,1)S(1)} %add_convert_fusion.x_ref.t_ref), channel_id=1, source_target_pairs={{0,1},{1,0},{2,3},{3,2},{4,5},{5,4},{6,7},{7,6},{8,9},{9,8},{10,11... | collective-permute-start | bytes 1572872 | tf_op jit(solution)/shard_map/mix/ppermute | solution.py:367
  93.9 0.1 pad_maximum_fusion.1
  94.0 7.8 %project_a.2.in_ref = f32[3,128,1024]{2,1,0:T(8,128)S(1)} custom-call(s32[8]{0:T(128)S(1)} %concatenate.12.s_ref, bf16[128,2048]{1,0:T(8,128)(2,1)S(1)} %add_convert_fusion.2.x_ref.t_ref, bf16[3,4096,1024]{2,1,0:T(8,128)(2,1)} %bitcast.12), custom_call_target="tpu_custom_call" | custom-call | flops 1610612736 | bytes 12582912 | tf_op jit(solution)/shard_map/project_a/pallas_call | solution.py:122
  101.8 0.0 collective-permute-done.9.x_ref.o_ref
  101.9 9.4 %project_a.3.qa_ref.a_ref = bf16[3,128,1024]{2,1,0:T(8,128)(2,1)S(1)} custom-call(s32[8]{0:T(128)S(1)} %concatenate.12.s_ref, bf16[128,2048]{1,0:T(8,128)(2,1)S(1)} %collective-permute-done.9.x_ref.o_ref, bf16[3,4096,1024]{2,1,0:T(8,128)(2,1)} %bitcast.13, f32[3,128,1024]{2,1,0:T(8,128)S(1)} %project_a.2.in_ref, ...), custom_call_target="tpu_custom_call" | custom-call | flops 1610612736 | bytes 12582912 | tf_op jit(solution)/shard_map/project_a/pallas_call | solution.py:122
  111.2 0.8 slice.18
  112.1 1.9 %collective-permute-start.11 = (bf16[2,128,1024]{2,1,0:T(8,128)(2,1)}, bf16[2,128,1024]{2,1,0:T(8,128)(2,1)S(1)}, u32[]{:S(2)}, u32[]{:S(2)}) collective-permute-start(bf16[2,128,1024]{2,1,0:T(8,128)(2,1)} %slice.18), channel_id=1, source_target_pairs={{0,4},{4,8},{8,12},{12,16},{16,20},{20,24},{24,28},{1,5},{5,9},{9,... | collective-permute-start | bytes 1572872 | tf_op jit(solution)/shard_map/project_a/ppermute | solution.py:24
  114.0 7.8 %project_b.2.in_ref = f32[3,128,1024]{2,1,0:T(8,128)S(1)} custom-call(s32[8]{0:T(128)S(1)} %concatenate.12.s_ref, bf16[128,2048]{1,0:T(8,128)(2,1)S(1)} %add_convert_fusion.x_ref.t_ref, bf16[3,4096,1024]{2,1,0:T(8,128)(2,1)} %bitcast.14), custom_call_target="tpu_custom_call" | custom-call | flops 1610612736 | bytes 12582912 | tf_op jit(solution)/shard_map/project_b/pallas_call | solution.py:122
  121.8 0.0 collective-permute-done.10.x_ref.o_ref
  121.8 9.4 %project_b.3.qb_ref.b_ref = bf16[3,128,1024]{2,1,0:T(8,128)(2,1)S(1)} custom-call(s32[8]{0:T(128)S(1)} %concatenate.12.s_ref, bf16[128,2048]{1,0:T(8,128)(2,1)S(1)} %collective-permute-done.10.x_ref.o_ref, bf16[3,4096,1024]{2,1,0:T(8,128)(2,1)} %bitcast.15, f32[3,128,1024]{2,1,0:T(8,128)S(1)} %project_b.2.in_ref, ...), custom_call_target="tpu_custom_call" | custom-call | flops 1610612736 | bytes 12582912 | tf_op jit(solution)/shard_map/project_b/pallas_call | solution.py:122
  131.2 0.8 slice.19
  132.0 3.0 %collective-permute-start.12 = (bf16[2,128,1024]{2,1,0:T(8,128)(2,1)}, bf16[2,128,1024]{2,1,0:T(8,128)(2,1)}, u32[]{:S(2)}, u32[]{:S(2)}) collective-permute-start(bf16[2,128,1024]{2,1,0:T(8,128)(2,1)} %slice.19), channel_id=1, source_target_pairs={{0,4},{4,8},{8,12},{12,16},{16,20},{20,24},{24,28},{1,5},{5,9},{9,... | collective-permute-start | bytes 1572872 | tf_op jit(solution)/shard_map/project_b/ppermute | solution.py:24
  135.0 1.0 fusion.1
  136.0 7.7 %collective-permute-done.12.pb_ref = bf16[2,128,1024]{2,1,0:T(8,128)(2,1)} collective-permute-done((bf16[2,128,1024]{2,1,0:T(8,128)(2,1)}, bf16[2,128,1024]{2,1,0:T(8,128)(2,1)}, u32[]{:S(2)}, u32[]{:S(2)}) %collective-permute-start.12) | collective-permute-done | bytes 524320 | tf_op jit(solution)/shard_map/project_b/ppermute | solution.py:24
  143.7 6.0 %attend.1 = bf16[256,1024]{1,0:T(8,128)(2,1)} custom-call(s32[8]{0:T(128)S(1)} %concatenate.12.s_ref, bf16[3,128,1024]{2,1,0:T(8,128)(2,1)S(1)} %project_a.3.qa_ref.a_ref, bf16[3,128,1024]{2,1,0:T(8,128)(2,1)S(1)} %project_b.3.qb_ref.b_ref, bf16[3,128,1024]{2,1,0:T(8,128)(2,1)S(1)} %project_a.3.qa_ref.a_ref, ...), custom_call_target="tpu_custom_call" | custom-call | flops 536870912 | bytes 3145728 | tf_op jit(solution)/shard_map/attend/pallas_call | solution.py:122
  (13 shorter events, 0.1 us)
Async XLA Ops:
  1.4 1.4 copy-start
  2.8 6.0 %copy-start.1 = (bf16[256,3,1024]{2,0,1:T(8,128)(2,1)S(1)}, bf16[256,3,1024]{2,0,1:T(8,128)(2,1)}, u32[]{:S(2)}) copy-start(bf16[256,3,1024]{2,0,1:T(8,128)(2,1)} %param.6) | copy-start | bytes 4718596
  3.8 1.4 collective-permute-start
  5.3 7.3 %collective-permute-start.3 = (bf16[4,128,128]{2,1,0:T(8,128)(2,1)S(1)}, bf16[4,128,128]{2,1,0:T(8,128)(2,1)S(1)}, u32[]{:S(2)}, u32[]{:S(2)}) collective-permute-start(bf16[4,128,128]{2,1,0:T(8,128)(2,1)S(1)} %add_convert_fusion.5), channel_id=1, source_target_pairs={{0,24},{4,28},{8,16},{12,20},{16,8},{20,12},{24,0},{28,4},{1,25},{... | collective-permute-start | bytes 393224 | tf_op jit(solution)/shard_map/state/ppermute | solution.py:28
  6.8 7.8 %collective-permute-start.2 = (bf16[4,128,128]{2,1,0:T(8,128)(2,1)S(1)}, bf16[4,128,128]{2,1,0:T(8,128)(2,1)S(1)}, u32[]{:S(2)}, u32[]{:S(2)}) collective-permute-start(bf16[4,128,128]{2,1,0:T(8,128)(2,1)S(1)} %add_convert_fusion.5), channel_id=1, source_target_pairs={{0,16},{4,20},{8,24},{12,28},{16,0},{20,4},{24,8},{28,12},{1,17},{... | collective-permute-start | bytes 393224 | tf_op jit(solution)/shard_map/state/ppermute | solution.py:28
  8.3 6.3 %collective-permute-start.1 = (bf16[4,128,128]{2,1,0:T(8,128)(2,1)S(1)}, bf16[4,128,128]{2,1,0:T(8,128)(2,1)S(1)}, u32[]{:S(2)}, u32[]{:S(2)}) collective-permute-start(bf16[4,128,128]{2,1,0:T(8,128)(2,1)S(1)} %add_convert_fusion.5), channel_id=1, source_target_pairs={{0,8},{4,12},{8,0},{12,4},{16,24},{20,28},{24,16},{28,20},{1,9},{5... | collective-permute-start | bytes 393224 | tf_op jit(solution)/shard_map/state/ppermute | solution.py:28
  14.8 1.4 collective-permute-start.4
  16.2 3.4 %copy-start.2 = (bf16[1024,4096]{1,0:T(8,128)(2,1)S(1)}, bf16[1024,4096]{1,0:T(8,128)(2,1)}, u32[]{:S(2)}) copy-start(bf16[1024,4096]{1,0:T(8,128)(2,1)} %w_ref.3) | copy-start | bytes 25165828
  19.6 19.6 %copy-start.4 = (bf16[256,1024]{1,0:T(8,128)(2,1)S(1)}, bf16[256,1024]{1,0:T(8,128)(2,1)}, u32[]{:S(2)}) copy-start(bf16[256,1024]{1,0:T(8,128)(2,1)} %r_ref.1) | copy-start | bytes 1572868
  23.4 14.2 %collective-permute-start.5 = (bf16[128,2048]{1,0:T(8,128)(2,1)}, bf16[128,2048]{1,0:T(8,128)(2,1)S(1)}, u32[]{:S(2)}, u32[]{:S(2)}) collective-permute-start(bf16[128,2048]{1,0:T(8,128)(2,1)} %get-tuple-element.16), channel_id=1, source_target_pairs={{0,1},{1,0},{2,3},{3,2},{4,5},{5,4},{6,7},{7,6},{8,9},{9,8},{10,11... | collective-permute-start | bytes 1572872 | tf_op jit(solution)/shard_map/partials/ppermute | solution.py:314
  37.6 14.0 %collective-permute-start.7 = (bf16[128,2048]{1,0:T(8,128)(2,1)S(1)}, bf16[128,2048]{1,0:T(8,128)(2,1)S(1)}, u32[]{:S(2)}, u32[]{:S(2)}) collective-permute-start(bf16[128,2048]{1,0:T(8,128)(2,1)S(1)} %get-tuple-element.19), channel_id=1, source_target_pairs={{0,1},{1,0},{2,3},{3,2},{4,5},{5,4},{6,7},{7,6},{8,9},{9,8},{10,11... | collective-permute-start | bytes 1572872 | tf_op jit(solution)/shard_map/mix/ppermute | solution.py:359
  39.2 3.4 %copy-start.3 = (bf16[1024,4096]{1,0:T(8,128)(2,1)S(1)}, bf16[1024,4096]{1,0:T(8,128)(2,1)}, u32[]{:S(2)}) copy-start(bf16[1024,4096]{1,0:T(8,128)(2,1)} %w_ref.3) | copy-start | bytes 25165828
  45.6 26.3 %collective-permute-start.6 = (bf16[128,2048]{1,0:T(8,128)(2,1)S(1)}, bf16[128,2048]{1,0:T(8,128)(2,1)S(1)}, u32[]{:S(2)}, u32[]{:S(2)}) collective-permute-start(bf16[128,2048]{1,0:T(8,128)(2,1)S(1)} %add_convert_fusion.3), channel_id=1, source_target_pairs={{0,3},{3,0},{1,2},{2,1},{4,7},{7,4},{5,6},{6,5},{8,11},{11,8},{9,1... | collective-permute-start | bytes 1572872 | tf_op jit(solution)/shard_map/mix/ppermute | solution.py:361
  51.7 32.7 %collective-permute-start.8 = (bf16[128,2048]{1,0:T(8,128)(2,1)S(1)}, bf16[128,2048]{1,0:T(8,128)(2,1)S(1)}, u32[]{:S(2)}, u32[]{:S(2)}) collective-permute-start(bf16[128,2048]{1,0:T(8,128)(2,1)S(1)} %add_convert_fusion.1), channel_id=1, source_target_pairs={{0,3},{3,0},{1,2},{2,1},{4,7},{7,4},{5,6},{6,5},{8,11},{11,8},{9,1... | collective-permute-start | bytes 1572872 | tf_op jit(solution)/shard_map/mix/ppermute | solution.py:363
  72.1 29.8 %collective-permute-start.9 = (bf16[128,2048]{1,0:T(8,128)(2,1)S(1)}, bf16[128,2048]{1,0:T(8,128)(2,1)S(1)}, u32[]{:S(2)}, u32[]{:S(2)}) collective-permute-start(bf16[128,2048]{1,0:T(8,128)(2,1)S(1)} %add_convert_fusion.2.x_ref.t_ref), channel_id=1, source_target_pairs={{0,1},{1,0},{2,3},{3,2},{4,5},{5,4},{6,7},{7,6},{8,9},{9,8},{10,11... | collective-permute-start | bytes 1572872 | tf_op jit(solution)/shard_map/mix/ppermute | solution.py:365
  84.5 37.3 %collective-permute-start.10 = (bf16[128,2048]{1,0:T(8,128)(2,1)S(1)}, bf16[128,2048]{1,0:T(8,128)(2,1)S(1)}, u32[]{:S(2)}, u32[]{:S(2)}) collective-permute-start(bf16[128,2048]{1,0:T(8,128)(2,1)S(1)} %add_convert_fusion.x_ref.t_ref), channel_id=1, source_target_pairs={{0,1},{1,0},{2,3},{3,2},{4,5},{5,4},{6,7},{7,6},{8,9},{9,8},{10,11... | collective-permute-start | bytes 1572872 | tf_op jit(solution)/shard_map/mix/ppermute | solution.py:367
  112.1 23.9 %collective-permute-start.11 = (bf16[2,128,1024]{2,1,0:T(8,128)(2,1)}, bf16[2,128,1024]{2,1,0:T(8,128)(2,1)S(1)}, u32[]{:S(2)}, u32[]{:S(2)}) collective-permute-start(bf16[2,128,1024]{2,1,0:T(8,128)(2,1)} %slice.18), channel_id=1, source_target_pairs={{0,4},{4,8},{8,12},{12,16},{16,20},{20,24},{24,28},{1,5},{5,9},{9,... | collective-permute-start | bytes 1572872 | tf_op jit(solution)/shard_map/project_a/ppermute | solution.py:24
  132.0 11.7 %collective-permute-start.12 = (bf16[2,128,1024]{2,1,0:T(8,128)(2,1)}, bf16[2,128,1024]{2,1,0:T(8,128)(2,1)}, u32[]{:S(2)}, u32[]{:S(2)}) collective-permute-start(bf16[2,128,1024]{2,1,0:T(8,128)(2,1)} %slice.19), channel_id=1, source_target_pairs={{0,4},{4,8},{8,12},{12,16},{16,20},{20,24},{24,28},{1,5},{5,9},{9,... | collective-permute-start | bytes 1572872 | tf_op jit(solution)/shard_map/project_b/ppermute | solution.py:24

commit v2 on v0

--- a/solution.py
+++ b/solution.py
@@ -1,18 +1,31 @@
+import functools
 import math
 
 import jax
 import jax.numpy as jnp
 from jax import lax
+from jax.experimental import pallas as pl
+from jax.experimental.pallas import tpu as pltpu
 from jax.sharding import PartitionSpec as P
 
 D = 4096
 HD = 128
+BF16 = jnp.bfloat16
+F32 = jnp.float32
+NEG = -1e30
+
+PAIR = [(0, 1), (1, 0), (2, 3), (3, 2)]
+CROSS = [(0, 3), (3, 0), (1, 2), (2, 1)]
 
 
 def shifted(array, axis, by):
     devices = lax.axis_size(axis)
     pairs = [(i, i + by) for i in range(devices) if 0 <= i + by < devices]
     return lax.ppermute(array, axis, pairs)
+
+
+def swapped(array, axis, bits):
+    return lax.ppermute(array, axis, [(i, i ^ bits) for i in range(lax.axis_size(axis))])
 
 
 def rotary(values, positions):
@@ -28,7 +41,7 @@
     )
 
 
-def local(lin_qkv, resid, w_out, w_qkv):
+def general(lin_qkv, resid, w_out, w_qkv):
     tok_rows = lin_qkv.shape[0]
     local_width = lin_qkv.shape[2]
     nheads = local_width // HD
@@ -89,9 +102,351 @@
     return (hidden, attended.astype(jnp.bfloat16).reshape(tok_rows, local_width))
 
 
+def dot(a, b):
+    return jnp.dot(a, b, preferred_element_type=F32)
+
+
+def dot_nt(a, b):
+    return lax.dot_general(a, b, (((1,), (1,)), ((), ())), preferred_element_type=F32)
+
+
+def dot_tn(a, b):
+    return lax.dot_general(a, b, (((0,), (0,)), ((), ())), preferred_element_type=F32)
+
+
+def at(start, size):
+    return pl.ds(pl.multiple_of(start, size), size)
+
+
+ON_CHIP = pl.BlockSpec(memory_space=pltpu.VMEM)
+IN_HBM = pl.BlockSpec(memory_space=pltpu.HBM)
+ANYWHERE = pl.BlockSpec(memory_space=pl.ANY)
+
+
+def call(body, ins, outs, in_specs=None, scratch=(), vmem=20, flops=0, moved=0):
+    return pl.pallas_call(
+        body,
+        in_specs=in_specs or [ON_CHIP] * len(ins),
+        out_specs=jax.tree.map(lambda _: ON_CHIP, outs),
+        out_shape=outs,
+        scratch_shapes=scratch,
+        compiler_params=pltpu.CompilerParams(vmem_limit_bytes=vmem * 2**20),
+        cost_estimate=pl.CostEstimate(flops=flops, bytes_accessed=moved, transcendentals=0),
+    )(*ins)
+
+
+def load_body(source, after, target, sems):
+    copies = []
+    for i in range(sems.shape[0]):
+        copy = pltpu.make_async_copy(source.at[i], target.at[i], sems.at[i])
+        copy.start()
+        copies.append(copy)
+    for copy in copies:
+        copy.wait()
+
+
+def loaded(array, after):
+    return call(
+        load_body, (array, after), pltpu.VMEM(array.shape, array.dtype),
+        [IN_HBM, ANYWHERE], (pltpu.SemaphoreType.DMA((array.shape[0],)),), vmem=4, moved=2 * array.size,
+    )
+
+
+def state_body(qkv_ref, send_ref, keep_ref, k_ref, v_ref, sems):
+    core = lax.axis_index("seq") % 2
+    count = send_ref.shape[0]
+    wide = k_ref.shape[2]
+    copies = []
+    for slot in range(2):
+        group = core if slot else 1 - core
+        pair = []
+        for plane, ref in ((1, k_ref), (2, v_ref)):
+            copy = pltpu.make_async_copy(
+                qkv_ref.at[plane, :, at(group * wide, wide)], ref.at[slot], sems.at[slot, plane - 1]
+            )
+            copy.start()
+            pair.append(copy)
+        copies.append(pair)
+    for slot, out in ((0, send_ref), (1, keep_ref)):
+        for copy in copies[slot]:
+            copy.wait()
+        for j in range(count):
+            head = slice(j * HD, (j + 1) * HD)
+            out[j] = dot_tn(k_ref[slot, :, head], v_ref[slot, :, head]).astype(BF16)
+
+
+def intra_body(qkv_ref, o_ref, q_ref):
+    rows = qkv_ref.shape[1]
+    ahead = lax.broadcasted_iota(jnp.int32, (rows, rows), 1) > lax.broadcasted_iota(
+        jnp.int32, (rows, rows), 0
+    )
+    q_ref[...] = qkv_ref[0]
+    for h in range(qkv_ref.shape[2] // HD):
+        head = slice(h * HD, (h + 1) * HD)
+        scores = dot_nt(qkv_ref[0, :, head], qkv_ref[1, :, head])
+        inner = jnp.where(ahead, 0.0, scores).astype(BF16)
+        o_ref[:, head] = dot(inner, qkv_ref[2, :, head])
+
+
+def quarters():
+    z = lax.axis_index("head")
+    edge = (z == 0) | (z == 3)
+    outer, inner = (0, 3), (1, 2)
+    mine = [jnp.where(edge, a, b) for a, b in zip(outer, inner)]
+    other = [jnp.where(edge, b, a) for a, b in zip(outer, inner)]
+    return z, mine, other
+
+
+def send_body(scale, q_ref, intra_ref, own_ref, other_ref, w_ref, lin_ref, a_ref, b_ref):
+    core = lax.axis_index("seq") % 2
+    count = own_ref.shape[0]
+    for ref, group in ((own_ref, core), (other_ref, 1 - core)):
+        for j in range(count):
+            head = at((group * count + j) * HD, HD)
+            total = intra_ref[:, head] + dot(q_ref[:, head], ref[j])
+            lin_ref[:, head] = (total * scale).astype(BF16)
+    _, _, other = quarters()
+    half, width = a_ref.shape[0], a_ref.shape[1] // 2
+    block = width // 2
+    for p in range(2):
+        for n in range(2):
+            product = dot(lin_ref[...], w_ref[:, at(other[p] * width + n * block, block)]).astype(BF16)
+            to = slice(p * width + n * block, p * width + (n + 1) * block)
+            a_ref[:, to] = product[:half]
+            b_ref[:, to] = product[half:]
+
+
+def mine_body(lin_ref, w_ref, r_ref, a_ref, b_ref):
+    z, mine, _ = quarters()
+    half, width = a_ref.shape[0], a_ref.shape[1] // 2
+    block = width // 2
+    for p in range(2):
+        for n in range(2):
+            product = dot(lin_ref[...], w_ref[:, at(mine[p] * width + n * block, block)])
+            own = r_ref[:, n * block : (n + 1) * block].astype(F32)
+            product = (product + jnp.where(mine[p] == z, own, 0.0)).astype(BF16)
+            to = slice(p * width + n * block, p * width + (n + 1) * block)
+            a_ref[:, to] = product[:half]
+            b_ref[:, to] = product[half:]
+
+
+def two_quarters(x_ref, w_ref, plane, which, to):
+    width = x_ref.shape[1] // 2
+    low = dot(x_ref[:, :width], w_ref[plane, at(which[0] * width, width), to])
+    return low + dot(x_ref[:, width:], w_ref[plane, at(which[1] * width, width), to])
+
+
+def first_body(block, x_ref, w_ref, acc_ref):
+    _, mine, _ = quarters()
+    for plane in range(3):
+        for n in range(acc_ref.shape[2] // block):
+            to = slice(n * block, (n + 1) * block)
+            acc_ref[plane, :, to] = two_quarters(x_ref, w_ref, plane, mine, to)
+
+
+def first_hidden_body(block, x_ref, w_ref, a_ref, acc_ref, hidden_ref):
+    half, width = a_ref.shape[0], a_ref.shape[1] // 2
+    own = at((lax.axis_index("head") // 2) * width, width)
+    hidden_ref[:half] = a_ref[:, own]
+    hidden_ref[half:] = x_ref[:, own]
+    first_body(block, x_ref, w_ref, acc_ref)
+
+
+def finish(block, plane, x_ref, w_ref, acc_ref, inv, cos, sin, out_ref):
+    _, _, other = quarters()
+    for n in range(acc_ref.shape[2] // block):
+        to = slice(n * block, (n + 1) * block)
+        total = (acc_ref[plane, :, to] + two_quarters(x_ref, w_ref, plane, other, to)) * inv
+        if plane == 2:
+            out_ref[:, to] = total.astype(BF16)
+            continue
+        for h in range(block // HD):
+            value = total[:, h * HD : (h + 1) * HD]
+            turned = value * cos + pltpu.roll(value, HD // 2, 1) * sin
+            out_ref[:, n * block + h * HD : n * block + (h + 1) * HD] = turned.astype(BF16)
+
+
+def kv_body(block, t_ref, x_ref, w_ref, acc_ref, cos_ref, sin_ref, kv_ref, inv_ref):
+    t = t_ref[...].astype(F32)
+    x = x_ref[...].astype(F32)
+    total = jnp.sum(t * t + x * x, axis=1, keepdims=True)
+    inv = lax.rsqrt(total / D + 1e-05)
+    inv_ref[...] = jnp.broadcast_to(inv, inv_ref.shape)
+    for plane in (1, 2):
+        finish(block, plane, x_ref, w_ref, acc_ref, inv, cos_ref[...], sin_ref[...], kv_ref.at[plane - 1])
+
+
+def q_body(block, x_ref, w_ref, acc_ref, inv_ref, cos_ref, sin_ref, q_ref):
+    inv = inv_ref[:, :1]
+    finish(block, 0, x_ref, w_ref, acc_ref, inv, cos_ref[...], sin_ref[...], q_ref)
+
+
+SCORE = 1.0 / math.sqrt(HD)
+
+
+def early_body(qa_ref, qb_ref, a_ref, b_ref, pa_ref, acc_ref, top_ref, sum_ref):
+    has_prev = lax.axis_index("seq") > 0
+    half = qa_ref.shape[0]
+    shape = (2 * half, 3 * half)
+    row = lax.broadcasted_iota(jnp.int32, shape, 0)
+    col = lax.broadcasted_iota(jnp.int32, shape, 1)
+    allowed = ((col < half) & has_prev) | ((col >= half) & (col - half <= row))
+    for h in range(qa_ref.shape[1] // HD):
+        head = slice(h * HD, (h + 1) * HD)
+        queries = jnp.concatenate([qa_ref[:, head], qb_ref[:, head]], axis=0)
+        keys = jnp.concatenate([r[0, :, head] for r in (pa_ref, a_ref, b_ref)], axis=0)
+        values = jnp.concatenate([r[1, :, head] for r in (pa_ref, a_ref, b_ref)], axis=0)
+        logits = jnp.where(allowed, dot_nt(queries, keys) * SCORE, NEG)
+        top = jnp.max(logits, axis=1, keepdims=True)
+        expo = jnp.where(allowed, jnp.exp(logits - top), 0.0)
+        top_ref[h] = top
+        sum_ref[h] = jnp.sum(expo, axis=1, keepdims=True)
+        acc_ref[:, head] = dot(expo.astype(BF16), values)
+
+
+def late_body(qa_ref, qb_ref, pb_ref, acc_ref, top_ref, sum_ref, out_ref):
+    has_prev = lax.axis_index("seq") > 0
+    for h in range(qa_ref.shape[1] // HD):
+        head = slice(h * HD, (h + 1) * HD)
+        queries = jnp.concatenate([qa_ref[:, head], qb_ref[:, head]], axis=0)
+        logits = jnp.where(has_prev, dot_nt(queries, pb_ref[0, :, head]) * SCORE, NEG)
+        before = top_ref[h]
+        top = jnp.maximum(before, jnp.max(logits, axis=1, keepdims=True))
+        expo = jnp.where(has_prev, jnp.exp(logits - top), 0.0)
+        fade = jnp.exp(before - top)
+        total = sum_ref[h] * fade + jnp.sum(expo, axis=1, keepdims=True)
+        acc = acc_ref[:, head] * fade + dot(expo.astype(BF16), pb_ref[1, :, head])
+        out_ref[:, head] = (acc / total).astype(BF16)
+
+
+def tuned(lin_qkv, resid, w_out, w_qkv):
+    rows, _, width = lin_qkv.shape
+    nheads = width // HD
+    half = rows // 2
+    group = nheads // 2
+    full = w_out.shape[1]
+    block = width // 2
+    seq = lax.axis_index("seq")
+    core = seq % 2
+    shape = jax.ShapeDtypeStruct
+
+    qkv = jnp.transpose(lin_qkv, (1, 0, 2))
+    wqkv = jnp.transpose(w_qkv, (1, 0, 2))
+
+    with jax.named_scope("state"):
+        states = shape((group, HD, HD), BF16)
+        send, keep = call(
+            state_body, (qkv,), (states, states), [IN_HBM],
+            (
+                pltpu.VMEM((2, rows, width // 2), BF16),
+                pltpu.VMEM((2, rows, width // 2), BF16),
+                pltpu.SemaphoreType.DMA((2, 2)),
+            ),
+            flops=2 * rows * width * HD, moved=4 * rows * width,
+        )
+        other = swapped(send, "seq", 1)
+        chip_total = (keep.astype(F32) + other.astype(F32)).astype(BF16)
+        by_x = swapped(chip_total, "seq", 2)
+        by_y = swapped(chip_total, "seq", 4)
+        by_xy = swapped(chip_total, "seq", 6)
+    with jax.named_scope("intra"):
+        intra, q = call(
+            intra_body, (qkv,), (shape((rows, width), F32), shape((rows, width), BF16)),
+            flops=4 * rows * rows * width, moved=10 * rows * width,
+        )
+    with jax.named_scope("load_w_out"):
+        w_out_here = loaded(w_out.reshape(4, width // 4, full), chip_total).reshape(width, full)
+    with jax.named_scope("prefix"):
+        x_bit = ((seq // 2) % 2).astype(F32)
+        y_bit = (seq // 4).astype(F32)
+        chips = (
+            by_x.astype(F32) * x_bit + by_y.astype(F32) * y_bit + by_xy.astype(F32) * y_bit
+        )
+        low = chips.astype(BF16)
+        first_core = jnp.where(core == 0, keep, other)
+        high = (chips + first_core.astype(F32)).astype(BF16)
+        own_prefix = jnp.where(core == 0, low, high)
+        other_prefix = swapped(jnp.where(core == 0, high, low), "seq", 1)
+
+    scale = 1.0 / math.sqrt(HD * rows * lax.axis_size("seq"))
+    halves = shape((half, full // 2), BF16)
+    with jax.named_scope("partials"):
+        lin_out, send_a, send_b = call(
+            functools.partial(send_body, scale), (q, intra, own_prefix, other_prefix, w_out_here),
+            (shape((rows, width), BF16), halves, halves), flops=rows * width * full, moved=width * full,
+        )
+        got_a = lax.ppermute(send_a, "head", PAIR)
+        mine_a, mine_b = call(
+            mine_body, (lin_out, w_out_here, resid), (halves, halves),
+            flops=rows * width * full, moved=width * full,
+        )
+    with jax.named_scope("load_w_qkv"):
+        w_here = loaded(wqkv.reshape(3, 4, width, width).reshape(12, width, width), mine_a)
+        w_here = w_here.reshape(3, full, width)
+
+    positions = seq * rows + jnp.arange(rows, dtype=jnp.int32)
+    freq = 500000.0 ** (-(jnp.arange(HD // 2, dtype=F32) * 2.0 / HD))
+    angle = positions.astype(F32)[:, None] * freq[None, :]
+    cosine, sine = jnp.cos(angle), jnp.sin(angle)
+    cos2 = jnp.concatenate([cosine, cosine], axis=1)
+    sin2 = jnp.concatenate([-sine, sine], axis=1)
+
+    accs = shape((3, half, width), F32)
+    cost = dict(flops=half * full * 3 * width, moved=3 * width * full)
+
+    def add(a, b):
+        return (a.astype(F32) + b.astype(F32)).astype(BF16)
+
+    def project(total, got, acc, index):
+        turn = (cos2[index * half : (index + 1) * half], sin2[index * half : (index + 1) * half])
+        kv, inv = call(
+            functools.partial(kv_body, block), (total, got, w_here, acc, *turn),
+            (shape((2, half, width), BF16), shape((half, HD), F32)), **cost,
+        )
+        before = shifted(kv, "seq", 1)
+        query = call(
+            functools.partial(q_body, block), (got, w_here, acc, inv, *turn), shape((half, width), BF16), **cost,
+        )
+        return kv, before, query
+
+    with jax.named_scope("mix"):
+        send_b, got_a = lax.optimization_barrier((send_b, got_a))
+        got_b = lax.ppermute(send_b, "head", PAIR)
+        sum_a = add(mine_a, got_a)
+        far_a = lax.ppermute(sum_a, "head", CROSS)
+        sum_b = add(mine_b, got_b)
+        sum_b, far_a = lax.optimization_barrier((sum_b, far_a))
+        far_b = lax.ppermute(sum_b, "head", CROSS)
+        total_a = add(sum_a, far_a)
+        rest_a = lax.ppermute(total_a, "head", PAIR)
+        total_b = add(sum_b, far_b)
+        rest_b = lax.ppermute(total_b, "head", PAIR)
+    with jax.named_scope("project_a"):
+        acc_a = call(functools.partial(first_body, block), (total_a, w_here), accs, **cost)
+        kv_a, prev_a, query_a = project(total_a, rest_a, acc_a, 0)
+    with jax.named_scope("project_b"):
+        acc_b, hidden = call(
+            functools.partial(first_hidden_body, block), (total_b, w_here, total_a),
+            (accs, shape((rows, width), BF16)), **cost,
+        )
+        kv_b, prev_b, query_b = project(total_b, rest_b, acc_b, 1)
+    with jax.named_scope("attend"):
+        stat = shape((nheads, rows, 1), F32)
+        acc, top, total = call(
+            early_body, (query_a, query_b, kv_a, kv_b, prev_a), (shape((rows, width), F32), stat, stat),
+            flops=6 * rows * rows * width, moved=12 * rows * width,
+        )
+        attended = call(
+            late_body, (query_a, query_b, prev_b, acc, top, total), shape((rows, width), BF16),
+            flops=2 * rows * rows * width, moved=12 * rows * width,
+        )
+    return hidden, attended
+
+
 def solution(mesh):
+    line = mesh.shape["seq"] == 8 and mesh.shape["head"] == 4
     return jax.shard_map(
-        local,
+        tuned if line else general,
         mesh=mesh,
         in_specs=(P("seq", None, "head"), P("seq", "head"), P("head", None), P(None, None, "head")),
         out_specs=(P("seq", "head"), P("seq", "head")),

time: 202 us -> 135 us (0.67)
  waiting for transfers between devices: 99.3 us -> 39.9 us
  starting transfers between devices: 5.68 us -> 34 us
  matrix products: 23.6 us -> 0 us
  Pallas kernels: 0 us -> 21.4 us
  between operations: 13.9 us -> 0.91 us
  blocking collectives: 10 us -> 0 us
  other arithmetic: 9.29 us -> 1.38 us
    all_gather x2 -> x0, waiting for transfers between devices: 48.2 us -> none  [the longest x1 37.7 us: local(): piece = lax.all_gather(own_state[None], 'seq', axis=0, tiled=True)]
    reduce_scatter x1 -> x0, waiting for transfers between devices: 44.1 us -> none  [local(): lax.psum_scatter(lax.dot_general(w_out, lin_out, (((0,), (1,)), ((), ()))...]
    ppermute x0 -> x11, waiting for transfers between devices: none -> 36.1 us  [the longest x1 12.4 us: tuned(): far_a = lax.ppermute(sum_a, 'head', CROSS)]
    ppermute x0 -> x11, starting transfers between devices: none -> 28.4 us  [the longest x1 10.7 us: tuned(): rest_a = lax.ppermute(total_a, 'head', PAIR)]
    dot_general x7 -> x0, matrix products: 23.6 us -> none  [the longest x1 12.5 us: local(): jnp.dot(lax.all_gather(normed, 'head', axis=1, tiled=True), flat_w, prefe...]
    pallas_call x0 -> x14, Pallas kernels: none -> 21.4 us  [call(): pl.pallas_call(body, in_specs=in_specs or [ON_CHIP] * len(ins), out_specs...]
    psum x1 -> x0, blocking collectives: 10 us -> none  [local(): squared = lax.psum(jnp.sum(mixed_f * mixed_f, axis=1), 'head')]
    reduce_sum x2 -> x0, other arithmetic: 3.97 us -> none  [the longest x1 2.68 us: local(): before = jnp.sum(piece * keep[:, None, None, None], axis=0)]
  transfers between devices with their start and end apart: 5 -> 13, of which waited for: 5 -> 8; matrix products, arithmetic and copies ran while one was open for 19% -> 1% of each run, Pallas kernels for 0% -> 12%
where the time goes in v2:
time: 135 us
  waiting for transfers between devices  39.9 us (30%)
  local copies, waits for them, and re-layouts  37.4 us (28%)
  starting transfers between devices  34 us (25%)
  Pallas kernels  21.4 us (16%)
  other arithmetic  1.38 us (1%)
    unnamed x18, local copies, waits for them, and re-layouts  37.4 us
    pallas_call x14, Pallas kernels, call(): pl.pallas_call(body, in_specs=in_specs or [ON_CHIP] * len(ins), out_specs...  21.4 us
    ppermute x1, waiting for transfers between devices, tuned(): far_a = lax.ppermute(sum_a, 'head', CROSS)  12.4 us
    ppermute x1, starting transfers between devices, tuned(): rest_a = lax.ppermute(total_a, 'head', PAIR)  10.7 us
    ppermute x1, waiting for transfers between devices, tuned(): got_b = lax.ppermute(send_b, 'head', PAIR)  9.7 us
    ppermute x1, waiting for transfers between devices, tuned(): got_a = lax.ppermute(send_a, 'head', PAIR)  7.74 us
    ppermute x1, starting transfers between devices, tuned(): rest_b = lax.ppermute(total_b, 'head', PAIR)  6.65 us
    ppermute x2, starting transfers between devices, shifted(): return lax.ppermute(array, axis, pairs)  5.6 us
  transfers between devices with their start and end apart: 13, of which 8 were waited for; matrix products, arithmetic and copies ran while one was open for 1% of the time, Pallas kernels for 12%

profile of v2, /device:TPU:4, one launch (start us, length us, event | category | flops | bytes accessed | tf_op | source)
XLA Modules:
  0.0 135.1 jit_solution(15398031345990771064)
XLA Ops:
  0.6 1.4 %copy-done.6 = bf16[256,3,1024]{2,0,1:T(8,128)(2,1)S(1)} copy-done((bf16[256,3,1024]{2,0,1:T(8,128)(2,1)S(1)}, bf16[256,3,1024]{2,0,1:T(8,128)(2,1)}, u32[]{:S(2)}) %copy-start.6) | copy-done | bytes 1572888
  2.0 0.7 state.1
  2.8 1.3 collective-permute-done
  4.2 1.6 %collective-permute-start.1 = (bf16[4,128,128]{2,1,0:T(8,128)(2,1)S(1)}, bf16[4,128,128]{2,1,0:T(8,128)(2,1)S(1)}, u32[]{:S(2)}, u32[]{:S(2)}) collective-permute-start(bf16[4,128,128]{2,1,0:T(8,128)(2,1)S(1)} %add_convert_fusion.5.after), channel_id=1, source_target_pairs={{0,8},{4,12},{8,0},{12,4},{16,24},{20,28},{24,16},{28,20},{1,9},{5... | collective-permute-start | bytes 393224 | tf_op jit(solution)/shard_map/state/ppermute | solution.py:28
  5.7 0.5 collective-permute-start.2
  6.2 1.5 %collective-permute-start.3 = (bf16[4,128,128]{2,1,0:T(8,128)(2,1)S(1)}, bf16[4,128,128]{2,1,0:T(8,128)(2,1)S(1)}, u32[]{:S(2)}, u32[]{:S(2)}) collective-permute-start(bf16[4,128,128]{2,1,0:T(8,128)(2,1)S(1)} %add_convert_fusion.5.after), channel_id=1, source_target_pairs={{0,24},{4,28},{8,16},{12,20},{16,8},{20,12},{24,0},{28,4},{1,25},{... | collective-permute-start | bytes 393224 | tf_op jit(solution)/shard_map/state/ppermute | solution.py:28
  7.7 1.4 %copy-done.7 = bf16[256,3,1024]{2,0,1:T(8,128)(2,1)S(1)} copy-done((bf16[256,3,1024]{2,0,1:T(8,128)(2,1)S(1)}, bf16[256,3,1024]{2,0,1:T(8,128)(2,1)}, u32[]{:S(2)}) %copy-start.7) | copy-done | bytes 1572888
  9.1 1.0 intra.1
  10.1 3.4 %copy-done.5 = bf16[1024,4096]{1,0:T(8,128)(2,1)S(1)} copy-done((bf16[1024,4096]{1,0:T(8,128)(2,1)S(1)}, bf16[1024,4096]{1,0:T(8,128)(2,1)}, u32[]{:S(2)}) %copy-start.5) | copy-done | bytes 8388632
  13.5 0.6 load_w_out.1
  14.1 0.1 broadcast_select_fusion
  14.4 1.3 collective-permute-done.4.other_ref
  15.7 1.6 %partials.2 = (bf16[256,1024]{1,0:T(8,128)(2,1)S(1)}, bf16[128,2048]{1,0:T(8,128)(2,1)S(1)}, bf16[128,2048]{1,0:T(8,128)(2,1)S(1)}) custom-call(bf16[256,1024]{1,0:T(8,128)(2,1)S(1)} %get-tuple-element.24.q_ref, f32[256,1024]{1,0:T(8,128)S(1)} %get-tuple-element.25.intra_ref, bf16[4,128,128]{2,1,0:T(8,128)(2,1)S(1)} %broadcast_select_fusion.1.own_ref, ...), custom_call_target="tpu_custom_call" | custom-call | flops 1073741824 | bytes 4194304 | tf_op jit(solution)/shard_map/partials/pallas_call | solution.py:127
  17.3 3.3 %copy-done.2 = bf16[4,256,4096]{2,1,0:T(8,128)(2,1)} copy-done((bf16[4,256,4096]{2,1,0:T(8,128)(2,1)}, bf16[4,256,4096]{2,1,0:T(8,128)(2,1)S(1)}, u32[]{:S(2)}) %copy-start.2) | copy-done | bytes 8388632
  20.5 1.6 %collective-permute-start.5 = (bf16[128,2048]{1,0:T(8,128)(2,1)S(1)}, bf16[128,2048]{1,0:T(8,128)(2,1)S(1)}, u32[]{:S(2)}, u32[]{:S(2)}) collective-permute-start(bf16[128,2048]{1,0:T(8,128)(2,1)S(1)} %get-tuple-element.31), channel_id=1, source_target_pairs={{0,1},{1,0},{2,3},{3,2},{4,5},{5,4},{6,7},{7,6},{8,9},{9,8},{10,11... | collective-permute-start | bytes 1572872 | tf_op jit(solution)/shard_map/partials/ppermute | solution.py:378
  22.1 3.4 %copy-done.3 = bf16[4,256,4096]{2,1,0:T(8,128)(2,1)S(1)} copy-done((bf16[4,256,4096]{2,1,0:T(8,128)(2,1)S(1)}, bf16[4,256,4096]{2,1,0:T(8,128)(2,1)}, u32[]{:S(2)}) %copy-start.3) | copy-done | bytes 8388632
  25.5 1.3 partials.3
  26.8 7.7 %collective-permute-done.5 = bf16[128,2048]{1,0:T(8,128)(2,1)S(1)} collective-permute-done((bf16[128,2048]{1,0:T(8,128)(2,1)S(1)}, bf16[128,2048]{1,0:T(8,128)(2,1)S(1)}, u32[]{:S(2)}, u32[]{:S(2)}) %collective-permute-start.5) | collective-permute-done | bytes 524320 | tf_op jit(solution)/shard_map/partials/ppermute | solution.py:378
  34.5 1.6 %collective-permute-start.6 = (bf16[128,2048]{1,0:T(8,128)(2,1)S(1)}, bf16[128,2048]{1,0:T(8,128)(2,1)S(1)}, u32[]{:S(2)}, u32[]{:S(2)}) collective-permute-start(bf16[128,2048]{1,0:T(8,128)(2,1)S(1)} %get-tuple-element.32), channel_id=1, source_target_pairs={{0,1},{1,0},{2,3},{3,2},{4,5},{5,4},{6,7},{7,6},{8,9},{9,8},{10,11... | collective-permute-start | bytes 1572872 | tf_op jit(solution)/shard_map/mix/ppermute | solution.py:414
  36.1 0.1 add_convert_fusion.2
  36.2 2.5 %collective-permute-start.7 = (bf16[128,2048]{1,0:T(8,128)(2,1)S(1)}, bf16[128,2048]{1,0:T(8,128)(2,1)S(1)}, u32[]{:S(2)}, u32[]{:S(2)}) collective-permute-start(bf16[128,2048]{1,0:T(8,128)(2,1)S(1)} %add_convert_fusion.2), channel_id=1, source_target_pairs={{0,3},{3,0},{1,2},{2,1},{4,7},{7,4},{5,6},{6,5},{8,11},{11,8},{9,1... | collective-permute-start | bytes 1572872 | tf_op jit(solution)/shard_map/mix/ppermute | solution.py:416
  38.8 9.7 %collective-permute-done.6 = bf16[128,2048]{1,0:T(8,128)(2,1)S(1)} collective-permute-done((bf16[128,2048]{1,0:T(8,128)(2,1)S(1)}, bf16[128,2048]{1,0:T(8,128)(2,1)S(1)}, u32[]{:S(2)}, u32[]{:S(2)}) %collective-permute-start.6) | collective-permute-done | bytes 524320 | tf_op jit(solution)/shard_map/mix/ppermute | solution.py:414
  48.5 0.1 add_convert_fusion.3
  48.6 12.4 %collective-permute-done.7 = bf16[128,2048]{1,0:T(8,128)(2,1)S(1)} collective-permute-done((bf16[128,2048]{1,0:T(8,128)(2,1)S(1)}, bf16[128,2048]{1,0:T(8,128)(2,1)S(1)}, u32[]{:S(2)}, u32[]{:S(2)}) %collective-permute-start.7) | collective-permute-done | bytes 524320 | tf_op jit(solution)/shard_map/mix/ppermute | solution.py:416
  61.0 1.7 %collective-permute-start.8 = (bf16[128,2048]{1,0:T(8,128)(2,1)S(1)}, bf16[128,2048]{1,0:T(8,128)(2,1)S(1)}, u32[]{:S(2)}, u32[]{:S(2)}) collective-permute-start(bf16[128,2048]{1,0:T(8,128)(2,1)S(1)} %add_convert_fusion.3), channel_id=1, source_target_pairs={{0,3},{3,0},{1,2},{2,1},{4,7},{7,4},{5,6},{6,5},{8,11},{11,8},{9,1... | collective-permute-start | bytes 1572872 | tf_op jit(solution)/shard_map/mix/ppermute | solution.py:419
  62.7 0.5 multiply_sine_fusion
  63.3 0.1 add_convert_fusion.a_ref.x_ref.t_ref
  63.4 10.7 %collective-permute-start.9 = (bf16[128,2048]{1,0:T(8,128)(2,1)S(1)}, bf16[128,2048]{1,0:T(8,128)(2,1)S(1)}, u32[]{:S(2)}, u32[]{:S(2)}) collective-permute-start(bf16[128,2048]{1,0:T(8,128)(2,1)S(1)} %add_convert_fusion.a_ref.x_ref.t_ref), channel_id=1, source_target_pairs={{0,1},{1,0},{2,3},{3,2},{4,5},{5,4},{6,7},{7,6},{8,9},{9,8},{10,11... | collective-permute-start | bytes 1572872 | tf_op jit(solution)/shard_map/mix/ppermute | solution.py:421
  74.1 3.6 %collective-permute-done.8 = bf16[128,2048]{1,0:T(8,128)(2,1)S(1)} collective-permute-done((bf16[128,2048]{1,0:T(8,128)(2,1)S(1)}, bf16[128,2048]{1,0:T(8,128)(2,1)S(1)}, u32[]{:S(2)}, u32[]{:S(2)}) %collective-permute-start.8) | collective-permute-done | bytes 524320 | tf_op jit(solution)/shard_map/mix/ppermute | solution.py:419
  77.7 0.1 add_convert_fusion.1.x_ref.t_ref
  77.8 6.7 %collective-permute-start.10 = (bf16[128,2048]{1,0:T(8,128)(2,1)S(1)}, bf16[128,2048]{1,0:T(8,128)(2,1)S(1)}, u32[]{:S(2)}, u32[]{:S(2)}) collective-permute-start(bf16[128,2048]{1,0:T(8,128)(2,1)S(1)} %add_convert_fusion.1.x_ref.t_ref), channel_id=1, source_target_pairs={{0,1},{1,0},{2,3},{3,2},{4,5},{5,4},{6,7},{7,6},{8,9},{9,8},{10,11... | collective-permute-start | bytes 1572872 | tf_op jit(solution)/shard_map/mix/ppermute | solution.py:423
  84.5 0.1 pad_maximum_fusion
  84.6 8.1 %copy-done.4 = bf16[4096,3,1024]{2,0,1:T(8,128)(2,1)S(1)} copy-done((bf16[4096,3,1024]{2,0,1:T(8,128)(2,1)S(1)}, bf16[4096,3,1024]{2,0,1:T(8,128)(2,1)}, u32[]{:S(2)}) %copy-start.4) | copy-done | bytes 25165848
  92.8 1.8 %load_w_qkv.1 = bf16[12,1024,1024]{2,1,0:T(8,128)(2,1)S(1)} custom-call(bf16[12,1024,1024]{2,1,0:T(8,128)(2,1)S(1)} %bitcast.15, bf16[128,2048]{1,0:T(8,128)(2,1)S(1)} %get-tuple-element.33.after), custom_call_target="tpu_custom_call" | custom-call | bytes 25165824 | tf_op jit(solution)/shard_map/load_w_qkv/pallas_call | solution.py:127
  94.6 8.3 %copy-done = bf16[12,1024,1024]{2,1,0:T(8,128)(2,1)} copy-done((bf16[12,1024,1024]{2,1,0:T(8,128)(2,1)}, bf16[12,1024,1024]{2,1,0:T(8,128)(2,1)S(1)}, u32[]{:S(2)}) %copy-start) | copy-done | bytes 25165848
  102.9 8.2 %copy-done.1 = bf16[12,1024,1024]{2,1,0:T(8,128)(2,1)S(1)} copy-done((bf16[12,1024,1024]{2,1,0:T(8,128)(2,1)S(1)}, bf16[12,1024,1024]{2,1,0:T(8,128)(2,1)}, u32[]{:S(2)}) %copy-start.1) | copy-done | bytes 25165848
  111.1 1.8 %project_a.3.acc_ref = f32[3,128,1024]{2,1,0:T(8,128)S(1)} custom-call(bf16[128,2048]{1,0:T(8,128)(2,1)S(1)} %add_convert_fusion.a_ref.x_ref.t_ref, bf16[3,4096,1024]{2,1,0:T(8,128)(2,1)S(1)} %bitcast.7), custom_call_target="tpu_custom_call" | custom-call | flops 1610612736 | bytes 12582912 | tf_op jit(solution)/shard_map/project_a/pallas_call | solution.py:127
  112.9 1.5 %project_a.4 = (bf16[2,128,1024]{2,1,0:T(8,128)(2,1)S(1)}, f32[128,128]{1,0:T(8,128)S(1)}) custom-call(bf16[128,2048]{1,0:T(8,128)(2,1)S(1)} %add_convert_fusion.a_ref.x_ref.t_ref, bf16[128,2048]{1,0:T(8,128)(2,1)S(1)} %collective-permute-done.9.x_ref, bf16[3,4096,1024]{2,1,0:T(8,128)(2,1)S(1)} %bitcast.8, f32[3,128,1024]{2,1,0:T(8,128)S(1)} %project_a.3.acc_ref, ...), custom_call_target="tpu_custom_call" | custom-call | flops 1610612736 | bytes 12582912 | tf_op jit(solution)/shard_map/project_a/pallas_call | solution.py:127
  114.4 2.1 %collective-permute-start.12 = (bf16[2,128,1024]{2,1,0:T(8,128)(2,1)S(1)}, bf16[2,128,1024]{2,1,0:T(8,128)(2,1)S(1)}, u32[]{:S(2)}, u32[]{:S(2)}) collective-permute-start(bf16[2,128,1024]{2,1,0:T(8,128)(2,1)S(1)} %get-tuple-element.42.a_ref), channel_id=1, source_target_pairs={{0,4},{4,8},{8,12},{12,16},{16,20},{20,24},{24,28},{1,5},{5,9},{9,... | collective-permute-start | bytes 1572872 | tf_op jit(solution)/shard_map/project_a/ppermute | solution.py:24
  116.5 2.5 %project_b.3 = (f32[3,128,1024]{2,1,0:T(8,128)S(1)}, bf16[256,1024]{1,0:T(8,128)(2,1)}) custom-call(bf16[128,2048]{1,0:T(8,128)(2,1)S(1)} %add_convert_fusion.1.x_ref.t_ref, bf16[3,4096,1024]{2,1,0:T(8,128)(2,1)S(1)} %bitcast.9, bf16[128,2048]{1,0:T(8,128)(2,1)S(1)} %add_convert_fusion.a_ref.x_ref.t_ref), custom_call_target="tpu_custom_call" | custom-call | flops 1610612736 | bytes 12582912 | tf_op jit(solution)/shard_map/project_b/pallas_call | solution.py:127
  119.0 1.4 %project_b.4 = (bf16[2,128,1024]{2,1,0:T(8,128)(2,1)S(1)}, f32[128,128]{1,0:T(8,128)S(1)}) custom-call(bf16[128,2048]{1,0:T(8,128)(2,1)S(1)} %add_convert_fusion.1.x_ref.t_ref, bf16[128,2048]{1,0:T(8,128)(2,1)S(1)} %collective-permute-done.10.x_ref, bf16[3,4096,1024]{2,1,0:T(8,128)(2,1)S(1)} %bitcast.10, f32[3,128,1024]{2,1,0:T(8,128)S(1)} %get-tuple-element.39.acc_ref, ...), custom_call_target="tpu_custom_call" | custom-call | flops 1610612736 | bytes 12582912 | tf_op jit(solution)/shard_map/project_b/pallas_call | solution.py:127
  120.4 3.5 %collective-permute-start.11 = (bf16[2,128,1024]{2,1,0:T(8,128)(2,1)S(1)}, bf16[2,128,1024]{2,1,0:T(8,128)(2,1)S(1)}, u32[]{:S(2)}, u32[]{:S(2)}) collective-permute-start(bf16[2,128,1024]{2,1,0:T(8,128)(2,1)S(1)} %get-tuple-element.41.b_ref), channel_id=1, source_target_pairs={{0,4},{4,8},{8,12},{12,16},{16,20},{20,24},{24,28},{1,5},{5,9},{9,... | collective-permute-start | bytes 1572872 | tf_op jit(solution)/shard_map/project_b/ppermute | solution.py:24
  123.9 0.8 project_a.5.qa_ref
  124.8 0.8 project_b.5.qb_ref
  125.7 0.1 collective-permute-done.12.pa_ref
  125.8 2.4 %attend.2 = (f32[256,1024]{1,0:T(8,128)S(1)}, f32[8,256,1]{2,1,0:T(8,128)S(1)}, f32[8,256,1]{2,1,0:T(8,128)S(1)}) custom-call(bf16[128,1024]{1,0:T(8,128)(2,1)S(1)} %project_a.5.qa_ref, bf16[128,1024]{1,0:T(8,128)(2,1)S(1)} %project_b.5.qb_ref, bf16[2,128,1024]{2,1,0:T(8,128)(2,1)S(1)} %get-tuple-element.42.a_ref, ...), custom_call_target="tpu_custom_call" | custom-call | flops 402653184 | bytes 3145728 | tf_op jit(solution)/shard_map/attend/pallas_call | solution.py:127
  128.2 3.7 %collective-permute-done.11.pb_ref = bf16[2,128,1024]{2,1,0:T(8,128)(2,1)S(1)} collective-permute-done((bf16[2,128,1024]{2,1,0:T(8,128)(2,1)S(1)}, bf16[2,128,1024]{2,1,0:T(8,128)(2,1)S(1)}, u32[]{:S(2)}, u32[]{:S(2)}) %collective-permute-start.11) | collective-permute-done | bytes 524320 | tf_op jit(solution)/shard_map/project_b/ppermute | solution.py:24
  131.8 3.2 %attend.3 = bf16[256,1024]{1,0:T(8,128)(2,1)} custom-call(bf16[128,1024]{1,0:T(8,128)(2,1)S(1)} %project_a.5.qa_ref, bf16[128,1024]{1,0:T(8,128)(2,1)S(1)} %project_b.5.qb_ref, bf16[2,128,1024]{2,1,0:T(8,128)(2,1)S(1)} %collective-permute-done.11.pb_ref, f32[256,1024]{1,0:T(8,128)S(1)} %get-tuple-element.43.acc_ref, ...), custom_call_target="tpu_custom_call" | custom-call | flops 134217728 | bytes 3145728 | tf_op jit(solution)/shard_map/attend/pallas_call | solution.py:127
  (21 shorter events, 0.3 us)
Async XLA Ops:
  0.6 1.4 %copy-start.6 = (bf16[256,3,1024]{2,0,1:T(8,128)(2,1)S(1)}, bf16[256,3,1024]{2,0,1:T(8,128)(2,1)}, u32[]{:S(2)}) copy-start(bf16[256,3,1024]{2,0,1:T(8,128)(2,1)} %param.4) | copy-start | bytes 4718596
  2.7 1.4 %collective-permute-start = (bf16[4,128,128]{2,1,0:T(8,128)(2,1)S(1)}, bf16[4,128,128]{2,1,0:T(8,128)(2,1)S(1)}, u32[]{:S(2)}, u32[]{:S(2)}) collective-permute-start(bf16[4,128,128]{2,1,0:T(8,128)(2,1)S(1)} %get-tuple-element.27), channel_id=1, source_target_pairs={{0,4},{4,0},{8,12},{12,8},{16,20},{20,16},{24,28},{28,24},{1,5},{5... | collective-permute-start | bytes 393224 | tf_op jit(solution)/shard_map/state/ppermute | solution.py:28
  4.2 9.9 %collective-permute-start.1 = (bf16[4,128,128]{2,1,0:T(8,128)(2,1)S(1)}, bf16[4,128,128]{2,1,0:T(8,128)(2,1)S(1)}, u32[]{:S(2)}, u32[]{:S(2)}) collective-permute-start(bf16[4,128,128]{2,1,0:T(8,128)(2,1)S(1)} %add_convert_fusion.5.after), channel_id=1, source_target_pairs={{0,8},{4,12},{8,0},{12,4},{16,24},{20,28},{24,16},{28,20},{1,9},{5... | collective-permute-start | bytes 393224 | tf_op jit(solution)/shard_map/state/ppermute | solution.py:28
  5.7 8.4 %collective-permute-start.2 = (bf16[4,128,128]{2,1,0:T(8,128)(2,1)S(1)}, bf16[4,128,128]{2,1,0:T(8,128)(2,1)S(1)}, u32[]{:S(2)}, u32[]{:S(2)}) collective-permute-start(bf16[4,128,128]{2,1,0:T(8,128)(2,1)S(1)} %add_convert_fusion.5.after), channel_id=1, source_target_pairs={{0,16},{4,20},{8,24},{12,28},{16,0},{20,4},{24,8},{28,12},{1,17},{... | collective-permute-start | bytes 393224 | tf_op jit(solution)/shard_map/state/ppermute | solution.py:28
  6.2 7.9 %collective-permute-start.3 = (bf16[4,128,128]{2,1,0:T(8,128)(2,1)S(1)}, bf16[4,128,128]{2,1,0:T(8,128)(2,1)S(1)}, u32[]{:S(2)}, u32[]{:S(2)}) collective-permute-start(bf16[4,128,128]{2,1,0:T(8,128)(2,1)S(1)} %add_convert_fusion.5.after), channel_id=1, source_target_pairs={{0,24},{4,28},{8,16},{12,20},{16,8},{20,12},{24,0},{28,4},{1,25},{... | collective-permute-start | bytes 393224 | tf_op jit(solution)/shard_map/state/ppermute | solution.py:28
  7.7 1.4 %copy-start.7 = (bf16[256,3,1024]{2,0,1:T(8,128)(2,1)S(1)}, bf16[256,3,1024]{2,0,1:T(8,128)(2,1)}, u32[]{:S(2)}) copy-start(bf16[256,3,1024]{2,0,1:T(8,128)(2,1)} %param.4) | copy-start | bytes 4718596
  10.1 3.4 %copy-start.5 = (bf16[1024,4096]{1,0:T(8,128)(2,1)S(1)}, bf16[1024,4096]{1,0:T(8,128)(2,1)}, u32[]{:S(2)}) copy-start(bf16[1024,4096]{1,0:T(8,128)(2,1)} %param.6) | copy-start | bytes 25165828
  14.1 8.0 %copy-start.8 = (bf16[256,1024]{1,0:T(8,128)(2,1)S(1)}, bf16[256,1024]{1,0:T(8,128)(2,1)}, u32[]{:S(2)}) copy-start(bf16[256,1024]{1,0:T(8,128)(2,1)} %r_ref.1) | copy-start | bytes 1572868
  14.3 1.4 %collective-permute-start.4 = (bf16[4,128,128]{2,1,0:T(8,128)(2,1)S(1)}, bf16[4,128,128]{2,1,0:T(8,128)(2,1)S(1)}, u32[]{:S(2)}, u32[]{:S(2)}) collective-permute-start(bf16[4,128,128]{2,1,0:T(8,128)(2,1)S(1)} %get-tuple-element.46), channel_id=1, source_target_pairs={{0,4},{4,0},{8,12},{12,8},{16,20},{20,16},{24,28},{28,24},{1,5},{5... | collective-permute-start | bytes 393224 | tf_op jit(solution)/shard_map/prefix/ppermute | solution.py:28
  17.3 3.3 %copy-start.2 = (bf16[4,256,4096]{2,1,0:T(8,128)(2,1)}, bf16[4,256,4096]{2,1,0:T(8,128)(2,1)S(1)}, u32[]{:S(2)}) copy-start(bf16[4,256,4096]{2,1,0:T(8,128)(2,1)S(1)} %load_w_out.1) | copy-start | bytes 25165828
  20.5 14.0 %collective-permute-start.5 = (bf16[128,2048]{1,0:T(8,128)(2,1)S(1)}, bf16[128,2048]{1,0:T(8,128)(2,1)S(1)}, u32[]{:S(2)}, u32[]{:S(2)}) collective-permute-start(bf16[128,2048]{1,0:T(8,128)(2,1)S(1)} %get-tuple-element.31), channel_id=1, source_target_pairs={{0,1},{1,0},{2,3},{3,2},{4,5},{5,4},{6,7},{7,6},{8,9},{9,8},{10,11... | collective-permute-start | bytes 1572872 | tf_op jit(solution)/shard_map/partials/ppermute | solution.py:378
  22.1 3.4 %copy-start.3 = (bf16[4,256,4096]{2,1,0:T(8,128)(2,1)S(1)}, bf16[4,256,4096]{2,1,0:T(8,128)(2,1)}, u32[]{:S(2)}) copy-start(bf16[4,256,4096]{2,1,0:T(8,128)(2,1)} %copy-done.2) | copy-start | bytes 25165828
  34.5 14.0 %collective-permute-start.6 = (bf16[128,2048]{1,0:T(8,128)(2,1)S(1)}, bf16[128,2048]{1,0:T(8,128)(2,1)S(1)}, u32[]{:S(2)}, u32[]{:S(2)}) collective-permute-start(bf16[128,2048]{1,0:T(8,128)(2,1)S(1)} %get-tuple-element.32), channel_id=1, source_target_pairs={{0,1},{1,0},{2,3},{3,2},{4,5},{5,4},{6,7},{7,6},{8,9},{9,8},{10,11... | collective-permute-start | bytes 1572872 | tf_op jit(solution)/shard_map/mix/ppermute | solution.py:414
  36.2 24.8 %collective-permute-start.7 = (bf16[128,2048]{1,0:T(8,128)(2,1)S(1)}, bf16[128,2048]{1,0:T(8,128)(2,1)S(1)}, u32[]{:S(2)}, u32[]{:S(2)}) collective-permute-start(bf16[128,2048]{1,0:T(8,128)(2,1)S(1)} %add_convert_fusion.2), channel_id=1, source_target_pairs={{0,3},{3,0},{1,2},{2,1},{4,7},{7,4},{5,6},{6,5},{8,11},{11,8},{9,1... | collective-permute-start | bytes 1572872 | tf_op jit(solution)/shard_map/mix/ppermute | solution.py:416
  61.0 16.7 %collective-permute-start.8 = (bf16[128,2048]{1,0:T(8,128)(2,1)S(1)}, bf16[128,2048]{1,0:T(8,128)(2,1)S(1)}, u32[]{:S(2)}, u32[]{:S(2)}) collective-permute-start(bf16[128,2048]{1,0:T(8,128)(2,1)S(1)} %add_convert_fusion.3), channel_id=1, source_target_pairs={{0,3},{3,0},{1,2},{2,1},{4,7},{7,4},{5,6},{6,5},{8,11},{11,8},{9,1... | collective-permute-start | bytes 1572872 | tf_op jit(solution)/shard_map/mix/ppermute | solution.py:419
  63.4 49.5 %collective-permute-start.9 = (bf16[128,2048]{1,0:T(8,128)(2,1)S(1)}, bf16[128,2048]{1,0:T(8,128)(2,1)S(1)}, u32[]{:S(2)}, u32[]{:S(2)}) collective-permute-start(bf16[128,2048]{1,0:T(8,128)(2,1)S(1)} %add_convert_fusion.a_ref.x_ref.t_ref), channel_id=1, source_target_pairs={{0,1},{1,0},{2,3},{3,2},{4,5},{5,4},{6,7},{7,6},{8,9},{9,8},{10,11... | collective-permute-start | bytes 1572872 | tf_op jit(solution)/shard_map/mix/ppermute | solution.py:421
  77.8 41.1 %collective-permute-start.10 = (bf16[128,2048]{1,0:T(8,128)(2,1)S(1)}, bf16[128,2048]{1,0:T(8,128)(2,1)S(1)}, u32[]{:S(2)}, u32[]{:S(2)}) collective-permute-start(bf16[128,2048]{1,0:T(8,128)(2,1)S(1)} %add_convert_fusion.1.x_ref.t_ref), channel_id=1, source_target_pairs={{0,1},{1,0},{2,3},{3,2},{4,5},{5,4},{6,7},{7,6},{8,9},{9,8},{10,11... | collective-permute-start | bytes 1572872 | tf_op jit(solution)/shard_map/mix/ppermute | solution.py:423
  84.6 8.2 %copy-start.4 = (bf16[4096,3,1024]{2,0,1:T(8,128)(2,1)S(1)}, bf16[4096,3,1024]{2,0,1:T(8,128)(2,1)}, u32[]{:S(2)}) copy-start(bf16[4096,3,1024]{2,0,1:T(8,128)(2,1)} %param.7) | copy-start | bytes 75497472
  94.6 8.3 %copy-start = (bf16[12,1024,1024]{2,1,0:T(8,128)(2,1)}, bf16[12,1024,1024]{2,1,0:T(8,128)(2,1)S(1)}, u32[]{:S(2)}) copy-start(bf16[12,1024,1024]{2,1,0:T(8,128)(2,1)S(1)} %load_w_qkv.1) | copy-start | bytes 75497472
  102.9 8.2 %copy-start.1 = (bf16[12,1024,1024]{2,1,0:T(8,128)(2,1)S(1)}, bf16[12,1024,1024]{2,1,0:T(8,128)(2,1)}, u32[]{:S(2)}) copy-start(bf16[12,1024,1024]{2,1,0:T(8,128)(2,1)} %copy-done) | copy-start | bytes 75497472
  114.4 11.4 %collective-permute-start.12 = (bf16[2,128,1024]{2,1,0:T(8,128)(2,1)S(1)}, bf16[2,128,1024]{2,1,0:T(8,128)(2,1)S(1)}, u32[]{:S(2)}, u32[]{:S(2)}) collective-permute-start(bf16[2,128,1024]{2,1,0:T(8,128)(2,1)S(1)} %get-tuple-element.42.a_ref), channel_id=1, source_target_pairs={{0,4},{4,8},{8,12},{12,16},{16,20},{20,24},{24,28},{1,5},{5,9},{9,... | collective-permute-start | bytes 1572872 | tf_op jit(solution)/shard_map/project_a/ppermute | solution.py:24
  120.4 11.4 %collective-permute-start.11 = (bf16[2,128,1024]{2,1,0:T(8,128)(2,1)S(1)}, bf16[2,128,1024]{2,1,0:T(8,128)(2,1)S(1)}, u32[]{:S(2)}, u32[]{:S(2)}) collective-permute-start(bf16[2,128,1024]{2,1,0:T(8,128)(2,1)S(1)} %get-tuple-element.41.b_ref), channel_id=1, source_target_pairs={{0,4},{4,8},{8,12},{12,16},{16,20},{20,24},{24,28},{1,5},{5,9},{9,... | collective-permute-start | bytes 1572872 | tf_op jit(solution)/shard_map/project_b/ppermute | solution.py:24

commit v3 on v2

--- a/solution.py
+++ b/solution.py
@@ -136,19 +136,31 @@
 
 
 def load_body(source, after, target, sems):
+    rows = source.shape[-2] // sems.shape[1]
     copies = []
-    for i in range(sems.shape[0]):
-        copy = pltpu.make_async_copy(source.at[i], target.at[i], sems.at[i])
-        copy.start()
-        copies.append(copy)
+    for plane in range(sems.shape[0]):
+        for i in range(sems.shape[1]):
+            piece = (plane, pl.ds(i * rows, rows)) if len(source.shape) == 3 else pl.ds(i * rows, rows)
+            copy = pltpu.make_async_copy(source.at[piece], target.at[piece], sems.at[plane, i])
+            copy.start()
+            copies.append(copy)
     for copy in copies:
         copy.wait()
 
 
+def in_hbm(array):
+    return pltpu.with_memory_space_constraint(array, pltpu.HBM)
+
+
+def in_vmem(array):
+    return pltpu.with_memory_space_constraint(array, pltpu.VMEM)
+
+
 def loaded(array, after):
+    planes = array.shape[0] if array.ndim == 3 else 1
     return call(
-        load_body, (array, after), pltpu.VMEM(array.shape, array.dtype),
-        [IN_HBM, ANYWHERE], (pltpu.SemaphoreType.DMA((array.shape[0],)),), vmem=4, moved=2 * array.size,
+        load_body, (in_hbm(array), after), pltpu.VMEM(array.shape, array.dtype),
+        [IN_HBM, ANYWHERE], (pltpu.SemaphoreType.DMA((planes, 4)),), vmem=4, moved=2 * array.size,
     )
 
 
@@ -336,7 +348,7 @@
     with jax.named_scope("state"):
         states = shape((group, HD, HD), BF16)
         send, keep = call(
-            state_body, (qkv,), (states, states), [IN_HBM],
+            state_body, (in_hbm(qkv),), (states, states), [IN_HBM],
             (
                 pltpu.VMEM((2, rows, width // 2), BF16),
                 pltpu.VMEM((2, rows, width // 2), BF16),
@@ -355,7 +367,7 @@
             flops=4 * rows * rows * width, moved=10 * rows * width,
         )
     with jax.named_scope("load_w_out"):
-        w_out_here = loaded(w_out.reshape(4, width // 4, full), chip_total).reshape(width, full)
+        w_out_here = in_vmem(loaded(w_out, chip_total))
     with jax.named_scope("prefix"):
         x_bit = ((seq // 2) % 2).astype(F32)
         y_bit = (seq // 4).astype(F32)
@@ -381,8 +393,7 @@
             flops=rows * width * full, moved=width * full,
         )
     with jax.named_scope("load_w_qkv"):
-        w_here = loaded(wqkv.reshape(3, 4, width, width).reshape(12, width, width), mine_a)
-        w_here = w_here.reshape(3, full, width)
+        w_here = in_vmem(loaded(wqkv, mine_a))
 
     positions = seq * rows + jnp.arange(rows, dtype=jnp.int32)
     freq = 500000.0 ** (-(jnp.arange(HD // 2, dtype=F32) * 2.0 / HD))

time: 135 us -> 116 us (0.86)
  local copies, waits for them, and re-layouts: 37.4 us -> 8.06 us
  Pallas kernels: 21.4 us -> 31.9 us
    unnamed x18 -> x8, local copies, waits for them, and re-layouts: 37.4 us -> 8.06 us
    pallas_call x14, Pallas kernels: 21.4 us -> 31.9 us  [call(): pl.pallas_call(body, in_specs=in_specs or [ON_CHIP] * len(ins), out_specs...]
  transfers between devices with their start and end apart: 13 -> 13, of which waited for: 8 -> 9; matrix products, arithmetic and copies ran while one was open for 1% -> 1% of each run, Pallas kernels for 12% -> 22%
where the time goes in v3:
time: 116 us
  waiting for transfers between devices  40.2 us (35%)
  starting transfers between devices  33.9 us (29%)
  Pallas kernels  31.9 us (28%)
  local copies, waits for them, and re-layouts  8.06 us (7%)
  other arithmetic  1.38 us (1%)
    pallas_call x14, Pallas kernels, call(): pl.pallas_call(body, in_specs=in_specs or [ON_CHIP] * len(ins), out_specs...  31.9 us
    ppermute x1, waiting for transfers between devices, tuned(): far_a = lax.ppermute(sum_a, 'head', CROSS)  12.4 us
    ppermute x1, starting transfers between devices, tuned(): rest_a = lax.ppermute(total_a, 'head', PAIR)  10.7 us
    ppermute x1, waiting for transfers between devices, tuned(): got_b = lax.ppermute(send_b, 'head', PAIR)  9.7 us
    unnamed x8, local copies, waits for them, and re-layouts  8.06 us
    ppermute x1, waiting for transfers between devices, tuned(): got_a = lax.ppermute(send_a, 'head', PAIR)  7.74 us
    ppermute x1, starting transfers between devices, tuned(): rest_b = lax.ppermute(total_b, 'head', PAIR)  6.66 us
    ppermute x2, starting transfers between devices, shifted(): return lax.ppermute(array, axis, pairs)  5.45 us
  transfers between devices with their start and end apart: 13, of which 9 were waited for; matrix products, arithmetic and copies ran while one was open for 1% of the time, Pallas kernels for 22%

profile of v3, /device:TPU:4, one launch (start us, length us, event | category | flops | bytes accessed | tf_op | source)
XLA Modules:
  0.0 116.3 jit_solution(14805522504636092669)
XLA Ops:
  0.6 1.6 %state.1 = (bf16[4,128,128]{2,1,0:T(8,128)(2,1)S(1)}, bf16[4,128,128]{2,1,0:T(8,128)(2,1)S(1)}) custom-call(bf16[3,256,1024]{2,1,0:T(8,128)(2,1)} %bitcast.2), custom_call_target="tpu_custom_call" | custom-call | flops 67108864 | bytes 1048576 | tf_op jit(solution)/shard_map/state/pallas_call | solution.py:127
  2.3 0.1 collective-permute-start
  2.3 1.3 %collective-permute-done = bf16[4,128,128]{2,1,0:T(8,128)(2,1)S(1)} collective-permute-done((bf16[4,128,128]{2,1,0:T(8,128)(2,1)S(1)}, bf16[4,128,128]{2,1,0:T(8,128)(2,1)S(1)}, u32[]{:S(2)}, u32[]{:S(2)}) %collective-permute-start) | collective-permute-done | bytes 131104 | tf_op jit(solution)/shard_map/state/ppermute | solution.py:28
  3.7 1.6 %collective-permute-start.1 = (bf16[4,128,128]{2,1,0:T(8,128)(2,1)S(1)}, bf16[4,128,128]{2,1,0:T(8,128)(2,1)S(1)}, u32[]{:S(2)}, u32[]{:S(2)}) collective-permute-start(bf16[4,128,128]{2,1,0:T(8,128)(2,1)S(1)} %add_convert_fusion.5.after), channel_id=1, source_target_pairs={{0,8},{4,12},{8,0},{12,4},{16,24},{20,28},{24,16},{28,20},{1,9},{5... | collective-permute-start | bytes 393224 | tf_op jit(solution)/shard_map/state/ppermute | solution.py:28
  5.3 0.5 collective-permute-start.2
  5.8 1.5 %collective-permute-start.3 = (bf16[4,128,128]{2,1,0:T(8,128)(2,1)S(1)}, bf16[4,128,128]{2,1,0:T(8,128)(2,1)S(1)}, u32[]{:S(2)}, u32[]{:S(2)}) collective-permute-start(bf16[4,128,128]{2,1,0:T(8,128)(2,1)S(1)} %add_convert_fusion.5.after), channel_id=1, source_target_pairs={{0,24},{4,28},{8,16},{12,20},{16,8},{20,12},{24,0},{28,4},{1,25},{... | collective-permute-start | bytes 393224 | tf_op jit(solution)/shard_map/state/ppermute | solution.py:28
  7.3 1.4 %copy-done.2 = bf16[256,3,1024]{2,0,1:T(8,128)(2,1)S(1)} copy-done((bf16[256,3,1024]{2,0,1:T(8,128)(2,1)S(1)}, bf16[256,3,1024]{2,0,1:T(8,128)(2,1)}, u32[]{:S(2)}) %copy-start.2) | copy-done | bytes 1572888
  8.7 1.0 intra.1
  9.7 3.5 %load_w_out.1.w_ref = bf16[1024,4096]{1,0:T(8,128)(2,1)S(1)} custom-call(bf16[1024,4096]{1,0:T(8,128)(2,1)} %source.1, bf16[4,128,128]{2,1,0:T(8,128)(2,1)S(1)} %add_convert_fusion.5.after), custom_call_target="tpu_custom_call" | custom-call | bytes 8388608 | tf_op jit(solution)/shard_map/load_w_out/pallas_call | solution.py:127
  13.2 0.0 copy-start.3
  13.2 0.0 collective-permute-done.1
  13.2 0.2 collective-permute-done.2
  13.4 0.1 broadcast_select_fusion
  13.5 0.1 collective-permute-start.4
  13.6 1.3 %collective-permute-done.4.other_ref = bf16[4,128,128]{2,1,0:T(8,128)(2,1)S(1)} collective-permute-done((bf16[4,128,128]{2,1,0:T(8,128)(2,1)S(1)}, bf16[4,128,128]{2,1,0:T(8,128)(2,1)S(1)}, u32[]{:S(2)}, u32[]{:S(2)}) %collective-permute-start.4) | collective-permute-done | bytes 131104 | tf_op jit(solution)/shard_map/prefix/ppermute | solution.py:28
  14.9 1.6 %partials.2 = (bf16[256,1024]{1,0:T(8,128)(2,1)S(1)}, bf16[128,2048]{1,0:T(8,128)(2,1)S(1)}, bf16[128,2048]{1,0:T(8,128)(2,1)S(1)}) custom-call(bf16[256,1024]{1,0:T(8,128)(2,1)S(1)} %get-tuple-element.24.q_ref, f32[256,1024]{1,0:T(8,128)S(1)} %get-tuple-element.25.intra_ref, bf16[4,128,128]{2,1,0:T(8,128)(2,1)S(1)} %broadcast_select_fusion.1.own_ref, ...), custom_call_target="tpu_custom_call" | custom-call | flops 1073741824 | bytes 4194304 | tf_op jit(solution)/shard_map/partials/pallas_call | solution.py:127
  16.5 3.3 %copy-done = bf16[1024,4096]{1,0:T(8,128)(2,1)} copy-done((bf16[1024,4096]{1,0:T(8,128)(2,1)}, bf16[1024,4096]{1,0:T(8,128)(2,1)S(1)}, u32[]{:S(2)}) %copy-start) | copy-done | bytes 8388632
  19.8 1.6 %collective-permute-start.5 = (bf16[128,2048]{1,0:T(8,128)(2,1)S(1)}, bf16[128,2048]{1,0:T(8,128)(2,1)S(1)}, u32[]{:S(2)}, u32[]{:S(2)}) collective-permute-start(bf16[128,2048]{1,0:T(8,128)(2,1)S(1)} %get-tuple-element.31), channel_id=1, source_target_pairs={{0,1},{1,0},{2,3},{3,2},{4,5},{5,4},{6,7},{7,6},{8,9},{9,8},{10,11... | collective-permute-start | bytes 1572872 | tf_op jit(solution)/shard_map/partials/ppermute | solution.py:390
  21.4 3.4 %copy-done.1 = bf16[1024,4096]{1,0:T(8,128)(2,1)S(1)} copy-done((bf16[1024,4096]{1,0:T(8,128)(2,1)S(1)}, bf16[1024,4096]{1,0:T(8,128)(2,1)}, u32[]{:S(2)}) %copy-start.1) | copy-done | bytes 8388632
  24.7 1.3 %partials.3 = (bf16[128,2048]{1,0:T(8,128)(2,1)S(1)}, bf16[128,2048]{1,0:T(8,128)(2,1)S(1)}) custom-call(bf16[256,1024]{1,0:T(8,128)(2,1)S(1)} %get-tuple-element.28.lin_ref, bf16[1024,4096]{1,0:T(8,128)(2,1)S(1)} %copy-done.1, bf16[256,1024]{1,0:T(8,128)(2,1)S(1)} %copy-done.3), custom_call_target="tpu_custom_call" | custom-call | flops 1073741824 | bytes 4194304 | tf_op jit(solution)/shard_map/partials/pallas_call | solution.py:127
  26.0 7.7 %collective-permute-done.5 = bf16[128,2048]{1,0:T(8,128)(2,1)S(1)} collective-permute-done((bf16[128,2048]{1,0:T(8,128)(2,1)S(1)}, bf16[128,2048]{1,0:T(8,128)(2,1)S(1)}, u32[]{:S(2)}, u32[]{:S(2)}) %collective-permute-start.5) | collective-permute-done | bytes 524320 | tf_op jit(solution)/shard_map/partials/ppermute | solution.py:390
  33.8 1.6 %collective-permute-start.6 = (bf16[128,2048]{1,0:T(8,128)(2,1)S(1)}, bf16[128,2048]{1,0:T(8,128)(2,1)S(1)}, u32[]{:S(2)}, u32[]{:S(2)}) collective-permute-start(bf16[128,2048]{1,0:T(8,128)(2,1)S(1)} %get-tuple-element.32), channel_id=1, source_target_pairs={{0,1},{1,0},{2,3},{3,2},{4,5},{5,4},{6,7},{7,6},{8,9},{9,8},{10,11... | collective-permute-start | bytes 1572872 | tf_op jit(solution)/shard_map/mix/ppermute | solution.py:425
  35.3 0.1 add_convert_fusion.2
  35.5 2.5 %collective-permute-start.7 = (bf16[128,2048]{1,0:T(8,128)(2,1)S(1)}, bf16[128,2048]{1,0:T(8,128)(2,1)S(1)}, u32[]{:S(2)}, u32[]{:S(2)}) collective-permute-start(bf16[128,2048]{1,0:T(8,128)(2,1)S(1)} %add_convert_fusion.2), channel_id=1, source_target_pairs={{0,3},{3,0},{1,2},{2,1},{4,7},{7,4},{5,6},{6,5},{8,11},{11,8},{9,1... | collective-permute-start | bytes 1572872 | tf_op jit(solution)/shard_map/mix/ppermute | solution.py:427
  38.0 9.7 %collective-permute-done.6 = bf16[128,2048]{1,0:T(8,128)(2,1)S(1)} collective-permute-done((bf16[128,2048]{1,0:T(8,128)(2,1)S(1)}, bf16[128,2048]{1,0:T(8,128)(2,1)S(1)}, u32[]{:S(2)}, u32[]{:S(2)}) %collective-permute-start.6) | collective-permute-done | bytes 524320 | tf_op jit(solution)/shard_map/mix/ppermute | solution.py:425
  47.7 0.1 add_convert_fusion.3
  47.8 12.4 %collective-permute-done.7 = bf16[128,2048]{1,0:T(8,128)(2,1)S(1)} collective-permute-done((bf16[128,2048]{1,0:T(8,128)(2,1)S(1)}, bf16[128,2048]{1,0:T(8,128)(2,1)S(1)}, u32[]{:S(2)}, u32[]{:S(2)}) %collective-permute-start.7) | collective-permute-done | bytes 524320 | tf_op jit(solution)/shard_map/mix/ppermute | solution.py:427
  60.3 1.7 %collective-permute-start.8 = (bf16[128,2048]{1,0:T(8,128)(2,1)S(1)}, bf16[128,2048]{1,0:T(8,128)(2,1)S(1)}, u32[]{:S(2)}, u32[]{:S(2)}) collective-permute-start(bf16[128,2048]{1,0:T(8,128)(2,1)S(1)} %add_convert_fusion.3), channel_id=1, source_target_pairs={{0,3},{3,0},{1,2},{2,1},{4,7},{7,4},{5,6},{6,5},{8,11},{11,8},{9,1... | collective-permute-start | bytes 1572872 | tf_op jit(solution)/shard_map/mix/ppermute | solution.py:430
  62.0 0.5 multiply_sine_fusion
  62.5 0.1 add_convert_fusion.a_ref.x_ref.t_ref
  62.6 10.7 %collective-permute-start.9 = (bf16[128,2048]{1,0:T(8,128)(2,1)S(1)}, bf16[128,2048]{1,0:T(8,128)(2,1)S(1)}, u32[]{:S(2)}, u32[]{:S(2)}) collective-permute-start(bf16[128,2048]{1,0:T(8,128)(2,1)S(1)} %add_convert_fusion.a_ref.x_ref.t_ref), channel_id=1, source_target_pairs={{0,1},{1,0},{2,3},{3,2},{4,5},{5,4},{6,7},{7,6},{8,9},{9,8},{10,11... | collective-permute-start | bytes 1572872 | tf_op jit(solution)/shard_map/mix/ppermute | solution.py:432
  73.4 3.6 %collective-permute-done.8 = bf16[128,2048]{1,0:T(8,128)(2,1)S(1)} collective-permute-done((bf16[128,2048]{1,0:T(8,128)(2,1)S(1)}, bf16[128,2048]{1,0:T(8,128)(2,1)S(1)}, u32[]{:S(2)}, u32[]{:S(2)}) %collective-permute-start.8) | collective-permute-done | bytes 524320 | tf_op jit(solution)/shard_map/mix/ppermute | solution.py:430
  76.9 0.1 add_convert_fusion.1.x_ref.t_ref
  77.1 6.7 %collective-permute-start.10 = (bf16[128,2048]{1,0:T(8,128)(2,1)S(1)}, bf16[128,2048]{1,0:T(8,128)(2,1)S(1)}, u32[]{:S(2)}, u32[]{:S(2)}) collective-permute-start(bf16[128,2048]{1,0:T(8,128)(2,1)S(1)} %add_convert_fusion.1.x_ref.t_ref), channel_id=1, source_target_pairs={{0,1},{1,0},{2,3},{3,2},{4,5},{5,4},{6,7},{7,6},{8,9},{9,8},{10,11... | collective-permute-start | bytes 1572872 | tf_op jit(solution)/shard_map/mix/ppermute | solution.py:434
  83.7 0.1 pad_maximum_fusion
  83.9 8.3 %load_w_qkv.1.w_ref = bf16[3,4096,1024]{2,1,0:T(8,128)(2,1)S(1)} custom-call(bf16[3,4096,1024]{2,1,0:T(8,128)(2,1)} %bitcast.4, bf16[128,2048]{1,0:T(8,128)(2,1)S(1)} %get-tuple-element.33.after), custom_call_target="tpu_custom_call" | custom-call | bytes 25165824 | tf_op jit(solution)/shard_map/load_w_qkv/pallas_call | solution.py:127
  92.2 1.8 %project_a.3.acc_ref = f32[3,128,1024]{2,1,0:T(8,128)S(1)} custom-call(bf16[128,2048]{1,0:T(8,128)(2,1)S(1)} %add_convert_fusion.a_ref.x_ref.t_ref, bf16[3,4096,1024]{2,1,0:T(8,128)(2,1)S(1)} %load_w_qkv.1.w_ref), custom_call_target="tpu_custom_call" | custom-call | flops 1610612736 | bytes 12582912 | tf_op jit(solution)/shard_map/project_a/pallas_call | solution.py:127
  94.1 1.5 %project_a.4 = (bf16[2,128,1024]{2,1,0:T(8,128)(2,1)S(1)}, f32[128,128]{1,0:T(8,128)S(1)}) custom-call(bf16[128,2048]{1,0:T(8,128)(2,1)S(1)} %add_convert_fusion.a_ref.x_ref.t_ref, bf16[128,2048]{1,0:T(8,128)(2,1)S(1)} %collective-permute-done.9.x_ref, bf16[3,4096,1024]{2,1,0:T(8,128)(2,1)S(1)} %load_w_qkv.1.w_ref, f32[3,128,1024]{2,1,0:T(8,128)S(1)} %project_a.3.acc_ref, ...), custom_call_target="tpu_custom_call" | custom-call | flops 1610612736 | bytes 12582912 | tf_op jit(solution)/shard_map/project_a/pallas_call | solution.py:127
  95.5 2.1 %collective-permute-start.12 = (bf16[2,128,1024]{2,1,0:T(8,128)(2,1)S(1)}, bf16[2,128,1024]{2,1,0:T(8,128)(2,1)S(1)}, u32[]{:S(2)}, u32[]{:S(2)}) collective-permute-start(bf16[2,128,1024]{2,1,0:T(8,128)(2,1)S(1)} %get-tuple-element.42.a_ref), channel_id=1, source_target_pairs={{0,4},{4,8},{8,12},{12,16},{16,20},{20,24},{24,28},{1,5},{5,9},{9,... | collective-permute-start | bytes 1572872 | tf_op jit(solution)/shard_map/project_a/ppermute | solution.py:24
  97.6 2.5 %project_b.3 = (f32[3,128,1024]{2,1,0:T(8,128)S(1)}, bf16[256,1024]{1,0:T(8,128)(2,1)}) custom-call(bf16[128,2048]{1,0:T(8,128)(2,1)S(1)} %add_convert_fusion.1.x_ref.t_ref, bf16[3,4096,1024]{2,1,0:T(8,128)(2,1)S(1)} %load_w_qkv.1.w_ref, bf16[128,2048]{1,0:T(8,128)(2,1)S(1)} %add_convert_fusion.a_ref.x_ref.t_ref), custom_call_target="tpu_custom_call" | custom-call | flops 1610612736 | bytes 12582912 | tf_op jit(solution)/shard_map/project_b/pallas_call | solution.py:127
  100.2 1.4 %project_b.4 = (bf16[2,128,1024]{2,1,0:T(8,128)(2,1)S(1)}, f32[128,128]{1,0:T(8,128)S(1)}) custom-call(bf16[128,2048]{1,0:T(8,128)(2,1)S(1)} %add_convert_fusion.1.x_ref.t_ref, bf16[128,2048]{1,0:T(8,128)(2,1)S(1)} %collective-permute-done.10.x_ref, bf16[3,4096,1024]{2,1,0:T(8,128)(2,1)S(1)} %load_w_qkv.1.w_ref, ...), custom_call_target="tpu_custom_call" | custom-call | flops 1610612736 | bytes 12582912 | tf_op jit(solution)/shard_map/project_b/pallas_call | solution.py:127
  101.6 3.3 %collective-permute-start.11 = (bf16[2,128,1024]{2,1,0:T(8,128)(2,1)S(1)}, bf16[2,128,1024]{2,1,0:T(8,128)(2,1)S(1)}, u32[]{:S(2)}, u32[]{:S(2)}) collective-permute-start(bf16[2,128,1024]{2,1,0:T(8,128)(2,1)S(1)} %get-tuple-element.41.b_ref), channel_id=1, source_target_pairs={{0,4},{4,8},{8,12},{12,16},{16,20},{20,24},{24,28},{1,5},{5,9},{9,... | collective-permute-start | bytes 1572872 | tf_op jit(solution)/shard_map/project_b/ppermute | solution.py:24
  105.0 0.8 project_a.5.qa_ref
  105.8 0.8 project_b.5.qb_ref
  106.7 0.3 collective-permute-done.12.pa_ref
  106.9 2.4 %attend.2 = (f32[256,1024]{1,0:T(8,128)S(1)}, f32[8,256,1]{2,1,0:T(8,128)S(1)}, f32[8,256,1]{2,1,0:T(8,128)S(1)}) custom-call(bf16[128,1024]{1,0:T(8,128)(2,1)S(1)} %project_a.5.qa_ref, bf16[128,1024]{1,0:T(8,128)(2,1)S(1)} %project_b.5.qb_ref, bf16[2,128,1024]{2,1,0:T(8,128)(2,1)S(1)} %get-tuple-element.42.a_ref, ...), custom_call_target="tpu_custom_call" | custom-call | flops 402653184 | bytes 3145728 | tf_op jit(solution)/shard_map/attend/pallas_call | solution.py:127
  109.3 3.7 %collective-permute-done.11.pb_ref = bf16[2,128,1024]{2,1,0:T(8,128)(2,1)S(1)} collective-permute-done((bf16[2,128,1024]{2,1,0:T(8,128)(2,1)S(1)}, bf16[2,128,1024]{2,1,0:T(8,128)(2,1)S(1)}, u32[]{:S(2)}, u32[]{:S(2)}) %collective-permute-start.11) | collective-permute-done | bytes 524320 | tf_op jit(solution)/shard_map/project_b/ppermute | solution.py:24
  113.0 3.2 %attend.3 = bf16[256,1024]{1,0:T(8,128)(2,1)} custom-call(bf16[128,1024]{1,0:T(8,128)(2,1)S(1)} %project_a.5.qa_ref, bf16[128,1024]{1,0:T(8,128)(2,1)S(1)} %project_b.5.qb_ref, bf16[2,128,1024]{2,1,0:T(8,128)(2,1)S(1)} %collective-permute-done.11.pb_ref, f32[256,1024]{1,0:T(8,128)S(1)} %get-tuple-element.43.acc_ref, ...), custom_call_target="tpu_custom_call" | custom-call | flops 134217728 | bytes 3145728 | tf_op jit(solution)/shard_map/attend/pallas_call | solution.py:127
  (11 shorter events, 0.1 us)
Async XLA Ops:
  2.3 1.4 %collective-permute-start = (bf16[4,128,128]{2,1,0:T(8,128)(2,1)S(1)}, bf16[4,128,128]{2,1,0:T(8,128)(2,1)S(1)}, u32[]{:S(2)}, u32[]{:S(2)}) collective-permute-start(bf16[4,128,128]{2,1,0:T(8,128)(2,1)S(1)} %get-tuple-element.27), channel_id=1, source_target_pairs={{0,4},{4,0},{8,12},{12,8},{16,20},{20,16},{24,28},{28,24},{1,5},{5... | collective-permute-start | bytes 393224 | tf_op jit(solution)/shard_map/state/ppermute | solution.py:28
  3.7 9.5 %collective-permute-start.1 = (bf16[4,128,128]{2,1,0:T(8,128)(2,1)S(1)}, bf16[4,128,128]{2,1,0:T(8,128)(2,1)S(1)}, u32[]{:S(2)}, u32[]{:S(2)}) collective-permute-start(bf16[4,128,128]{2,1,0:T(8,128)(2,1)S(1)} %add_convert_fusion.5.after), channel_id=1, source_target_pairs={{0,8},{4,12},{8,0},{12,4},{16,24},{20,28},{24,16},{28,20},{1,9},{5... | collective-permute-start | bytes 393224 | tf_op jit(solution)/shard_map/state/ppermute | solution.py:28
  5.3 8.1 %collective-permute-start.2 = (bf16[4,128,128]{2,1,0:T(8,128)(2,1)S(1)}, bf16[4,128,128]{2,1,0:T(8,128)(2,1)S(1)}, u32[]{:S(2)}, u32[]{:S(2)}) collective-permute-start(bf16[4,128,128]{2,1,0:T(8,128)(2,1)S(1)} %add_convert_fusion.5.after), channel_id=1, source_target_pairs={{0,16},{4,20},{8,24},{12,28},{16,0},{20,4},{24,8},{28,12},{1,17},{... | collective-permute-start | bytes 393224 | tf_op jit(solution)/shard_map/state/ppermute | solution.py:28
  5.8 7.6 %collective-permute-start.3 = (bf16[4,128,128]{2,1,0:T(8,128)(2,1)S(1)}, bf16[4,128,128]{2,1,0:T(8,128)(2,1)S(1)}, u32[]{:S(2)}, u32[]{:S(2)}) collective-permute-start(bf16[4,128,128]{2,1,0:T(8,128)(2,1)S(1)} %add_convert_fusion.5.after), channel_id=1, source_target_pairs={{0,24},{4,28},{8,16},{12,20},{16,8},{20,12},{24,0},{28,4},{1,25},{... | collective-permute-start | bytes 393224 | tf_op jit(solution)/shard_map/state/ppermute | solution.py:28
  7.3 1.4 %copy-start.2 = (bf16[256,3,1024]{2,0,1:T(8,128)(2,1)S(1)}, bf16[256,3,1024]{2,0,1:T(8,128)(2,1)}, u32[]{:S(2)}) copy-start(bf16[256,3,1024]{2,0,1:T(8,128)(2,1)} %param.4) | copy-start | bytes 4718596
  13.2 8.2 %copy-start.3 = (bf16[256,1024]{1,0:T(8,128)(2,1)S(1)}, bf16[256,1024]{1,0:T(8,128)(2,1)}, u32[]{:S(2)}) copy-start(bf16[256,1024]{1,0:T(8,128)(2,1)} %r_ref.1) | copy-start | bytes 1572868
  13.5 1.4 %collective-permute-start.4 = (bf16[4,128,128]{2,1,0:T(8,128)(2,1)S(1)}, bf16[4,128,128]{2,1,0:T(8,128)(2,1)S(1)}, u32[]{:S(2)}, u32[]{:S(2)}) collective-permute-start(bf16[4,128,128]{2,1,0:T(8,128)(2,1)S(1)} %get-tuple-element.46), channel_id=1, source_target_pairs={{0,4},{4,0},{8,12},{12,8},{16,20},{20,16},{24,28},{28,24},{1,5},{5... | collective-permute-start | bytes 393224 | tf_op jit(solution)/shard_map/prefix/ppermute | solution.py:28
  16.5 3.3 %copy-start = (bf16[1024,4096]{1,0:T(8,128)(2,1)}, bf16[1024,4096]{1,0:T(8,128)(2,1)S(1)}, u32[]{:S(2)}) copy-start(bf16[1024,4096]{1,0:T(8,128)(2,1)S(1)} %load_w_out.1.w_ref) | copy-start | bytes 25165828
  19.8 14.0 %collective-permute-start.5 = (bf16[128,2048]{1,0:T(8,128)(2,1)S(1)}, bf16[128,2048]{1,0:T(8,128)(2,1)S(1)}, u32[]{:S(2)}, u32[]{:S(2)}) collective-permute-start(bf16[128,2048]{1,0:T(8,128)(2,1)S(1)} %get-tuple-element.31), channel_id=1, source_target_pairs={{0,1},{1,0},{2,3},{3,2},{4,5},{5,4},{6,7},{7,6},{8,9},{9,8},{10,11... | collective-permute-start | bytes 1572872 | tf_op jit(solution)/shard_map/partials/ppermute | solution.py:390
  21.4 3.4 %copy-start.1 = (bf16[1024,4096]{1,0:T(8,128)(2,1)S(1)}, bf16[1024,4096]{1,0:T(8,128)(2,1)}, u32[]{:S(2)}) copy-start(bf16[1024,4096]{1,0:T(8,128)(2,1)} %copy-done) | copy-start | bytes 25165828
  33.8 14.0 %collective-permute-start.6 = (bf16[128,2048]{1,0:T(8,128)(2,1)S(1)}, bf16[128,2048]{1,0:T(8,128)(2,1)S(1)}, u32[]{:S(2)}, u32[]{:S(2)}) collective-permute-start(bf16[128,2048]{1,0:T(8,128)(2,1)S(1)} %get-tuple-element.32), channel_id=1, source_target_pairs={{0,1},{1,0},{2,3},{3,2},{4,5},{5,4},{6,7},{7,6},{8,9},{9,8},{10,11... | collective-permute-start | bytes 1572872 | tf_op jit(solution)/shard_map/mix/ppermute | solution.py:425
  35.5 24.8 %collective-permute-start.7 = (bf16[128,2048]{1,0:T(8,128)(2,1)S(1)}, bf16[128,2048]{1,0:T(8,128)(2,1)S(1)}, u32[]{:S(2)}, u32[]{:S(2)}) collective-permute-start(bf16[128,2048]{1,0:T(8,128)(2,1)S(1)} %add_convert_fusion.2), channel_id=1, source_target_pairs={{0,3},{3,0},{1,2},{2,1},{4,7},{7,4},{5,6},{6,5},{8,11},{11,8},{9,1... | collective-permute-start | bytes 1572872 | tf_op jit(solution)/shard_map/mix/ppermute | solution.py:427
  60.3 16.7 %collective-permute-start.8 = (bf16[128,2048]{1,0:T(8,128)(2,1)S(1)}, bf16[128,2048]{1,0:T(8,128)(2,1)S(1)}, u32[]{:S(2)}, u32[]{:S(2)}) collective-permute-start(bf16[128,2048]{1,0:T(8,128)(2,1)S(1)} %add_convert_fusion.3), channel_id=1, source_target_pairs={{0,3},{3,0},{1,2},{2,1},{4,7},{7,4},{5,6},{6,5},{8,11},{11,8},{9,1... | collective-permute-start | bytes 1572872 | tf_op jit(solution)/shard_map/mix/ppermute | solution.py:430
  62.6 31.4 %collective-permute-start.9 = (bf16[128,2048]{1,0:T(8,128)(2,1)S(1)}, bf16[128,2048]{1,0:T(8,128)(2,1)S(1)}, u32[]{:S(2)}, u32[]{:S(2)}) collective-permute-start(bf16[128,2048]{1,0:T(8,128)(2,1)S(1)} %add_convert_fusion.a_ref.x_ref.t_ref), channel_id=1, source_target_pairs={{0,1},{1,0},{2,3},{3,2},{4,5},{5,4},{6,7},{7,6},{8,9},{9,8},{10,11... | collective-permute-start | bytes 1572872 | tf_op jit(solution)/shard_map/mix/ppermute | solution.py:432
  77.1 23.1 %collective-permute-start.10 = (bf16[128,2048]{1,0:T(8,128)(2,1)S(1)}, bf16[128,2048]{1,0:T(8,128)(2,1)S(1)}, u32[]{:S(2)}, u32[]{:S(2)}) collective-permute-start(bf16[128,2048]{1,0:T(8,128)(2,1)S(1)} %add_convert_fusion.1.x_ref.t_ref), channel_id=1, source_target_pairs={{0,1},{1,0},{2,3},{3,2},{4,5},{5,4},{6,7},{7,6},{8,9},{9,8},{10,11... | collective-permute-start | bytes 1572872 | tf_op jit(solution)/shard_map/mix/ppermute | solution.py:434
  95.5 11.4 %collective-permute-start.12 = (bf16[2,128,1024]{2,1,0:T(8,128)(2,1)S(1)}, bf16[2,128,1024]{2,1,0:T(8,128)(2,1)S(1)}, u32[]{:S(2)}, u32[]{:S(2)}) collective-permute-start(bf16[2,128,1024]{2,1,0:T(8,128)(2,1)S(1)} %get-tuple-element.42.a_ref), channel_id=1, source_target_pairs={{0,4},{4,8},{8,12},{12,16},{16,20},{20,24},{24,28},{1,5},{5,9},{9,... | collective-permute-start | bytes 1572872 | tf_op jit(solution)/shard_map/project_a/ppermute | solution.py:24
  101.6 11.4 %collective-permute-start.11 = (bf16[2,128,1024]{2,1,0:T(8,128)(2,1)S(1)}, bf16[2,128,1024]{2,1,0:T(8,128)(2,1)S(1)}, u32[]{:S(2)}, u32[]{:S(2)}) collective-permute-start(bf16[2,128,1024]{2,1,0:T(8,128)(2,1)S(1)} %get-tuple-element.41.b_ref), channel_id=1, source_target_pairs={{0,4},{4,8},{8,12},{12,16},{16,20},{20,24},{24,28},{1,5},{5,9},{9,... | collective-permute-start | bytes 1572872 | tf_op jit(solution)/shard_map/project_b/ppermute | solution.py:24

commit v4 on v3

--- a/solution.py
+++ b/solution.py
@@ -123,7 +123,7 @@
 ANYWHERE = pl.BlockSpec(memory_space=pl.ANY)
 
 
-def call(body, ins, outs, in_specs=None, scratch=(), vmem=20, flops=0, moved=0):
+def call(body, ins, outs, in_specs=None, scratch=(), vmem=8, flops=0, moved=0):
     return pl.pallas_call(
         body,
         in_specs=in_specs or [ON_CHIP] * len(ins),
@@ -135,17 +135,11 @@
     )(*ins)
 
 
-def load_body(source, after, target, sems):
-    rows = source.shape[-2] // sems.shape[1]
-    copies = []
-    for plane in range(sems.shape[0]):
-        for i in range(sems.shape[1]):
-            piece = (plane, pl.ds(i * rows, rows)) if len(source.shape) == 3 else pl.ds(i * rows, rows)
-            copy = pltpu.make_async_copy(source.at[piece], target.at[piece], sems.at[plane, i])
-            copy.start()
-            copies.append(copy)
+def start_all(pairs, sems):
+    copies = [pltpu.make_async_copy(a, b, sems.at[i]) for i, (a, b) in enumerate(pairs)]
     for copy in copies:
-        copy.wait()
+        copy.start()
+    return copies
 
 
 def in_hbm(array):
@@ -154,14 +148,6 @@
 
 def in_vmem(array):
     return pltpu.with_memory_space_constraint(array, pltpu.VMEM)
-
-
-def loaded(array, after):
-    planes = array.shape[0] if array.ndim == 3 else 1
-    return call(
-        load_body, (in_hbm(array), after), pltpu.VMEM(array.shape, array.dtype),
-        [IN_HBM, ANYWHERE], (pltpu.SemaphoreType.DMA((planes, 4)),), vmem=4, moved=2 * array.size,
-    )
 
 
 def state_body(qkv_ref, send_ref, keep_ref, k_ref, v_ref, sems):
@@ -187,7 +173,17 @@
             out[j] = dot_tn(k_ref[slot, :, head], v_ref[slot, :, head]).astype(BF16)
 
 
-def intra_body(qkv_ref, o_ref, q_ref):
+def intra_body(qkv_ref, after, cos_ref, sin_ref, w_ref, o_ref, q_ref, w_other_ref, w_mine_ref, sems):
+    _, mine, other = quarters()
+    width = w_mine_ref.shape[2]
+    copies = start_all(
+        [
+            (w_ref.at[:, at(which[p] * width, width)], to.at[p])
+            for which, to in ((other, w_other_ref), (mine, w_mine_ref))
+            for p in range(2)
+        ],
+        sems,
+    )
     rows = qkv_ref.shape[1]
     ahead = lax.broadcasted_iota(jnp.int32, (rows, rows), 1) > lax.broadcasted_iota(
         jnp.int32, (rows, rows), 0
@@ -198,6 +194,8 @@
         scores = dot_nt(qkv_ref[0, :, head], qkv_ref[1, :, head])
         inner = jnp.where(ahead, 0.0, scores).astype(BF16)
         o_ref[:, head] = dot(inner, qkv_ref[2, :, head])
+    for copy in copies:
+        copy.wait()
 
 
 def quarters():
@@ -217,29 +215,42 @@
             head = at((group * count + j) * HD, HD)
             total = intra_ref[:, head] + dot(q_ref[:, head], ref[j])
             lin_ref[:, head] = (total * scale).astype(BF16)
-    _, _, other = quarters()
     half, width = a_ref.shape[0], a_ref.shape[1] // 2
     block = width // 2
     for p in range(2):
         for n in range(2):
-            product = dot(lin_ref[...], w_ref[:, at(other[p] * width + n * block, block)]).astype(BF16)
+            product = dot(lin_ref[...], w_ref[p, :, n * block : (n + 1) * block]).astype(BF16)
             to = slice(p * width + n * block, p * width + (n + 1) * block)
             a_ref[:, to] = product[:half]
             b_ref[:, to] = product[half:]
 
 
-def mine_body(lin_ref, w_ref, r_ref, a_ref, b_ref):
+def mine_body(lin_ref, w_ref, r_ref, w_qkv_ref, a_ref, b_ref, w_qkv_to_ref, sems):
     z, mine, _ = quarters()
+    copies = start_all(
+        [
+            (w_qkv_ref.at[j, pl.ds(i, r_ref.shape[1])], w_qkv_to_ref.at[j, pl.ds(i, r_ref.shape[1])])
+            for j in range(3)
+            for i in range(0, w_qkv_ref.shape[1], r_ref.shape[1])
+        ],
+        sems,
+    )
     half, width = a_ref.shape[0], a_ref.shape[1] // 2
     block = width // 2
     for p in range(2):
         for n in range(2):
-            product = dot(lin_ref[...], w_ref[:, at(mine[p] * width + n * block, block)])
+            product = dot(lin_ref[...], w_ref[p, :, n * block : (n + 1) * block])
             own = r_ref[:, n * block : (n + 1) * block].astype(F32)
             product = (product + jnp.where(mine[p] == z, own, 0.0)).astype(BF16)
             to = slice(p * width + n * block, p * width + (n + 1) * block)
             a_ref[:, to] = product[:half]
             b_ref[:, to] = product[half:]
+    for copy in copies:
+        copy.wait()
+
+
+def add_body(a_ref, b_ref, o_ref):
+    o_ref[...] = (a_ref[...].astype(F32) + b_ref[...].astype(F32)).astype(BF16)
 
 
 def two_quarters(x_ref, w_ref, plane, which, to):
@@ -278,19 +289,19 @@
             out_ref[:, n * block + h * HD : n * block + (h + 1) * HD] = turned.astype(BF16)
 
 
-def kv_body(block, t_ref, x_ref, w_ref, acc_ref, cos_ref, sin_ref, kv_ref, inv_ref):
+def kv_body(block, mine, t_ref, x_ref, w_ref, acc_ref, cos_ref, sin_ref, kv_ref, inv_ref):
     t = t_ref[...].astype(F32)
     x = x_ref[...].astype(F32)
     total = jnp.sum(t * t + x * x, axis=1, keepdims=True)
     inv = lax.rsqrt(total / D + 1e-05)
     inv_ref[...] = jnp.broadcast_to(inv, inv_ref.shape)
     for plane in (1, 2):
-        finish(block, plane, x_ref, w_ref, acc_ref, inv, cos_ref[...], sin_ref[...], kv_ref.at[plane - 1])
-
-
-def q_body(block, x_ref, w_ref, acc_ref, inv_ref, cos_ref, sin_ref, q_ref):
+        finish(block, plane, x_ref, w_ref, acc_ref, inv, cos_ref[mine], sin_ref[mine], kv_ref.at[plane - 1])
+
+
+def q_body(block, mine, x_ref, w_ref, acc_ref, inv_ref, cos_ref, sin_ref, q_ref):
     inv = inv_ref[:, :1]
-    finish(block, 0, x_ref, w_ref, acc_ref, inv, cos_ref[...], sin_ref[...], q_ref)
+    finish(block, 0, x_ref, w_ref, acc_ref, inv, cos_ref[mine], sin_ref[mine], q_ref)
 
 
 SCORE = 1.0 / math.sqrt(HD)
@@ -345,6 +356,13 @@
     qkv = jnp.transpose(lin_qkv, (1, 0, 2))
     wqkv = jnp.transpose(w_qkv, (1, 0, 2))
 
+    positions = seq * rows + jnp.arange(rows, dtype=jnp.int32)
+    freq = 500000.0 ** (-(jnp.arange(HD // 2, dtype=F32) * 2.0 / HD))
+    angle = positions.astype(F32)[:, None] * freq[None, :]
+    cosine, sine = jnp.cos(angle), jnp.sin(angle)
+    cos2 = jnp.concatenate([cosine, cosine], axis=1)
+    sin2 = jnp.concatenate([-sine, sine], axis=1)
+
     with jax.named_scope("state"):
         states = shape((group, HD, HD), BF16)
         send, keep = call(
@@ -362,12 +380,13 @@
         by_y = swapped(chip_total, "seq", 4)
         by_xy = swapped(chip_total, "seq", 6)
     with jax.named_scope("intra"):
-        intra, q = call(
-            intra_body, (qkv,), (shape((rows, width), F32), shape((rows, width), BF16)),
-            flops=4 * rows * rows * width, moved=10 * rows * width,
-        )
-    with jax.named_scope("load_w_out"):
-        w_out_here = in_vmem(loaded(w_out, chip_total))
+        columns = pltpu.VMEM((2, width, width), BF16)
+        intra, q, w_other, w_mine = call(
+            intra_body, (qkv, chip_total, cos2, sin2, in_hbm(w_out)),
+            (shape((rows, width), F32), shape((rows, width), BF16), columns, columns),
+            [ON_CHIP, ANYWHERE, ANYWHERE, ANYWHERE, IN_HBM], (pltpu.SemaphoreType.DMA((4,)),),
+            flops=4 * rows * rows * width, moved=2 * width * full,
+        )
     with jax.named_scope("prefix"):
         x_bit = ((seq // 2) % 2).astype(F32)
         y_bit = (seq // 4).astype(F32)
@@ -384,39 +403,33 @@
     halves = shape((half, full // 2), BF16)
     with jax.named_scope("partials"):
         lin_out, send_a, send_b = call(
-            functools.partial(send_body, scale), (q, intra, own_prefix, other_prefix, w_out_here),
+            functools.partial(send_body, scale), (q, intra, own_prefix, other_prefix, in_vmem(w_other)),
             (shape((rows, width), BF16), halves, halves), flops=rows * width * full, moved=width * full,
         )
         got_a = lax.ppermute(send_a, "head", PAIR)
-        mine_a, mine_b = call(
-            mine_body, (lin_out, w_out_here, resid), (halves, halves),
-            flops=rows * width * full, moved=width * full,
-        )
-    with jax.named_scope("load_w_qkv"):
-        w_here = in_vmem(loaded(wqkv, mine_a))
-
-    positions = seq * rows + jnp.arange(rows, dtype=jnp.int32)
-    freq = 500000.0 ** (-(jnp.arange(HD // 2, dtype=F32) * 2.0 / HD))
-    angle = positions.astype(F32)[:, None] * freq[None, :]
-    cosine, sine = jnp.cos(angle), jnp.sin(angle)
-    cos2 = jnp.concatenate([cosine, cosine], axis=1)
-    sin2 = jnp.concatenate([-sine, sine], axis=1)
-
+        mine_a, mine_b, w_here = call(
+            mine_body, (lin_out, in_vmem(w_mine), resid, in_hbm(wqkv)),
+            (halves, halves, pltpu.VMEM(wqkv.shape, BF16)),
+            [ON_CHIP, ON_CHIP, ON_CHIP, IN_HBM], (pltpu.SemaphoreType.DMA((3 * full // width,)),),
+            flops=rows * width * full, moved=6 * width * full,
+        )
+        w_here = in_vmem(w_here)
     accs = shape((3, half, width), F32)
     cost = dict(flops=half * full * 3 * width, moved=3 * width * full)
 
     def add(a, b):
-        return (a.astype(F32) + b.astype(F32)).astype(BF16)
+        return call(add_body, (a, b), halves, vmem=4, moved=6 * half * full)
 
     def project(total, got, acc, index):
-        turn = (cos2[index * half : (index + 1) * half], sin2[index * half : (index + 1) * half])
+        turn = (cos2, sin2)
+        mine = pl.ds(index * half, half)
         kv, inv = call(
-            functools.partial(kv_body, block), (total, got, w_here, acc, *turn),
+            functools.partial(kv_body, block, mine), (total, got, w_here, acc, *turn),
             (shape((2, half, width), BF16), shape((half, HD), F32)), **cost,
         )
         before = shifted(kv, "seq", 1)
         query = call(
-            functools.partial(q_body, block), (got, w_here, acc, inv, *turn), shape((half, width), BF16), **cost,
+            functools.partial(q_body, block, mine), (got, w_here, acc, inv, *turn), shape((half, width), BF16), **cost,
         )
         return kv, before, query
 

time: 116 us -> 109 us (0.940)
  local copies, waits for them, and re-layouts: 8.06 us -> 0.01 us
  waiting for transfers between devices: 40.2 us -> 43 us
  starting transfers between devices: 33.9 us -> 32.5 us
    unnamed x8 -> x4, local copies, waits for them, and re-layouts: 8.06 us -> 0.01 us
    ppermute x1, waiting for transfers between devices: 7.74 us -> 3.54 us  [tuned(): got_a = lax.ppermute(send_a, 'head', PAIR)]
    ppermute x1, waiting for transfers between devices: 0.01 us -> 3.19 us  [tuned(): rest_b = lax.ppermute(total_b, 'head', PAIR)]
    ppermute x2, starting transfers between devices: 5.45 us -> 4.02 us  [shifted(): return lax.ppermute(array, axis, pairs)]
    ppermute x2, waiting for transfers between devices: 3.92 us -> 5.33 us  [shifted(): return lax.ppermute(array, axis, pairs)]
    ppermute x1, waiting for transfers between devices: 0.01 us -> 1.41 us  [tuned(): rest_a = lax.ppermute(total_a, 'head', PAIR)]
    pallas_call x14 -> x16, Pallas kernels: 31.9 us -> 31.6 us  [call(): pl.pallas_call(body, in_specs=in_specs or [ON_CHIP] * len(ins), out_specs...]
  transfers between devices with their start and end apart: 13 -> 13, of which waited for: 9 -> 10; matrix products, arithmetic and copies ran while one was open for 1% -> 1% of each run, Pallas kernels for 22% -> 23%
where the time goes in v4:
time: 109 us
  waiting for transfers between devices  43 us (39%)
  starting transfers between devices  32.5 us (30%)
  Pallas kernels  31.6 us (29%)
    pallas_call x16, Pallas kernels, call(): pl.pallas_call(body, in_specs=in_specs or [ON_CHIP] * len(ins), out_specs...  31.6 us
    ppermute x1, waiting for transfers between devices, tuned(): far_a = lax.ppermute(sum_a, 'head', CROSS)  12.4 us
    ppermute x1, starting transfers between devices, tuned(): rest_a = lax.ppermute(total_a, 'head', PAIR)  10.7 us
    ppermute x1, waiting for transfers between devices, tuned(): got_b = lax.ppermute(send_b, 'head', PAIR)  9.72 us
    ppermute x1, starting transfers between devices, tuned(): rest_b = lax.ppermute(total_b, 'head', PAIR)  6.64 us
    ppermute x2, waiting for transfers between devices, shifted(): return lax.ppermute(array, axis, pairs)  5.33 us
    ppermute x1, waiting for transfers between devices, tuned(): far_b = lax.ppermute(sum_b, 'head', CROSS)  4.17 us
    ppermute x2, starting transfers between devices, shifted(): return lax.ppermute(array, axis, pairs)  4.02 us
  transfers between devices with their start and end apart: 13, of which 10 were waited for; matrix products, arithmetic and copies ran while one was open for 1% of the time, Pallas kernels for 23%

profile of v4, /device:TPU:4, one launch (start us, length us, event | category | flops | bytes accessed | tf_op | source)
XLA Modules:
  0.0 108.9 jit_solution(11175888928314842751)
XLA Ops:
  0.6 1.7 %state.1 = (bf16[4,128,128]{2,1,0:T(8,128)(2,1)S(1)}, bf16[4,128,128]{2,1,0:T(8,128)(2,1)S(1)}) custom-call(bf16[3,256,1024]{2,1,0:T(8,128)(2,1)} %bitcast.2), custom_call_target="tpu_custom_call" | custom-call | flops 67108864 | bytes 1048576 | tf_op jit(solution)/shard_map/state/pallas_call | solution.py:127
  2.4 0.1 collective-permute-start
  2.6 0.5 fusion.1
  3.1 0.7 collective-permute-done
  3.8 1.5 %collective-permute-start.3 = (bf16[4,128,128]{2,1,0:T(8,128)(2,1)S(1)}, bf16[4,128,128]{2,1,0:T(8,128)(2,1)S(1)}, u32[]{:S(2)}, u32[]{:S(2)}) collective-permute-start(bf16[4,128,128]{2,1,0:T(8,128)(2,1)S(1)} %add_convert_fusion.1.after), channel_id=1, source_target_pairs={{0,24},{4,28},{8,16},{12,20},{16,8},{20,12},{24,0},{28,4},{1,25},{... | collective-permute-start | bytes 393224 | tf_op jit(solution)/shard_map/state/ppermute | solution.py:28
  5.3 1.5 %collective-permute-start.2 = (bf16[4,128,128]{2,1,0:T(8,128)(2,1)S(1)}, bf16[4,128,128]{2,1,0:T(8,128)(2,1)S(1)}, u32[]{:S(2)}, u32[]{:S(2)}) collective-permute-start(bf16[4,128,128]{2,1,0:T(8,128)(2,1)S(1)} %add_convert_fusion.1.after), channel_id=1, source_target_pairs={{0,16},{4,20},{8,24},{12,28},{16,0},{20,4},{24,8},{28,12},{1,17},{... | collective-permute-start | bytes 393224 | tf_op jit(solution)/shard_map/state/ppermute | solution.py:28
  6.9 0.5 collective-permute-start.1
  7.4 0.1 pad_maximum_fusion
  7.5 0.0 copy-done
  7.5 4.4 %intra.1 = (f32[256,1024]{1,0:T(8,128)S(1)}, bf16[256,1024]{1,0:T(8,128)(2,1)S(1)}, bf16[2,1024,1024]{2,1,0:T(8,128)(2,1)S(1)}, bf16[2,1024,1024]{2,1,0:T(8,128)(2,1)S(1)}) custom-call(bf16[3,256,1024]{2,1,0:T(8,128)(2,1)S(1)} %bitcast.3, bf16[4,128,128]{2,1,0:T(8,128)(2,1)S(1)} %add_convert_fusion.1.after, f32[256,128]{1,0:T(8,128)S(1)} %get-tuple-element.58.cos_ref, ...), custom_call_target="tpu_custom_call" | custom-call | flops 268435456 | bytes 8388608 | tf_op jit(solution)/shard_map/intra/pallas_call | solution.py:127
  12.0 0.0 copy-start.1
  12.0 0.0 collective-permute-done.3
  12.0 1.2 %collective-permute-done.2 = bf16[4,128,128]{2,1,0:T(8,128)(2,1)S(1)} collective-permute-done((bf16[4,128,128]{2,1,0:T(8,128)(2,1)S(1)}, bf16[4,128,128]{2,1,0:T(8,128)(2,1)S(1)}, u32[]{:S(2)}, u32[]{:S(2)}) %collective-permute-start.2) | collective-permute-done | bytes 131104 | tf_op jit(solution)/shard_map/state/ppermute | solution.py:28
  13.2 0.0 collective-permute-done.1
  13.2 0.1 broadcast_select_fusion
  13.3 0.1 collective-permute-start.4
  13.4 1.3 %collective-permute-done.4.other_ref = bf16[4,128,128]{2,1,0:T(8,128)(2,1)S(1)} collective-permute-done((bf16[4,128,128]{2,1,0:T(8,128)(2,1)S(1)}, bf16[4,128,128]{2,1,0:T(8,128)(2,1)S(1)}, u32[]{:S(2)}, u32[]{:S(2)}) %collective-permute-start.4) | collective-permute-done | bytes 131104 | tf_op jit(solution)/shard_map/prefix/ppermute | solution.py:28
  14.7 1.6 %partials.2 = (bf16[256,1024]{1,0:T(8,128)(2,1)S(1)}, bf16[128,2048]{1,0:T(8,128)(2,1)S(1)}, bf16[128,2048]{1,0:T(8,128)(2,1)S(1)}) custom-call(bf16[256,1024]{1,0:T(8,128)(2,1)S(1)} %get-tuple-element.29.q_ref, f32[256,1024]{1,0:T(8,128)S(1)} %get-tuple-element.30.intra_ref, bf16[4,128,128]{2,1,0:T(8,128)(2,1)S(1)} %broadcast_select_fusion.1.own_ref, ...), custom_call_target="tpu_custom_call" | custom-call | flops 1073741824 | bytes 4194304 | tf_op jit(solution)/shard_map/partials/pallas_call | solution.py:127
  16.3 1.6 %collective-permute-start.5 = (bf16[128,2048]{1,0:T(8,128)(2,1)S(1)}, bf16[128,2048]{1,0:T(8,128)(2,1)S(1)}, u32[]{:S(2)}, u32[]{:S(2)}) collective-permute-start(bf16[128,2048]{1,0:T(8,128)(2,1)S(1)} %get-tuple-element.36), channel_id=1, source_target_pairs={{0,1},{1,0},{2,3},{3,2},{4,5},{5,4},{6,7},{7,6},{8,9},{9,8},{10,11... | collective-permute-start | bytes 1572872 | tf_op jit(solution)/shard_map/partials/ppermute | solution.py:409
  17.9 0.0 copy-done.1
  17.9 8.9 %partials.3 = (bf16[128,2048]{1,0:T(8,128)(2,1)S(1)}, bf16[128,2048]{1,0:T(8,128)(2,1)S(1)}, bf16[3,4096,1024]{2,1,0:T(8,128)(2,1)S(1)}) custom-call(bf16[256,1024]{1,0:T(8,128)(2,1)S(1)} %get-tuple-element.32.lin_ref, bf16[2,1024,1024]{2,1,0:T(8,128)(2,1)S(1)} %get-tuple-element.33.w_ref, bf16[256,1024]{1,0:T(8,128)(2,1)S(1)} %copy-done.1, ...), custom_call_target="tpu_custom_call" | custom-call | flops 1073741824 | bytes 25165824 | tf_op jit(solution)/shard_map/partials/pallas_call | solution.py:127
  26.8 3.5 %collective-permute-done.5.b_ref = bf16[128,2048]{1,0:T(8,128)(2,1)S(1)} collective-permute-done((bf16[128,2048]{1,0:T(8,128)(2,1)S(1)}, bf16[128,2048]{1,0:T(8,128)(2,1)S(1)}, u32[]{:S(2)}, u32[]{:S(2)}) %collective-permute-start.5) | collective-permute-done | bytes 524320 | tf_op jit(solution)/shard_map/partials/ppermute | solution.py:409
  30.3 1.6 %collective-permute-start.6 = (bf16[128,2048]{1,0:T(8,128)(2,1)S(1)}, bf16[128,2048]{1,0:T(8,128)(2,1)S(1)}, u32[]{:S(2)}, u32[]{:S(2)}) collective-permute-start(bf16[128,2048]{1,0:T(8,128)(2,1)S(1)} %get-tuple-element.37), channel_id=1, source_target_pairs={{0,1},{1,0},{2,3},{3,2},{4,5},{5,4},{6,7},{7,6},{8,9},{9,8},{10,11... | collective-permute-start | bytes 1572872 | tf_op jit(solution)/shard_map/mix/ppermute | solution.py:438
  31.9 0.1 mix.5.a_ref
  32.0 2.5 %collective-permute-start.7 = (bf16[128,2048]{1,0:T(8,128)(2,1)S(1)}, bf16[128,2048]{1,0:T(8,128)(2,1)S(1)}, u32[]{:S(2)}, u32[]{:S(2)}) collective-permute-start(bf16[128,2048]{1,0:T(8,128)(2,1)S(1)} %mix.5.a_ref), channel_id=1, source_target_pairs={{0,3},{3,0},{1,2},{2,1},{4,7},{7,4},{5,6},{6,5},{8,11},{11,8},{9,1... | collective-permute-start | bytes 1572872 | tf_op jit(solution)/shard_map/mix/ppermute | solution.py:440
  34.6 9.7 %collective-permute-done.6.b_ref = bf16[128,2048]{1,0:T(8,128)(2,1)S(1)} collective-permute-done((bf16[128,2048]{1,0:T(8,128)(2,1)S(1)}, bf16[128,2048]{1,0:T(8,128)(2,1)S(1)}, u32[]{:S(2)}, u32[]{:S(2)}) %collective-permute-start.6) | collective-permute-done | bytes 524320 | tf_op jit(solution)/shard_map/mix/ppermute | solution.py:438
  44.3 0.1 mix.4.a_ref
  44.4 12.4 %collective-permute-done.7.b_ref = bf16[128,2048]{1,0:T(8,128)(2,1)S(1)} collective-permute-done((bf16[128,2048]{1,0:T(8,128)(2,1)S(1)}, bf16[128,2048]{1,0:T(8,128)(2,1)S(1)}, u32[]{:S(2)}, u32[]{:S(2)}) %collective-permute-start.7) | collective-permute-done | bytes 524320 | tf_op jit(solution)/shard_map/mix/ppermute | solution.py:440
  56.9 1.7 %collective-permute-start.8 = (bf16[128,2048]{1,0:T(8,128)(2,1)S(1)}, bf16[128,2048]{1,0:T(8,128)(2,1)S(1)}, u32[]{:S(2)}, u32[]{:S(2)}) collective-permute-start(bf16[128,2048]{1,0:T(8,128)(2,1)S(1)} %mix.4.a_ref), channel_id=1, source_target_pairs={{0,3},{3,0},{1,2},{2,1},{4,7},{7,4},{5,6},{6,5},{8,11},{11,8},{9,1... | collective-permute-start | bytes 1572872 | tf_op jit(solution)/shard_map/mix/ppermute | solution.py:443
  58.5 0.1 mix.7.a_ref.x_ref.t_ref
  58.7 10.7 %collective-permute-start.9 = (bf16[128,2048]{1,0:T(8,128)(2,1)S(1)}, bf16[128,2048]{1,0:T(8,128)(2,1)S(1)}, u32[]{:S(2)}, u32[]{:S(2)}) collective-permute-start(bf16[128,2048]{1,0:T(8,128)(2,1)S(1)} %mix.7.a_ref.x_ref.t_ref), channel_id=1, source_target_pairs={{0,1},{1,0},{2,3},{3,2},{4,5},{5,4},{6,7},{7,6},{8,9},{9,8},{10,11... | collective-permute-start | bytes 1572872 | tf_op jit(solution)/shard_map/mix/ppermute | solution.py:445
  69.4 4.2 %collective-permute-done.8.b_ref = bf16[128,2048]{1,0:T(8,128)(2,1)S(1)} collective-permute-done((bf16[128,2048]{1,0:T(8,128)(2,1)S(1)}, bf16[128,2048]{1,0:T(8,128)(2,1)S(1)}, u32[]{:S(2)}, u32[]{:S(2)}) %collective-permute-start.8) | collective-permute-done | bytes 524320 | tf_op jit(solution)/shard_map/mix/ppermute | solution.py:443
  73.5 0.1 mix.6.x_ref.t_ref
  73.7 6.6 %collective-permute-start.10 = (bf16[128,2048]{1,0:T(8,128)(2,1)S(1)}, bf16[128,2048]{1,0:T(8,128)(2,1)S(1)}, u32[]{:S(2)}, u32[]{:S(2)}) collective-permute-start(bf16[128,2048]{1,0:T(8,128)(2,1)S(1)} %mix.6.x_ref.t_ref), channel_id=1, source_target_pairs={{0,1},{1,0},{2,3},{3,2},{4,5},{5,4},{6,7},{7,6},{8,9},{9,8},{10,11... | collective-permute-start | bytes 1572872 | tf_op jit(solution)/shard_map/mix/ppermute | solution.py:447
  80.3 1.8 %project_a.3.acc_ref = f32[3,128,1024]{2,1,0:T(8,128)S(1)} custom-call(bf16[128,2048]{1,0:T(8,128)(2,1)S(1)} %mix.7.a_ref.x_ref.t_ref, bf16[3,4096,1024]{2,1,0:T(8,128)(2,1)S(1)} %get-tuple-element.41.w_ref), custom_call_target="tpu_custom_call" | custom-call | flops 1610612736 | bytes 12582912 | tf_op jit(solution)/shard_map/project_a/pallas_call | solution.py:127
  82.1 1.4 %collective-permute-done.9.x_ref = bf16[128,2048]{1,0:T(8,128)(2,1)S(1)} collective-permute-done((bf16[128,2048]{1,0:T(8,128)(2,1)S(1)}, bf16[128,2048]{1,0:T(8,128)(2,1)S(1)}, u32[]{:S(2)}, u32[]{:S(2)}) %collective-permute-start.9) | collective-permute-done | bytes 524320 | tf_op jit(solution)/shard_map/mix/ppermute | solution.py:445
  83.5 1.4 %project_a.4 = (bf16[2,128,1024]{2,1,0:T(8,128)(2,1)S(1)}, f32[128,128]{1,0:T(8,128)S(1)}) custom-call(bf16[128,2048]{1,0:T(8,128)(2,1)S(1)} %mix.7.a_ref.x_ref.t_ref, bf16[128,2048]{1,0:T(8,128)(2,1)S(1)} %collective-permute-done.9.x_ref, bf16[3,4096,1024]{2,1,0:T(8,128)(2,1)S(1)} %get-tuple-element.41.w_ref, f32[3,128,1024]{2,1,0:T(8,128)S(1)} %project_a.3.acc_ref, ...), custom_call_target="tpu_custom_call" | custom-call | flops 1610612736 | bytes 12582912 | tf_op jit(solution)/shard_map/project_a/pallas_call | solution.py:127
  85.0 2.1 %collective-permute-start.12 = (bf16[2,128,1024]{2,1,0:T(8,128)(2,1)S(1)}, bf16[2,128,1024]{2,1,0:T(8,128)(2,1)S(1)}, u32[]{:S(2)}, u32[]{:S(2)}) collective-permute-start(bf16[2,128,1024]{2,1,0:T(8,128)(2,1)S(1)} %get-tuple-element.48.a_ref), channel_id=1, source_target_pairs={{0,4},{4,8},{8,12},{12,16},{16,20},{20,24},{24,28},{1,5},{5,9},{9,... | collective-permute-start | bytes 1572872 | tf_op jit(solution)/shard_map/project_a/ppermute | solution.py:24
  87.1 2.5 %project_b.3 = (f32[3,128,1024]{2,1,0:T(8,128)S(1)}, bf16[256,1024]{1,0:T(8,128)(2,1)}) custom-call(bf16[128,2048]{1,0:T(8,128)(2,1)S(1)} %mix.6.x_ref.t_ref, bf16[3,4096,1024]{2,1,0:T(8,128)(2,1)S(1)} %get-tuple-element.41.w_ref, bf16[128,2048]{1,0:T(8,128)(2,1)S(1)} %mix.7.a_ref.x_ref.t_ref), custom_call_target="tpu_custom_call" | custom-call | flops 1610612736 | bytes 12582912 | tf_op jit(solution)/shard_map/project_b/pallas_call | solution.py:127
  89.6 3.2 %collective-permute-done.10.x_ref = bf16[128,2048]{1,0:T(8,128)(2,1)S(1)} collective-permute-done((bf16[128,2048]{1,0:T(8,128)(2,1)S(1)}, bf16[128,2048]{1,0:T(8,128)(2,1)S(1)}, u32[]{:S(2)}, u32[]{:S(2)}) %collective-permute-start.10) | collective-permute-done | bytes 524320 | tf_op jit(solution)/shard_map/mix/ppermute | solution.py:447
  92.8 1.4 %project_b.4 = (bf16[2,128,1024]{2,1,0:T(8,128)(2,1)S(1)}, f32[128,128]{1,0:T(8,128)S(1)}) custom-call(bf16[128,2048]{1,0:T(8,128)(2,1)S(1)} %mix.6.x_ref.t_ref, bf16[128,2048]{1,0:T(8,128)(2,1)S(1)} %collective-permute-done.10.x_ref, bf16[3,4096,1024]{2,1,0:T(8,128)(2,1)S(1)} %get-tuple-element.41.w_ref, f32[3,128,1024]{2,1,0:T(8,128)S(1)} %get-tuple-element.45.acc_ref, ...), custom_call_target="tpu_custom_call" | custom-call | flops 1610612736 | bytes 12582912 | tf_op jit(solution)/shard_map/project_b/pallas_call | solution.py:127
  94.2 1.9 %collective-permute-start.11 = (bf16[2,128,1024]{2,1,0:T(8,128)(2,1)S(1)}, bf16[2,128,1024]{2,1,0:T(8,128)(2,1)S(1)}, u32[]{:S(2)}, u32[]{:S(2)}) collective-permute-start(bf16[2,128,1024]{2,1,0:T(8,128)(2,1)S(1)} %get-tuple-element.47.b_ref), channel_id=1, source_target_pairs={{0,4},{4,8},{8,12},{12,16},{16,20},{20,24},{24,28},{1,5},{5,9},{9,... | collective-permute-start | bytes 1572872 | tf_op jit(solution)/shard_map/project_b/ppermute | solution.py:24
  96.1 0.9 project_a.5.qa_ref
  97.0 0.8 project_b.5.qb_ref
  97.9 0.0 collective-permute-done.12.pa_ref
  97.9 2.4 %attend.2 = (f32[256,1024]{1,0:T(8,128)S(1)}, f32[8,256,1]{2,1,0:T(8,128)S(1)}, f32[8,256,1]{2,1,0:T(8,128)S(1)}) custom-call(bf16[128,1024]{1,0:T(8,128)(2,1)S(1)} %project_a.5.qa_ref, bf16[128,1024]{1,0:T(8,128)(2,1)S(1)} %project_b.5.qb_ref, bf16[2,128,1024]{2,1,0:T(8,128)(2,1)S(1)} %get-tuple-element.48.a_ref, ...), custom_call_target="tpu_custom_call" | custom-call | flops 402653184 | bytes 3145728 | tf_op jit(solution)/shard_map/attend/pallas_call | solution.py:127
  100.3 5.3 %collective-permute-done.11.pb_ref = bf16[2,128,1024]{2,1,0:T(8,128)(2,1)S(1)} collective-permute-done((bf16[2,128,1024]{2,1,0:T(8,128)(2,1)S(1)}, bf16[2,128,1024]{2,1,0:T(8,128)(2,1)S(1)}, u32[]{:S(2)}, u32[]{:S(2)}) %collective-permute-start.11) | collective-permute-done | bytes 524320 | tf_op jit(solution)/shard_map/project_b/ppermute | solution.py:24
  105.6 3.2 %attend.3 = bf16[256,1024]{1,0:T(8,128)(2,1)} custom-call(bf16[128,1024]{1,0:T(8,128)(2,1)S(1)} %project_a.5.qa_ref, bf16[128,1024]{1,0:T(8,128)(2,1)S(1)} %project_b.5.qb_ref, bf16[2,128,1024]{2,1,0:T(8,128)(2,1)S(1)} %collective-permute-done.11.pb_ref, f32[256,1024]{1,0:T(8,128)S(1)} %get-tuple-element.49.acc_ref, ...), custom_call_target="tpu_custom_call" | custom-call | flops 134217728 | bytes 3145728 | tf_op jit(solution)/shard_map/attend/pallas_call | solution.py:127
  (5 shorter events, 0.1 us)
Async XLA Ops:
  0.6 6.9 %copy-start = (bf16[256,3,1024]{2,0,1:T(8,128)(2,1)S(1)}, bf16[256,3,1024]{2,0,1:T(8,128)(2,1)}, u32[]{:S(2)}) copy-start(bf16[256,3,1024]{2,0,1:T(8,128)(2,1)} %param.4) | copy-start | bytes 4718596
  2.4 1.4 %collective-permute-start = (bf16[4,128,128]{2,1,0:T(8,128)(2,1)S(1)}, bf16[4,128,128]{2,1,0:T(8,128)(2,1)S(1)}, u32[]{:S(2)}, u32[]{:S(2)}) collective-permute-start(bf16[4,128,128]{2,1,0:T(8,128)(2,1)S(1)} %get-tuple-element.28), channel_id=1, source_target_pairs={{0,4},{4,0},{8,12},{12,8},{16,20},{20,16},{24,28},{28,24},{1,5},{5... | collective-permute-start | bytes 393224 | tf_op jit(solution)/shard_map/state/ppermute | solution.py:28
  3.8 8.1 %collective-permute-start.3 = (bf16[4,128,128]{2,1,0:T(8,128)(2,1)S(1)}, bf16[4,128,128]{2,1,0:T(8,128)(2,1)S(1)}, u32[]{:S(2)}, u32[]{:S(2)}) collective-permute-start(bf16[4,128,128]{2,1,0:T(8,128)(2,1)S(1)} %add_convert_fusion.1.after), channel_id=1, source_target_pairs={{0,24},{4,28},{8,16},{12,20},{16,8},{20,12},{24,0},{28,4},{1,25},{... | collective-permute-start | bytes 393224 | tf_op jit(solution)/shard_map/state/ppermute | solution.py:28
  5.3 7.8 %collective-permute-start.2 = (bf16[4,128,128]{2,1,0:T(8,128)(2,1)S(1)}, bf16[4,128,128]{2,1,0:T(8,128)(2,1)S(1)}, u32[]{:S(2)}, u32[]{:S(2)}) collective-permute-start(bf16[4,128,128]{2,1,0:T(8,128)(2,1)S(1)} %add_convert_fusion.1.after), channel_id=1, source_target_pairs={{0,16},{4,20},{8,24},{12,28},{16,0},{20,4},{24,8},{28,12},{1,17},{... | collective-permute-start | bytes 393224 | tf_op jit(solution)/shard_map/state/ppermute | solution.py:28
  6.9 6.3 %collective-permute-start.1 = (bf16[4,128,128]{2,1,0:T(8,128)(2,1)S(1)}, bf16[4,128,128]{2,1,0:T(8,128)(2,1)S(1)}, u32[]{:S(2)}, u32[]{:S(2)}) collective-permute-start(bf16[4,128,128]{2,1,0:T(8,128)(2,1)S(1)} %add_convert_fusion.1.after), channel_id=1, source_target_pairs={{0,8},{4,12},{8,0},{12,4},{16,24},{20,28},{24,16},{28,20},{1,9},{5... | collective-permute-start | bytes 393224 | tf_op jit(solution)/shard_map/state/ppermute | solution.py:28
  12.0 6.0 %copy-start.1 = (bf16[256,1024]{1,0:T(8,128)(2,1)S(1)}, bf16[256,1024]{1,0:T(8,128)(2,1)}, u32[]{:S(2)}) copy-start(bf16[256,1024]{1,0:T(8,128)(2,1)} %r_ref.1) | copy-start | bytes 1572868
  13.3 1.4 %collective-permute-start.4 = (bf16[4,128,128]{2,1,0:T(8,128)(2,1)S(1)}, bf16[4,128,128]{2,1,0:T(8,128)(2,1)S(1)}, u32[]{:S(2)}, u32[]{:S(2)}) collective-permute-start(bf16[4,128,128]{2,1,0:T(8,128)(2,1)S(1)} %get-tuple-element.52), channel_id=1, source_target_pairs={{0,4},{4,0},{8,12},{12,8},{16,20},{20,16},{24,28},{28,24},{1,5},{5... | collective-permute-start | bytes 393224 | tf_op jit(solution)/shard_map/prefix/ppermute | solution.py:28
  16.3 14.0 %collective-permute-start.5 = (bf16[128,2048]{1,0:T(8,128)(2,1)S(1)}, bf16[128,2048]{1,0:T(8,128)(2,1)S(1)}, u32[]{:S(2)}, u32[]{:S(2)}) collective-permute-start(bf16[128,2048]{1,0:T(8,128)(2,1)S(1)} %get-tuple-element.36), channel_id=1, source_target_pairs={{0,1},{1,0},{2,3},{3,2},{4,5},{5,4},{6,7},{7,6},{8,9},{9,8},{10,11... | collective-permute-start | bytes 1572872 | tf_op jit(solution)/shard_map/partials/ppermute | solution.py:409
  30.3 14.0 %collective-permute-start.6 = (bf16[128,2048]{1,0:T(8,128)(2,1)S(1)}, bf16[128,2048]{1,0:T(8,128)(2,1)S(1)}, u32[]{:S(2)}, u32[]{:S(2)}) collective-permute-start(bf16[128,2048]{1,0:T(8,128)(2,1)S(1)} %get-tuple-element.37), channel_id=1, source_target_pairs={{0,1},{1,0},{2,3},{3,2},{4,5},{5,4},{6,7},{7,6},{8,9},{9,8},{10,11... | collective-permute-start | bytes 1572872 | tf_op jit(solution)/shard_map/mix/ppermute | solution.py:438
  32.0 24.8 %collective-permute-start.7 = (bf16[128,2048]{1,0:T(8,128)(2,1)S(1)}, bf16[128,2048]{1,0:T(8,128)(2,1)S(1)}, u32[]{:S(2)}, u32[]{:S(2)}) collective-permute-start(bf16[128,2048]{1,0:T(8,128)(2,1)S(1)} %mix.5.a_ref), channel_id=1, source_target_pairs={{0,3},{3,0},{1,2},{2,1},{4,7},{7,4},{5,6},{6,5},{8,11},{11,8},{9,1... | collective-permute-start | bytes 1572872 | tf_op jit(solution)/shard_map/mix/ppermute | solution.py:440
  56.9 16.7 %collective-permute-start.8 = (bf16[128,2048]{1,0:T(8,128)(2,1)S(1)}, bf16[128,2048]{1,0:T(8,128)(2,1)S(1)}, u32[]{:S(2)}, u32[]{:S(2)}) collective-permute-start(bf16[128,2048]{1,0:T(8,128)(2,1)S(1)} %mix.4.a_ref), channel_id=1, source_target_pairs={{0,3},{3,0},{1,2},{2,1},{4,7},{7,4},{5,6},{6,5},{8,11},{11,8},{9,1... | collective-permute-start | bytes 1572872 | tf_op jit(solution)/shard_map/mix/ppermute | solution.py:443
  58.7 24.9 %collective-permute-start.9 = (bf16[128,2048]{1,0:T(8,128)(2,1)S(1)}, bf16[128,2048]{1,0:T(8,128)(2,1)S(1)}, u32[]{:S(2)}, u32[]{:S(2)}) collective-permute-start(bf16[128,2048]{1,0:T(8,128)(2,1)S(1)} %mix.7.a_ref.x_ref.t_ref), channel_id=1, source_target_pairs={{0,1},{1,0},{2,3},{3,2},{4,5},{5,4},{6,7},{7,6},{8,9},{9,8},{10,11... | collective-permute-start | bytes 1572872 | tf_op jit(solution)/shard_map/mix/ppermute | solution.py:445
  73.7 19.1 %collective-permute-start.10 = (bf16[128,2048]{1,0:T(8,128)(2,1)S(1)}, bf16[128,2048]{1,0:T(8,128)(2,1)S(1)}, u32[]{:S(2)}, u32[]{:S(2)}) collective-permute-start(bf16[128,2048]{1,0:T(8,128)(2,1)S(1)} %mix.6.x_ref.t_ref), channel_id=1, source_target_pairs={{0,1},{1,0},{2,3},{3,2},{4,5},{5,4},{6,7},{7,6},{8,9},{9,8},{10,11... | collective-permute-start | bytes 1572872 | tf_op jit(solution)/shard_map/mix/ppermute | solution.py:447
  85.0 12.9 %collective-permute-start.12 = (bf16[2,128,1024]{2,1,0:T(8,128)(2,1)S(1)}, bf16[2,128,1024]{2,1,0:T(8,128)(2,1)S(1)}, u32[]{:S(2)}, u32[]{:S(2)}) collective-permute-start(bf16[2,128,1024]{2,1,0:T(8,128)(2,1)S(1)} %get-tuple-element.48.a_ref), channel_id=1, source_target_pairs={{0,4},{4,8},{8,12},{12,16},{16,20},{20,24},{24,28},{1,5},{5,9},{9,... | collective-permute-start | bytes 1572872 | tf_op jit(solution)/shard_map/project_a/ppermute | solution.py:24
  94.2 11.4 %collective-permute-start.11 = (bf16[2,128,1024]{2,1,0:T(8,128)(2,1)S(1)}, bf16[2,128,1024]{2,1,0:T(8,128)(2,1)S(1)}, u32[]{:S(2)}, u32[]{:S(2)}) collective-permute-start(bf16[2,128,1024]{2,1,0:T(8,128)(2,1)S(1)} %get-tuple-element.47.b_ref), channel_id=1, source_target_pairs={{0,4},{4,8},{8,12},{12,16},{16,20},{20,24},{24,28},{1,5},{5,9},{9,... | collective-permute-start | bytes 1572872 | tf_op jit(solution)/shard_map/project_b/ppermute | solution.py:24

commit v5 on v4

--- a/solution.py
+++ b/solution.py
@@ -13,6 +13,7 @@
 BF16 = jnp.bfloat16
 F32 = jnp.float32
 NEG = -1e30
+STREAMS = (1, 1)
 
 PAIR = [(0, 1), (1, 0), (2, 3), (3, 2)]
 CROSS = [(0, 3), (3, 0), (1, 2), (2, 1)]
@@ -207,44 +208,61 @@
     return z, mine, other
 
 
-def send_body(scale, q_ref, intra_ref, own_ref, other_ref, w_ref, lin_ref, a_ref, b_ref):
+def lin_out_rows(scale, rows, q_ref, intra_ref, own_ref, other_ref, lin_ref):
     core = lax.axis_index("seq") % 2
     count = own_ref.shape[0]
     for ref, group in ((own_ref, core), (other_ref, 1 - core)):
         for j in range(count):
             head = at((group * count + j) * HD, HD)
-            total = intra_ref[:, head] + dot(q_ref[:, head], ref[j])
-            lin_ref[:, head] = (total * scale).astype(BF16)
-    half, width = a_ref.shape[0], a_ref.shape[1] // 2
+            total = intra_ref[rows, head] + dot(q_ref[rows, head], ref[j])
+            lin_ref[rows, head] = (total * scale).astype(BF16)
+
+
+def send_body(scale, cuts, q_ref, intra_ref, own_ref, other_ref, w_ref, send_ref, lin_ref):
+    rows = slice(*cuts[0])
+    lin_out_rows(scale, rows, q_ref, intra_ref, own_ref, other_ref, lin_ref)
+    width = w_ref.shape[2]
     block = width // 2
     for p in range(2):
         for n in range(2):
-            product = dot(lin_ref[...], w_ref[p, :, n * block : (n + 1) * block]).astype(BF16)
             to = slice(p * width + n * block, p * width + (n + 1) * block)
-            a_ref[:, to] = product[:half]
-            b_ref[:, to] = product[half:]
-
-
-def mine_body(lin_ref, w_ref, r_ref, w_qkv_ref, a_ref, b_ref, w_qkv_to_ref, sems):
+            send_ref[:, to] = dot(lin_ref[rows], w_ref[p, :, n * block : (n + 1) * block]).astype(BF16)
+
+
+def mine_body(scale, cuts, *refs):
+    q_ref, intra_ref, own_ref, other_ref, w_other_ref, w_mine_ref, r_ref, w_qkv_ref = refs[:8]
+    count = len(cuts)
+    send_refs, mine_refs = refs[8 : 7 + count], refs[7 + count : 7 + 2 * count]
+    w_qkv_to_ref, lin_ref, sems = refs[7 + 2 * count :]
     z, mine, _ = quarters()
+    width = w_mine_ref.shape[2]
+    block = width // 2
     copies = start_all(
         [
-            (w_qkv_ref.at[j, pl.ds(i, r_ref.shape[1])], w_qkv_to_ref.at[j, pl.ds(i, r_ref.shape[1])])
+            (w_qkv_ref.at[j, pl.ds(i, width)], w_qkv_to_ref.at[j, pl.ds(i, width)])
             for j in range(3)
-            for i in range(0, w_qkv_ref.shape[1], r_ref.shape[1])
+            for i in range(0, w_qkv_ref.shape[1], width)
         ],
         sems,
     )
-    half, width = a_ref.shape[0], a_ref.shape[1] // 2
-    block = width // 2
+    lin_out_rows(scale, slice(None), q_ref, intra_ref, own_ref, other_ref, lin_ref)
+    skip = cuts[0][1]
     for p in range(2):
         for n in range(2):
-            product = dot(lin_ref[...], w_ref[p, :, n * block : (n + 1) * block])
-            own = r_ref[:, n * block : (n + 1) * block].astype(F32)
-            product = (product + jnp.where(mine[p] == z, own, 0.0)).astype(BF16)
+            part = slice(n * block, (n + 1) * block)
             to = slice(p * width + n * block, p * width + (n + 1) * block)
-            a_ref[:, to] = product[:half]
-            b_ref[:, to] = product[half:]
+            product = dot(lin_ref[skip:], w_other_ref[p, :, part]).astype(BF16)
+            for (a, b), ref in zip(cuts[1:], send_refs):
+                ref[:, to] = product[a - skip : b - skip]
+    for p in range(2):
+        for n in range(2):
+            part = slice(n * block, (n + 1) * block)
+            to = slice(p * width + n * block, p * width + (n + 1) * block)
+            product = dot(lin_ref[...], w_mine_ref[p, :, part])
+            own = jnp.where(mine[p] == z, r_ref[:, part].astype(F32), 0.0)
+            product = (product + own).astype(BF16)
+            for (a, b), ref in zip(cuts, mine_refs):
+                ref[:, to] = product[a:b]
     for copy in copies:
         copy.wait()
 
@@ -267,11 +285,12 @@
             acc_ref[plane, :, to] = two_quarters(x_ref, w_ref, plane, mine, to)
 
 
-def first_hidden_body(block, x_ref, w_ref, a_ref, acc_ref, hidden_ref):
-    half, width = a_ref.shape[0], a_ref.shape[1] // 2
+def first_hidden_body(block, cuts, x_ref, w_ref, *refs):
+    total_refs, (acc_ref, hidden_ref) = refs[:-2], refs[-2:]
+    width = acc_ref.shape[2]
     own = at((lax.axis_index("head") // 2) * width, width)
-    hidden_ref[:half] = a_ref[:, own]
-    hidden_ref[half:] = x_ref[:, own]
+    for (a, b), ref in zip(cuts, (*total_refs, x_ref)):
+        hidden_ref[a:b] = ref[:, own]
     first_body(block, x_ref, w_ref, acc_ref)
 
 
@@ -289,69 +308,90 @@
             out_ref[:, n * block + h * HD : n * block + (h + 1) * HD] = turned.astype(BF16)
 
 
-def kv_body(block, mine, t_ref, x_ref, w_ref, acc_ref, cos_ref, sin_ref, kv_ref, inv_ref):
+def kv_body(block, rows, t_ref, x_ref, w_ref, acc_ref, cos_ref, sin_ref, after, kv_ref, rest_ref):
     t = t_ref[...].astype(F32)
     x = x_ref[...].astype(F32)
     total = jnp.sum(t * t + x * x, axis=1, keepdims=True)
     inv = lax.rsqrt(total / D + 1e-05)
-    inv_ref[...] = jnp.broadcast_to(inv, inv_ref.shape)
+    cos, sin = cos_ref[slice(*rows)], sin_ref[slice(*rows)]
     for plane in (1, 2):
-        finish(block, plane, x_ref, w_ref, acc_ref, inv, cos_ref[mine], sin_ref[mine], kv_ref.at[plane - 1])
-
-
-def q_body(block, mine, x_ref, w_ref, acc_ref, inv_ref, cos_ref, sin_ref, q_ref):
-    inv = inv_ref[:, :1]
-    finish(block, 0, x_ref, w_ref, acc_ref, inv, cos_ref[mine], sin_ref[mine], q_ref)
+        finish(block, plane, x_ref, w_ref, acc_ref, inv, cos, sin, kv_ref.at[plane - 1])
+    if rest_ref.dtype == BF16:
+        finish(block, 0, x_ref, w_ref, acc_ref, inv, cos, sin, rest_ref)
+    else:
+        rest_ref[...] = jnp.broadcast_to(inv, rest_ref.shape)
 
 
 SCORE = 1.0 / math.sqrt(HD)
 
 
-def early_body(qa_ref, qb_ref, a_ref, b_ref, pa_ref, acc_ref, top_ref, sum_ref):
+def stacked(refs, *where):
+    return jnp.concatenate([ref[where] for ref in refs], axis=0)
+
+
+def early_body(block, cuts, *refs):
+    count = len(cuts)
+    x_ref, w_ref, acc_in_ref, inv_ref, cos_ref, sin_ref = refs[:6]
+    q_refs, kv_refs = refs[6 : 5 + count], refs[5 + count : 5 + 2 * count]
+    prev_refs = refs[5 + 2 * count : 4 + 3 * count]
+    q_ref, acc_ref, top_ref, sum_ref = refs[4 + 3 * count :]
+    rows = slice(*cuts[-1])
+    finish(block, 0, x_ref, w_ref, acc_in_ref, inv_ref[:, :1], cos_ref[rows], sin_ref[rows], q_ref)
+    q_refs = (*q_refs, q_ref)
     has_prev = lax.axis_index("seq") > 0
-    half = qa_ref.shape[0]
-    shape = (2 * half, 3 * half)
-    row = lax.broadcasted_iota(jnp.int32, shape, 0)
-    col = lax.broadcasted_iota(jnp.int32, shape, 1)
-    allowed = ((col < half) & has_prev) | ((col >= half) & (col - half <= row))
-    for h in range(qa_ref.shape[1] // HD):
+    before = cuts[-1][0]
+    shape = (before + cuts[-1][1], cuts[-1][1])
+    key = lax.broadcasted_iota(jnp.int32, shape, 0)
+    query = lax.broadcasted_iota(jnp.int32, shape, 1)
+    allowed = ((key < before) & has_prev) | ((key >= before) & (key - before <= query))
+    for h in range(q_ref.shape[1] // HD):
         head = slice(h * HD, (h + 1) * HD)
-        queries = jnp.concatenate([qa_ref[:, head], qb_ref[:, head]], axis=0)
-        keys = jnp.concatenate([r[0, :, head] for r in (pa_ref, a_ref, b_ref)], axis=0)
-        values = jnp.concatenate([r[1, :, head] for r in (pa_ref, a_ref, b_ref)], axis=0)
-        logits = jnp.where(allowed, dot_nt(queries, keys) * SCORE, NEG)
-        top = jnp.max(logits, axis=1, keepdims=True)
+        keys = stacked((*prev_refs, *kv_refs), 0, slice(None), head)
+        values = stacked((*prev_refs, *kv_refs), 1, slice(None), head)
+        logits = dot_nt(keys, stacked(q_refs, slice(None), head)) * SCORE
+        logits = jnp.where(allowed, logits, NEG)
+        top = jnp.max(logits, axis=0, keepdims=True)
         expo = jnp.where(allowed, jnp.exp(logits - top), 0.0)
-        top_ref[h] = top
-        sum_ref[h] = jnp.sum(expo, axis=1, keepdims=True)
-        acc_ref[:, head] = dot(expo.astype(BF16), values)
-
-
-def late_body(qa_ref, qb_ref, pb_ref, acc_ref, top_ref, sum_ref, out_ref):
+        top_ref[h : h + 1] = top
+        sum_ref[h : h + 1] = jnp.sum(expo, axis=0, keepdims=True)
+        acc_ref[h] = dot_tn(values, expo.astype(BF16))
+
+
+def late_body(count, *refs):
+    q_refs, (prev_ref, acc_ref, top_ref, sum_ref, out_ref) = refs[:count], refs[count:]
     has_prev = lax.axis_index("seq") > 0
-    for h in range(qa_ref.shape[1] // HD):
-        head = slice(h * HD, (h + 1) * HD)
-        queries = jnp.concatenate([qa_ref[:, head], qb_ref[:, head]], axis=0)
-        logits = jnp.where(has_prev, dot_nt(queries, pb_ref[0, :, head]) * SCORE, NEG)
-        before = top_ref[h]
-        top = jnp.maximum(before, jnp.max(logits, axis=1, keepdims=True))
-        expo = jnp.where(has_prev, jnp.exp(logits - top), 0.0)
-        fade = jnp.exp(before - top)
-        total = sum_ref[h] * fade + jnp.sum(expo, axis=1, keepdims=True)
-        acc = acc_ref[:, head] * fade + dot(expo.astype(BF16), pb_ref[1, :, head])
-        out_ref[:, head] = (acc / total).astype(BF16)
-
-
-def tuned(lin_qkv, resid, w_out, w_qkv):
+    heads = range(out_ref.shape[1] // HD)
+    at_head = [slice(h * HD, (h + 1) * HD) for h in heads]
+    logits = [
+        jnp.where(has_prev, dot_nt(prev_ref[0, :, at], stacked(q_refs, slice(None), at)) * SCORE, NEG)
+        for at in at_head
+    ]
+    highest = jnp.concatenate([jnp.max(x, axis=0, keepdims=True) for x in logits], axis=0)
+    top = jnp.maximum(top_ref[...], highest)
+    fade = jnp.exp(top_ref[...] - top)
+    expo = [jnp.where(has_prev, jnp.exp(logits[h] - top[h : h + 1]), 0.0) for h in heads]
+    sums = jnp.concatenate([jnp.sum(x, axis=0, keepdims=True) for x in expo], axis=0)
+    inverse = 1.0 / (sum_ref[...] * fade + sums)
+    fade = fade * inverse
+    for h in heads:
+        weights = (expo[h] * inverse[h : h + 1]).astype(BF16)
+        total = acc_ref[h] * fade[h : h + 1] + dot_tn(prev_ref[1, :, at_head[h]], weights)
+        out_ref[:, at_head[h]] = total.T.astype(BF16)
+
+
+def tuned(streams, lin_qkv, resid, w_out, w_qkv):
     rows, _, width = lin_qkv.shape
     nheads = width // HD
-    half = rows // 2
     group = nheads // 2
     full = w_out.shape[1]
     block = width // 2
     seq = lax.axis_index("seq")
     core = seq % 2
     shape = jax.ShapeDtypeStruct
+    edges = [rows * sum(streams[:i]) // sum(streams) for i in range(len(streams) + 1)]
+    cuts = list(zip(edges, edges[1:]))
+    sizes = [b - a for a, b in cuts]
+    last = len(cuts) - 1
 
     qkv = jnp.transpose(lin_qkv, (1, 0, 2))
     wqkv = jnp.transpose(w_qkv, (1, 0, 2))
@@ -387,6 +427,7 @@
             [ON_CHIP, ANYWHERE, ANYWHERE, ANYWHERE, IN_HBM], (pltpu.SemaphoreType.DMA((4,)),),
             flops=4 * rows * rows * width, moved=2 * width * full,
         )
+        w_other, w_mine = in_vmem(w_other), in_vmem(w_mine)
     with jax.named_scope("prefix"):
         x_bit = ((seq // 2) % 2).astype(F32)
         y_bit = (seq // 4).astype(F32)
@@ -400,69 +441,79 @@
         other_prefix = swapped(jnp.where(core == 0, high, low), "seq", 1)
 
     scale = 1.0 / math.sqrt(HD * rows * lax.axis_size("seq"))
-    halves = shape((half, full // 2), BF16)
+    halves = [shape((n, full // 2), BF16) for n in sizes]
+    lin_scratch = pltpu.VMEM((rows, width), BF16)
+    lin_inputs = (q, intra, own_prefix, other_prefix, w_other)
     with jax.named_scope("partials"):
-        lin_out, send_a, send_b = call(
-            functools.partial(send_body, scale), (q, intra, own_prefix, other_prefix, in_vmem(w_other)),
-            (shape((rows, width), BF16), halves, halves), flops=rows * width * full, moved=width * full,
-        )
-        got_a = lax.ppermute(send_a, "head", PAIR)
-        mine_a, mine_b, w_here = call(
-            mine_body, (lin_out, in_vmem(w_mine), resid, in_hbm(wqkv)),
-            (halves, halves, pltpu.VMEM(wqkv.shape, BF16)),
-            [ON_CHIP, ON_CHIP, ON_CHIP, IN_HBM], (pltpu.SemaphoreType.DMA((3 * full // width,)),),
-            flops=rows * width * full, moved=6 * width * full,
-        )
+        first_send = call(
+            functools.partial(send_body, scale, cuts), lin_inputs, halves[0], scratch=(lin_scratch,),
+            flops=sizes[0] * width * full, moved=width * full,
+        )
+        got = [lax.ppermute(first_send, "head", PAIR)]
+        *made, w_here = call(
+            functools.partial(mine_body, scale, cuts), (*lin_inputs, w_mine, resid, in_hbm(wqkv)),
+            (*halves[1:], *halves, pltpu.VMEM(wqkv.shape, BF16)),
+            [ON_CHIP] * 7 + [IN_HBM], (lin_scratch, pltpu.SemaphoreType.DMA((3 * full // width,))),
+            flops=2 * rows * width * full, moved=6 * width * full,
+        )
+        sends, mines = made[:last], made[last:]
         w_here = in_vmem(w_here)
-    accs = shape((3, half, width), F32)
-    cost = dict(flops=half * full * 3 * width, moved=3 * width * full)
 
     def add(a, b):
-        return call(add_body, (a, b), halves, vmem=4, moved=6 * half * full)
-
-    def project(total, got, acc, index):
-        turn = (cos2, sin2)
-        mine = pl.ds(index * half, half)
-        kv, inv = call(
-            functools.partial(kv_body, block, mine), (total, got, w_here, acc, *turn),
-            (shape((2, half, width), BF16), shape((half, HD), F32)), **cost,
-        )
-        before = shifted(kv, "seq", 1)
-        query = call(
-            functools.partial(q_body, block, mine), (got, w_here, acc, inv, *turn), shape((half, width), BF16), **cost,
-        )
-        return kv, before, query
+        return call(add_body, (a, b), shape(a.shape, BF16), vmem=4, moved=3 * a.size)
 
     with jax.named_scope("mix"):
-        send_b, got_a = lax.optimization_barrier((send_b, got_a))
-        got_b = lax.ppermute(send_b, "head", PAIR)
-        sum_a = add(mine_a, got_a)
-        far_a = lax.ppermute(sum_a, "head", CROSS)
-        sum_b = add(mine_b, got_b)
-        sum_b, far_a = lax.optimization_barrier((sum_b, far_a))
-        far_b = lax.ppermute(sum_b, "head", CROSS)
-        total_a = add(sum_a, far_a)
-        rest_a = lax.ppermute(total_a, "head", PAIR)
-        total_b = add(sum_b, far_b)
-        rest_b = lax.ppermute(total_b, "head", PAIR)
-    with jax.named_scope("project_a"):
-        acc_a = call(functools.partial(first_body, block), (total_a, w_here), accs, **cost)
-        kv_a, prev_a, query_a = project(total_a, rest_a, acc_a, 0)
-    with jax.named_scope("project_b"):
-        acc_b, hidden = call(
-            functools.partial(first_hidden_body, block), (total_b, w_here, total_a),
-            (accs, shape((rows, width), BF16)), **cost,
-        )
-        kv_b, prev_b, query_b = project(total_b, rest_b, acc_b, 1)
+        totals, rests = [], []
+        far = None
+        for i in range(last + 1):
+            if i > 0:
+                ready = sends[i - 1]
+                got.append(lax.ppermute(ready, "head", PAIR))
+        for i in range(last + 1):
+            partial = add(mines[i], got[i])
+            if i > 0:
+                pass
+                totals.append(add(held, far))
+            far = lax.ppermute(partial, "head", CROSS)
+            held = partial
+        totals.append(add(held, far))
+        rests = [lax.ppermute(total, "head", PAIR) for total in totals]
+
+    queries, kvs, prevs, accs = [], [], [], []
+    cost = dict(flops=rows * full * 3 * width, moved=3 * width * full)
+    with jax.named_scope("project"):
+        for i in range(last):
+            acc = shape((3, sizes[i], width), F32)
+            accs.append(call(functools.partial(first_body, block), (totals[i], w_here), acc, **cost))
+        acc, hidden = call(
+            functools.partial(first_hidden_body, block, cuts), (totals[last], w_here, *totals[:last]),
+            (shape((3, sizes[last], width), F32), shape((rows, width), BF16)), **cost,
+        )
+        accs.append(acc)
+    for i in range(last + 1):
+        n = sizes[i]
+        with jax.named_scope("project"):
+            kv, other = call(
+                functools.partial(kv_body, block, cuts[i]),
+                (totals[i], rests[i], w_here, accs[i], cos2, sin2, hidden),
+                (shape((2, n, width), BF16), shape((n, width), BF16) if i < last else shape((n, HD), F32)),
+                [ON_CHIP] * 6 + [ANYWHERE], **cost,
+            )
+            kvs.append(kv)
+            queries.append(other)
+            prevs.append(lax.ppermute(kv, "seq", [(i, (i + 1) % 8) for i in range(8)]))
     with jax.named_scope("attend"):
-        stat = shape((nheads, rows, 1), F32)
-        acc, top, total = call(
-            early_body, (query_a, query_b, kv_a, kv_b, prev_a), (shape((rows, width), F32), stat, stat),
-            flops=6 * rows * rows * width, moved=12 * rows * width,
+        inv = queries.pop()
+        stat = shape((nheads, rows), F32)
+        query, acc, top, total = call(
+            functools.partial(early_body, block, cuts),
+            (rests[last], w_here, acc, inv, cos2, sin2, *queries, *kvs, *prevs[:last]),
+            (shape((sizes[last], width), BF16), shape((nheads, HD, rows), F32), stat, stat),
+            flops=8 * rows * rows * width, moved=12 * rows * width,
         )
         attended = call(
-            late_body, (query_a, query_b, prev_b, acc, top, total), shape((rows, width), BF16),
-            flops=2 * rows * rows * width, moved=12 * rows * width,
+            functools.partial(late_body, last + 1), (*queries, query, prevs[last], acc, top, total),
+            shape((rows, width), BF16), flops=2 * rows * rows * width, moved=12 * rows * width,
         )
     return hidden, attended
 
@@ -470,7 +521,7 @@
 def solution(mesh):
     line = mesh.shape["seq"] == 8 and mesh.shape["head"] == 4
     return jax.shard_map(
-        tuned if line else general,
+        functools.partial(tuned, STREAMS) if line else general,
         mesh=mesh,
         in_specs=(P("seq", None, "head"), P("seq", "head"), P("head", None), P(None, None, "head")),
         out_specs=(P("seq", "head"), P("seq", "head")),

time: 109 us -> 104 us (0.954); the launches traced: 109 us -> 102 us
  waiting for transfers between devices: 43 us -> 32.8 us
  starting transfers between devices: 32.5 us -> 38.6 us
  Pallas kernels: 31.6 us -> 29.4 us
    ppermute x8, waiting for transfers between devices: 39.8 us -> 29.6 us  [the longest x2 8.46 us: tuned(): far = lax.ppermute(partial, 'head', CROSS)]
    ppermute x8, starting transfers between devices: 28.8 us -> 34.9 us  [the longest x2 24.2 us: tuned(): far = lax.ppermute(partial, 'head', CROSS)]
    pallas_call x16 -> x14, Pallas kernels: 31.6 us -> 29.4 us  [call(): pl.pallas_call(body, in_specs=in_specs or [ON_CHIP] * len(ins), out_specs...]
  transfers between devices with their start and end apart: 13 -> 13, of which waited for: 10 -> 9; matrix products, arithmetic and copies ran while one was open for 1% -> 1% of each run, Pallas kernels for 23% -> 24%
where the time goes in v5:
time: 104 us; the launch traced here: 102 us
  starting transfers between devices  38.6 us (37%)
  waiting for transfers between devices  32.8 us (32%)
  Pallas kernels  29.4 us (28%)
    pallas_call x14, Pallas kernels, call(): pl.pallas_call(body, in_specs=in_specs or [ON_CHIP] * len(ins), out_specs...  29.4 us
    ppermute x2, starting transfers between devices, tuned(): far = lax.ppermute(partial, 'head', CROSS)  24.2 us
    ppermute x2, waiting for transfers between devices, tuned(): far = lax.ppermute(partial, 'head', CROSS)  8.46 us
    ppermute x2, starting transfers between devices, tuned(): rests = [lax.ppermute(total, 'head', PAIR) for total in totals]  8.22 us
    ppermute x1, waiting for transfers between devices, tuned(): got.append(lax.ppermute(ready, 'head', PAIR))  6.63 us
    ppermute x2, waiting for transfers between devices, tuned(): prevs.append(lax.ppermute(kv, 'seq', [(i, (i + 1) % 8) for i in range(8)]))  5.93 us
    ppermute x2, waiting for transfers between devices, tuned(): rests = [lax.ppermute(total, 'head', PAIR) for total in totals]  4.57 us
    ppermute x1, waiting for transfers between devices, tuned(): got = [lax.ppermute(first_send, 'head', PAIR)]  4.01 us
  transfers between devices with their start and end apart: 13, of which 9 were waited for; matrix products, arithmetic and copies ran while one was open for 1% of the time, Pallas kernels for 24%

profile of v5, /device:TPU:4, one launch (start us, length us, event | category | flops | bytes accessed | tf_op | source)
XLA Modules:
  0.0 102.5 jit_solution(5825791399206477903)
XLA Ops:
  0.6 0.0 copy-start
  0.6 1.7 %state.1 = (bf16[4,128,128]{2,1,0:T(8,128)(2,1)S(1)}, bf16[4,128,128]{2,1,0:T(8,128)(2,1)S(1)}) custom-call(bf16[3,256,1024]{2,1,0:T(8,128)(2,1)} %bitcast.2), custom_call_target="tpu_custom_call" | custom-call | flops 67108864 | bytes 1048576 | tf_op jit(solution)/shard_map/state/pallas_call | solution.py:128
  2.4 0.1 collective-permute-start
  2.6 0.5 fusion.1
  3.1 0.7 collective-permute-done
  3.8 1.5 %collective-permute-start.3 = (bf16[4,128,128]{2,1,0:T(8,128)(2,1)S(1)}, bf16[4,128,128]{2,1,0:T(8,128)(2,1)S(1)}, u32[]{:S(2)}, u32[]{:S(2)}) collective-permute-start(bf16[4,128,128]{2,1,0:T(8,128)(2,1)S(1)} %add_convert_fusion.1.after), channel_id=1, source_target_pairs={{0,24},{4,28},{8,16},{12,20},{16,8},{20,12},{24,0},{28,4},{1,25},{... | collective-permute-start | bytes 393224 | tf_op jit(solution)/shard_map/state/ppermute | solution.py:29
  5.3 1.5 %collective-permute-start.2 = (bf16[4,128,128]{2,1,0:T(8,128)(2,1)S(1)}, bf16[4,128,128]{2,1,0:T(8,128)(2,1)S(1)}, u32[]{:S(2)}, u32[]{:S(2)}) collective-permute-start(bf16[4,128,128]{2,1,0:T(8,128)(2,1)S(1)} %add_convert_fusion.1.after), channel_id=1, source_target_pairs={{0,16},{4,20},{8,24},{12,28},{16,0},{20,4},{24,8},{28,12},{1,17},{... | collective-permute-start | bytes 393224 | tf_op jit(solution)/shard_map/state/ppermute | solution.py:29
  6.9 0.5 collective-permute-start.1
  7.4 0.1 pad_maximum_fusion
  7.5 0.0 copy-done
  7.5 4.4 %intra.1 = (f32[256,1024]{1,0:T(8,128)S(1)}, bf16[256,1024]{1,0:T(8,128)(2,1)S(1)}, bf16[2,1024,1024]{2,1,0:T(8,128)(2,1)S(1)}, bf16[2,1024,1024]{2,1,0:T(8,128)(2,1)S(1)}) custom-call(bf16[3,256,1024]{2,1,0:T(8,128)(2,1)S(1)} %bitcast.3, bf16[4,128,128]{2,1,0:T(8,128)(2,1)S(1)} %add_convert_fusion.1.after, ...), custom_call_target="tpu_custom_call" | custom-call | flops 268435456 | bytes 8388608 | tf_op jit(solution)/shard_map/intra/pallas_call | solution.py:128
  12.0 0.0 copy-start.2
  12.0 0.0 collective-permute-done.3
  12.0 1.2 %collective-permute-done.2 = bf16[4,128,128]{2,1,0:T(8,128)(2,1)S(1)} collective-permute-done((bf16[4,128,128]{2,1,0:T(8,128)(2,1)S(1)}, bf16[4,128,128]{2,1,0:T(8,128)(2,1)S(1)}, u32[]{:S(2)}, u32[]{:S(2)}) %collective-permute-start.2) | collective-permute-done | bytes 131104 | tf_op jit(solution)/shard_map/state/ppermute | solution.py:29
  13.2 0.0 collective-permute-done.1
  13.2 0.1 broadcast_select_fusion
  13.3 0.1 collective-permute-start.4
  13.4 1.3 %collective-permute-done.4.refs_3_.other_ref = bf16[4,128,128]{2,1,0:T(8,128)(2,1)S(1)} collective-permute-done((bf16[4,128,128]{2,1,0:T(8,128)(2,1)S(1)}, bf16[4,128,128]{2,1,0:T(8,128)(2,1)S(1)}, u32[]{:S(2)}, u32[]{:S(2)}) %collective-permute-start.4) | collective-permute-done | bytes 131104 | tf_op jit(solution)/shard_map/prefix/ppermute | solution.py:29
  14.7 0.9 partials.3
  15.7 1.6 %collective-permute-start.7 = (bf16[128,2048]{1,0:T(8,128)(2,1)S(1)}, bf16[128,2048]{1,0:T(8,128)(2,1)S(1)}, u32[]{:S(2)}, u32[]{:S(2)}) collective-permute-start(bf16[128,2048]{1,0:T(8,128)(2,1)S(1)} %partials.3), channel_id=1, source_target_pairs={{0,1},{1,0},{2,3},{3,2},{4,5},{5,4},{6,7},{7,6},{8,9},{9,8},{10,11... | collective-permute-start | bytes 1572872 | tf_op jit(solution)/shard_map/partials/ppermute | solution.py:452
  17.3 0.0 copy-done.2
  17.3 8.7 %partials.2 = (bf16[128,2048]{1,0:T(8,128)(2,1)S(1)}, bf16[128,2048]{1,0:T(8,128)(2,1)S(1)}, bf16[128,2048]{1,0:T(8,128)(2,1)S(1)}, bf16[3,4096,1024]{2,1,0:T(8,128)(2,1)S(1)}) custom-call(bf16[256,1024]{1,0:T(8,128)(2,1)S(1)} %get-tuple-element.24.refs_0_.q_ref, f32[256,1024]{1,0:T(8,128)S(1)} %get-tuple-element.25.refs_1_.intra_ref, ...), custom_call_target="tpu_custom_call" | custom-call | flops 2147483648 | bytes 25165824 | tf_op jit(solution)/shard_map/partials/pallas_call | solution.py:128
  26.0 0.5 collective-permute-start.5
  26.5 4.0 %collective-permute-done.7.b_ref = bf16[128,2048]{1,0:T(8,128)(2,1)S(1)} collective-permute-done((bf16[128,2048]{1,0:T(8,128)(2,1)S(1)}, bf16[128,2048]{1,0:T(8,128)(2,1)S(1)}, u32[]{:S(2)}, u32[]{:S(2)}) %collective-permute-start.7) | collective-permute-done | bytes 524320 | tf_op jit(solution)/shard_map/partials/ppermute | solution.py:452
  30.5 0.1 mix.6.a_ref
  30.6 3.7 %collective-permute-start.8 = (bf16[128,2048]{1,0:T(8,128)(2,1)S(1)}, bf16[128,2048]{1,0:T(8,128)(2,1)S(1)}, u32[]{:S(2)}, u32[]{:S(2)}) collective-permute-start(bf16[128,2048]{1,0:T(8,128)(2,1)S(1)} %mix.6.a_ref), channel_id=1, source_target_pairs={{0,3},{3,0},{1,2},{2,1},{4,7},{7,4},{5,6},{6,5},{8,11},{11,8},{9,1... | collective-permute-start | bytes 1572872 | tf_op jit(solution)/shard_map/mix/ppermute | solution.py:477
  34.3 6.6 %collective-permute-done.5.b_ref = bf16[128,2048]{1,0:T(8,128)(2,1)S(1)} collective-permute-done((bf16[128,2048]{1,0:T(8,128)(2,1)S(1)}, bf16[128,2048]{1,0:T(8,128)(2,1)S(1)}, u32[]{:S(2)}, u32[]{:S(2)}) %collective-permute-start.5) | collective-permute-done | bytes 524320 | tf_op jit(solution)/shard_map/mix/ppermute | solution.py:471
  40.9 0.1 mix.4.a_ref
  41.1 20.5 %collective-permute-start.6 = (bf16[128,2048]{1,0:T(8,128)(2,1)S(1)}, bf16[128,2048]{1,0:T(8,128)(2,1)S(1)}, u32[]{:S(2)}, u32[]{:S(2)}) collective-permute-start(bf16[128,2048]{1,0:T(8,128)(2,1)S(1)} %mix.4.a_ref), channel_id=1, source_target_pairs={{0,3},{3,0},{1,2},{2,1},{4,7},{7,4},{5,6},{6,5},{8,11},{11,8},{9,1... | collective-permute-start | bytes 1572872 | tf_op jit(solution)/shard_map/mix/ppermute | solution.py:477
  61.6 0.0 collective-permute-done.8.b_ref
  61.6 0.1 mix.7.refs_0_.x_ref.t_ref
  61.7 1.1 %collective-permute-start.9 = (bf16[128,2048]{1,0:T(8,128)(2,1)S(1)}, bf16[128,2048]{1,0:T(8,128)(2,1)S(1)}, u32[]{:S(2)}, u32[]{:S(2)}) collective-permute-start(bf16[128,2048]{1,0:T(8,128)(2,1)S(1)} %mix.7.refs_0_.x_ref.t_ref), channel_id=1, source_target_pairs={{0,1},{1,0},{2,3},{3,2},{4,5},{5,4},{6,7},{7,6},{8,9},{9,8},{10,11... | collective-permute-start | bytes 1572872 | tf_op jit(solution)/shard_map/mix/ppermute | solution.py:480
  62.8 8.5 %collective-permute-done.6.b_ref = bf16[128,2048]{1,0:T(8,128)(2,1)S(1)} collective-permute-done((bf16[128,2048]{1,0:T(8,128)(2,1)S(1)}, bf16[128,2048]{1,0:T(8,128)(2,1)S(1)}, u32[]{:S(2)}, u32[]{:S(2)}) %collective-permute-start.6) | collective-permute-done | bytes 524320 | tf_op jit(solution)/shard_map/mix/ppermute | solution.py:477
  71.3 0.1 mix.5.x_ref.t_ref
  71.4 7.1 %collective-permute-start.10 = (bf16[128,2048]{1,0:T(8,128)(2,1)S(1)}, bf16[128,2048]{1,0:T(8,128)(2,1)S(1)}, u32[]{:S(2)}, u32[]{:S(2)}) collective-permute-start(bf16[128,2048]{1,0:T(8,128)(2,1)S(1)} %mix.5.x_ref.t_ref), channel_id=1, source_target_pairs={{0,1},{1,0},{2,3},{3,2},{4,5},{5,4},{6,7},{7,6},{8,9},{9,8},{10,11... | collective-permute-start | bytes 1572872 | tf_op jit(solution)/shard_map/mix/ppermute | solution.py:480
  78.5 2.5 %project.4 = (f32[3,128,1024]{2,1,0:T(8,128)S(1)}, bf16[256,1024]{1,0:T(8,128)(2,1)}) custom-call(bf16[128,2048]{1,0:T(8,128)(2,1)S(1)} %mix.5.x_ref.t_ref, bf16[3,4096,1024]{2,1,0:T(8,128)(2,1)S(1)} %get-tuple-element.30.w_ref.refs_1_, bf16[128,2048]{1,0:T(8,128)(2,1)S(1)} %mix.7.refs_0_.x_ref.t_ref), custom_call_target="tpu_custom_call" | custom-call | flops 3221225472 | bytes 12582912 | tf_op jit(solution)/shard_map/project/pallas_call | solution.py:128
  81.0 1.8 %project.5.acc_ref = f32[3,128,1024]{2,1,0:T(8,128)S(1)} custom-call(bf16[128,2048]{1,0:T(8,128)(2,1)S(1)} %mix.7.refs_0_.x_ref.t_ref, bf16[3,4096,1024]{2,1,0:T(8,128)(2,1)S(1)} %get-tuple-element.30.w_ref.refs_1_), custom_call_target="tpu_custom_call" | custom-call | flops 3221225472 | bytes 12582912 | tf_op jit(solution)/shard_map/project/pallas_call | solution.py:128
  82.8 0.0 collective-permute-done.9.x_ref
  82.9 0.0 copy-done.1
  82.9 2.1 %project.6 = (bf16[2,128,1024]{2,1,0:T(8,128)(2,1)S(1)}, bf16[128,1024]{1,0:T(8,128)(2,1)S(1)}) custom-call(bf16[128,2048]{1,0:T(8,128)(2,1)S(1)} %mix.7.refs_0_.x_ref.t_ref, bf16[128,2048]{1,0:T(8,128)(2,1)S(1)} %collective-permute-done.9.x_ref, bf16[3,4096,1024]{2,1,0:T(8,128)(2,1)S(1)} %get-tuple-element.30.w_ref.refs_1_, ...), custom_call_target="tpu_custom_call" | custom-call | flops 3221225472 | bytes 12582912 | tf_op jit(solution)/shard_map/project/pallas_call | solution.py:128
  85.0 0.2 collective-permute-start.11
  85.2 4.6 %collective-permute-done.10.x_ref.refs_0_ = bf16[128,2048]{1,0:T(8,128)(2,1)S(1)} collective-permute-done((bf16[128,2048]{1,0:T(8,128)(2,1)S(1)}, bf16[128,2048]{1,0:T(8,128)(2,1)S(1)}, u32[]{:S(2)}, u32[]{:S(2)}) %collective-permute-start.10) | collective-permute-done | bytes 524320 | tf_op jit(solution)/shard_map/mix/ppermute | solution.py:480
  89.8 1.4 %project.7 = (bf16[2,128,1024]{2,1,0:T(8,128)(2,1)S(1)}, f32[128,128]{1,0:T(8,128)S(1)}) custom-call(bf16[128,2048]{1,0:T(8,128)(2,1)S(1)} %mix.5.x_ref.t_ref, bf16[128,2048]{1,0:T(8,128)(2,1)S(1)} %collective-permute-done.10.x_ref.refs_0_, bf16[3,4096,1024]{2,1,0:T(8,128)(2,1)S(1)} %get-tuple-element.30.w_ref.refs_1_, ...), custom_call_target="tpu_custom_call" | custom-call | flops 3221225472 | bytes 12582912 | tf_op jit(solution)/shard_map/project/pallas_call | solution.py:128
  91.2 0.1 collective-permute-start.12
  91.3 3.4 %collective-permute-done.11.refs_9_ = bf16[2,128,1024]{2,1,0:T(8,128)(2,1)S(1)} collective-permute-done((bf16[2,128,1024]{2,1,0:T(8,128)(2,1)S(1)}, bf16[2,128,1024]{2,1,0:T(8,128)(2,1)S(1)}, u32[]{:S(2)}, u32[]{:S(2)}) %collective-permute-start.11) | collective-permute-done | bytes 524320 | tf_op jit(solution)/shard_map/project/ppermute | solution.py:504
  94.7 3.6 %attend.2 = (bf16[128,1024]{1,0:T(8,128)(2,1)S(1)}, f32[8,128,256]{2,1,0:T(8,128)S(1)}, f32[8,256]{1,0:T(8,128)S(1)}, f32[8,256]{1,0:T(8,128)S(1)}) custom-call(bf16[128,2048]{1,0:T(8,128)(2,1)S(1)} %collective-permute-done.10.x_ref.refs_0_, bf16[3,4096,1024]{2,1,0:T(8,128)(2,1)S(1)} %get-tuple-element.30.w_ref.refs_1_, ...), custom_call_target="tpu_custom_call" | custom-call | flops 536870912 | bytes 3145728 | tf_op jit(solution)/shard_map/attend/pallas_call | solution.py:128
  98.3 2.5 %collective-permute-done.12.refs_2_ = bf16[2,128,1024]{2,1,0:T(8,128)(2,1)S(1)} collective-permute-done((bf16[2,128,1024]{2,1,0:T(8,128)(2,1)S(1)}, bf16[2,128,1024]{2,1,0:T(8,128)(2,1)S(1)}, u32[]{:S(2)}, u32[]{:S(2)}) %collective-permute-start.12) | collective-permute-done | bytes 524320 | tf_op jit(solution)/shard_map/project/ppermute | solution.py:504
  100.8 1.7 %attend.3 = bf16[256,1024]{1,0:T(8,128)(2,1)} custom-call(bf16[128,1024]{1,0:T(8,128)(2,1)S(1)} %get-tuple-element.33.refs_6_.refs_0_, bf16[128,1024]{1,0:T(8,128)(2,1)S(1)} %get-tuple-element.38.refs_1_, bf16[2,128,1024]{2,1,0:T(8,128)(2,1)S(1)} %collective-permute-done.12.refs_2_, f32[8,128,256]{2,1,0:T(8,128)S(1)} %get-tuple-element.39.refs_3_, ...), custom_call_target="tpu_custom_call" | custom-call | flops 134217728 | bytes 3145728 | tf_op jit(solution)/shard_map/attend/pallas_call | solution.py:128
  (5 shorter events, 0.1 us)
Async XLA Ops:
  0.6 6.9 %copy-start = (bf16[256,3,1024]{2,0,1:T(8,128)(2,1)S(1)}, bf16[256,3,1024]{2,0,1:T(8,128)(2,1)}, u32[]{:S(2)}) copy-start(bf16[256,3,1024]{2,0,1:T(8,128)(2,1)} %param.4) | copy-start | bytes 4718596
  2.4 1.4 %collective-permute-start = (bf16[4,128,128]{2,1,0:T(8,128)(2,1)S(1)}, bf16[4,128,128]{2,1,0:T(8,128)(2,1)S(1)}, u32[]{:S(2)}, u32[]{:S(2)}) collective-permute-start(bf16[4,128,128]{2,1,0:T(8,128)(2,1)S(1)} %get-tuple-element.23), channel_id=1, source_target_pairs={{0,4},{4,0},{8,12},{12,8},{16,20},{20,16},{24,28},{28,24},{1,5},{5... | collective-permute-start | bytes 393224 | tf_op jit(solution)/shard_map/state/ppermute | solution.py:29
  3.8 8.1 %collective-permute-start.3 = (bf16[4,128,128]{2,1,0:T(8,128)(2,1)S(1)}, bf16[4,128,128]{2,1,0:T(8,128)(2,1)S(1)}, u32[]{:S(2)}, u32[]{:S(2)}) collective-permute-start(bf16[4,128,128]{2,1,0:T(8,128)(2,1)S(1)} %add_convert_fusion.1.after), channel_id=1, source_target_pairs={{0,24},{4,28},{8,16},{12,20},{16,8},{20,12},{24,0},{28,4},{1,25},{... | collective-permute-start | bytes 393224 | tf_op jit(solution)/shard_map/state/ppermute | solution.py:29
  5.3 7.8 %collective-permute-start.2 = (bf16[4,128,128]{2,1,0:T(8,128)(2,1)S(1)}, bf16[4,128,128]{2,1,0:T(8,128)(2,1)S(1)}, u32[]{:S(2)}, u32[]{:S(2)}) collective-permute-start(bf16[4,128,128]{2,1,0:T(8,128)(2,1)S(1)} %add_convert_fusion.1.after), channel_id=1, source_target_pairs={{0,16},{4,20},{8,24},{12,28},{16,0},{20,4},{24,8},{28,12},{1,17},{... | collective-permute-start | bytes 393224 | tf_op jit(solution)/shard_map/state/ppermute | solution.py:29
  6.9 6.3 %collective-permute-start.1 = (bf16[4,128,128]{2,1,0:T(8,128)(2,1)S(1)}, bf16[4,128,128]{2,1,0:T(8,128)(2,1)S(1)}, u32[]{:S(2)}, u32[]{:S(2)}) collective-permute-start(bf16[4,128,128]{2,1,0:T(8,128)(2,1)S(1)} %add_convert_fusion.1.after), channel_id=1, source_target_pairs={{0,8},{4,12},{8,0},{12,4},{16,24},{20,28},{24,16},{28,20},{1,9},{5... | collective-permute-start | bytes 393224 | tf_op jit(solution)/shard_map/state/ppermute | solution.py:29
  12.0 5.3 %copy-start.2 = (bf16[256,1024]{1,0:T(8,128)(2,1)S(1)}, bf16[256,1024]{1,0:T(8,128)(2,1)}, u32[]{:S(2)}) copy-start(bf16[256,1024]{1,0:T(8,128)(2,1)} %refs_6_.1) | copy-start | bytes 1572868
  13.3 1.4 %collective-permute-start.4 = (bf16[4,128,128]{2,1,0:T(8,128)(2,1)S(1)}, bf16[4,128,128]{2,1,0:T(8,128)(2,1)S(1)}, u32[]{:S(2)}, u32[]{:S(2)}) collective-permute-start(bf16[4,128,128]{2,1,0:T(8,128)(2,1)S(1)} %get-tuple-element.42), channel_id=1, source_target_pairs={{0,4},{4,0},{8,12},{12,8},{16,20},{20,16},{24,28},{28,24},{1,5},{5... | collective-permute-start | bytes 393224 | tf_op jit(solution)/shard_map/prefix/ppermute | solution.py:29
  15.7 14.8 %collective-permute-start.7 = (bf16[128,2048]{1,0:T(8,128)(2,1)S(1)}, bf16[128,2048]{1,0:T(8,128)(2,1)S(1)}, u32[]{:S(2)}, u32[]{:S(2)}) collective-permute-start(bf16[128,2048]{1,0:T(8,128)(2,1)S(1)} %partials.3), channel_id=1, source_target_pairs={{0,1},{1,0},{2,3},{3,2},{4,5},{5,4},{6,7},{7,6},{8,9},{9,8},{10,11... | collective-permute-start | bytes 1572872 | tf_op jit(solution)/shard_map/partials/ppermute | solution.py:452
  26.0 15.0 %collective-permute-start.5 = (bf16[128,2048]{1,0:T(8,128)(2,1)S(1)}, bf16[128,2048]{1,0:T(8,128)(2,1)S(1)}, u32[]{:S(2)}, u32[]{:S(2)}) collective-permute-start(bf16[128,2048]{1,0:T(8,128)(2,1)S(1)} %get-tuple-element.29), channel_id=1, source_target_pairs={{0,1},{1,0},{2,3},{3,2},{4,5},{5,4},{6,7},{7,6},{8,9},{9,8},{10,11... | collective-permute-start | bytes 1572872 | tf_op jit(solution)/shard_map/mix/ppermute | solution.py:471
  30.6 31.0 %collective-permute-start.8 = (bf16[128,2048]{1,0:T(8,128)(2,1)S(1)}, bf16[128,2048]{1,0:T(8,128)(2,1)S(1)}, u32[]{:S(2)}, u32[]{:S(2)}) collective-permute-start(bf16[128,2048]{1,0:T(8,128)(2,1)S(1)} %mix.6.a_ref), channel_id=1, source_target_pairs={{0,3},{3,0},{1,2},{2,1},{4,7},{7,4},{5,6},{6,5},{8,11},{11,8},{9,1... | collective-permute-start | bytes 1572872 | tf_op jit(solution)/shard_map/mix/ppermute | solution.py:477
  41.1 30.2 %collective-permute-start.6 = (bf16[128,2048]{1,0:T(8,128)(2,1)S(1)}, bf16[128,2048]{1,0:T(8,128)(2,1)S(1)}, u32[]{:S(2)}, u32[]{:S(2)}) collective-permute-start(bf16[128,2048]{1,0:T(8,128)(2,1)S(1)} %mix.4.a_ref), channel_id=1, source_target_pairs={{0,3},{3,0},{1,2},{2,1},{4,7},{7,4},{5,6},{6,5},{8,11},{11,8},{9,1... | collective-permute-start | bytes 1572872 | tf_op jit(solution)/shard_map/mix/ppermute | solution.py:477
  61.7 21.1 %collective-permute-start.9 = (bf16[128,2048]{1,0:T(8,128)(2,1)S(1)}, bf16[128,2048]{1,0:T(8,128)(2,1)S(1)}, u32[]{:S(2)}, u32[]{:S(2)}) collective-permute-start(bf16[128,2048]{1,0:T(8,128)(2,1)S(1)} %mix.7.refs_0_.x_ref.t_ref), channel_id=1, source_target_pairs={{0,1},{1,0},{2,3},{3,2},{4,5},{5,4},{6,7},{7,6},{8,9},{9,8},{10,11... | collective-permute-start | bytes 1572872 | tf_op jit(solution)/shard_map/mix/ppermute | solution.py:480
  71.4 18.4 %collective-permute-start.10 = (bf16[128,2048]{1,0:T(8,128)(2,1)S(1)}, bf16[128,2048]{1,0:T(8,128)(2,1)S(1)}, u32[]{:S(2)}, u32[]{:S(2)}) collective-permute-start(bf16[128,2048]{1,0:T(8,128)(2,1)S(1)} %mix.5.x_ref.t_ref), channel_id=1, source_target_pairs={{0,1},{1,0},{2,3},{3,2},{4,5},{5,4},{6,7},{7,6},{8,9},{9,8},{10,11... | collective-permute-start | bytes 1572872 | tf_op jit(solution)/shard_map/mix/ppermute | solution.py:480
  81.0 1.8 %copy-start.1 = (bf16[256,1024]{1,0:T(8,128)(2,1)S(1)}, bf16[256,1024]{1,0:T(8,128)(2,1)}, u32[]{:S(2)}) copy-start(bf16[256,1024]{1,0:T(8,128)(2,1)} %get-tuple-element.20.after) | copy-start | bytes 1572868
  85.0 9.7 %collective-permute-start.11 = (bf16[2,128,1024]{2,1,0:T(8,128)(2,1)S(1)}, bf16[2,128,1024]{2,1,0:T(8,128)(2,1)S(1)}, u32[]{:S(2)}, u32[]{:S(2)}) collective-permute-start(bf16[2,128,1024]{2,1,0:T(8,128)(2,1)S(1)} %get-tuple-element.36.refs_7_), channel_id=1, source_target_pairs={{0,4},{4,8},{8,12},{12,16},{16,20},{20,24},{24,28},{28,0},{1,5},{5... | collective-permute-start | bytes 1572872 | tf_op jit(solution)/shard_map/project/ppermute | solution.py:504
  91.2 9.6 %collective-permute-start.12 = (bf16[2,128,1024]{2,1,0:T(8,128)(2,1)S(1)}, bf16[2,128,1024]{2,1,0:T(8,128)(2,1)S(1)}, u32[]{:S(2)}, u32[]{:S(2)}) collective-permute-start(bf16[2,128,1024]{2,1,0:T(8,128)(2,1)S(1)} %get-tuple-element.37.refs_8_), channel_id=1, source_target_pairs={{0,4},{4,8},{8,12},{12,16},{16,20},{20,24},{24,28},{28,0},{1,5},{5... | collective-permute-start | bytes 1572872 | tf_op jit(solution)/shard_map/project/ppermute | solution.py:504

commit v6 on v5

--- a/solution.py
+++ b/solution.py
@@ -13,7 +13,7 @@
 BF16 = jnp.bfloat16
 F32 = jnp.float32
 NEG = -1e30
-STREAMS = (1, 1)
+FIRST, ACROSS, OWN, LAST, TURN = (1, 1), (2, 1, 1), (2, 1, 1), (2, 1, 1), (2, 1, 1)
 
 PAIR = [(0, 1), (1, 0), (2, 3), (3, 2)]
 CROSS = [(0, 3), (3, 0), (1, 2), (2, 1)]
@@ -124,7 +124,7 @@
 ANYWHERE = pl.BlockSpec(memory_space=pl.ANY)
 
 
-def call(body, ins, outs, in_specs=None, scratch=(), vmem=8, flops=0, moved=0):
+def call(body, ins, outs, in_specs=None, scratch=(), vmem=8, flops=0, moved=0, cost=0):
     return pl.pallas_call(
         body,
         in_specs=in_specs or [ON_CHIP] * len(ins),
@@ -132,7 +132,7 @@
         out_shape=outs,
         scratch_shapes=scratch,
         compiler_params=pltpu.CompilerParams(vmem_limit_bytes=vmem * 2**20),
-        cost_estimate=pl.CostEstimate(flops=flops, bytes_accessed=moved, transcendentals=0),
+        cost_estimate=pl.CostEstimate(flops=cost, bytes_accessed=0, transcendentals=0),
     )(*ins)
 
 
@@ -230,10 +230,10 @@
 
 
 def mine_body(scale, cuts, *refs):
-    q_ref, intra_ref, own_ref, other_ref, w_other_ref, w_mine_ref, r_ref, w_qkv_ref = refs[:8]
+    q_ref, intra_ref, own_ref, other_ref, w_other_ref, w_mine_ref, r_ref, w_qkv_ref, after = refs[:9]
     count = len(cuts)
-    send_refs, mine_refs = refs[8 : 7 + count], refs[7 + count : 7 + 2 * count]
-    w_qkv_to_ref, lin_ref, sems = refs[7 + 2 * count :]
+    send_refs, mine_refs = refs[9 : 8 + count], refs[8 + count : 8 + 2 * count]
+    w_qkv_to_ref, lin_ref, sems = refs[8 + 2 * count :]
     z, mine, _ = quarters()
     width = w_mine_ref.shape[2]
     block = width // 2
@@ -267,38 +267,56 @@
         copy.wait()
 
 
-def add_body(a_ref, b_ref, o_ref):
-    o_ref[...] = (a_ref[...].astype(F32) + b_ref[...].astype(F32)).astype(BF16)
-
-
-def two_quarters(x_ref, w_ref, plane, which, to):
-    width = x_ref.shape[1] // 2
-    low = dot(x_ref[:, :width], w_ref[plane, at(which[0] * width, width), to])
-    return low + dot(x_ref[:, width:], w_ref[plane, at(which[1] * width, width), to])
-
-
-def first_body(block, x_ref, w_ref, acc_ref):
+def overlaps(groups, rows):
+    found = []
+    for i, (a, b) in enumerate(groups):
+        low, high = max(a, rows[0]), min(b, rows[1])
+        if low < high:
+            found.append((i, slice(low - a, high - a), slice(low - rows[0], high - rows[0])))
+    return found
+
+
+def add_body(places, *refs):
+    *refs, o_ref = refs
+    for i, (_, source, target) in enumerate(places):
+        total = refs[2 * i][source].astype(F32) + refs[2 * i + 1][source].astype(F32)
+        o_ref[target] = total.astype(BF16)
+
+
+def two_quarters(x, w_ref, plane, which, to):
+    width = x.shape[1] // 2
+    low = dot(x[:, :width], w_ref[plane, at(which[0] * width, width), to])
+    return low + dot(x[:, width:], w_ref[plane, at(which[1] * width, width), to])
+
+
+def joined(refs):
+    return refs[0] if len(refs) == 1 else jnp.concatenate([ref[...] for ref in refs], axis=0)
+
+
+def first_body(block, w_ref, *refs):
+    *x_refs, acc_ref = refs
     _, mine, _ = quarters()
+    x = joined(x_refs)
     for plane in range(3):
         for n in range(acc_ref.shape[2] // block):
             to = slice(n * block, (n + 1) * block)
-            acc_ref[plane, :, to] = two_quarters(x_ref, w_ref, plane, mine, to)
-
-
-def first_hidden_body(block, cuts, x_ref, w_ref, *refs):
-    total_refs, (acc_ref, hidden_ref) = refs[:-2], refs[-2:]
+            acc_ref[plane, :, to] = two_quarters(x, w_ref, plane, mine, to)
+
+
+def first_hidden_body(block, cuts, count, w_ref, *refs):
+    *total_refs, acc_ref, hidden_ref = refs
     width = acc_ref.shape[2]
     own = at((lax.axis_index("head") // 2) * width, width)
-    for (a, b), ref in zip(cuts, (*total_refs, x_ref)):
+    for (a, b), ref in zip(cuts, total_refs):
         hidden_ref[a:b] = ref[:, own]
-    first_body(block, x_ref, w_ref, acc_ref)
-
-
-def finish(block, plane, x_ref, w_ref, acc_ref, inv, cos, sin, out_ref):
+    first_body(block, w_ref, *total_refs[-count:], acc_ref)
+
+
+def finish(block, plane, x, w_ref, acc_ref, rows, inv, cos, sin, out_ref):
     _, _, other = quarters()
     for n in range(acc_ref.shape[2] // block):
         to = slice(n * block, (n + 1) * block)
-        total = (acc_ref[plane, :, to] + two_quarters(x_ref, w_ref, plane, other, to)) * inv
+        total = (acc_ref[plane, rows, to] + two_quarters(x, w_ref, plane, other, to)) * inv
         if plane == 2:
             out_ref[:, to] = total.astype(BF16)
             continue
@@ -308,16 +326,19 @@
             out_ref[:, n * block + h * HD : n * block + (h + 1) * HD] = turned.astype(BF16)
 
 
-def kv_body(block, rows, t_ref, x_ref, w_ref, acc_ref, cos_ref, sin_ref, after, kv_ref, rest_ref):
-    t = t_ref[...].astype(F32)
+def kv_body(block, rows, own, count, *refs):
+    t_refs, x_refs = refs[:count], refs[count : 2 * count]
+    w_ref, acc_ref, cos_ref, sin_ref, _, kv_ref, rest_ref = refs[2 * count :]
+    x_ref = joined(x_refs)
+    t = joined(t_refs)[...].astype(F32)
     x = x_ref[...].astype(F32)
     total = jnp.sum(t * t + x * x, axis=1, keepdims=True)
     inv = lax.rsqrt(total / D + 1e-05)
     cos, sin = cos_ref[slice(*rows)], sin_ref[slice(*rows)]
     for plane in (1, 2):
-        finish(block, plane, x_ref, w_ref, acc_ref, inv, cos, sin, kv_ref.at[plane - 1])
+        finish(block, plane, x_ref, w_ref, acc_ref, own, inv, cos, sin, kv_ref.at[plane - 1])
     if rest_ref.dtype == BF16:
-        finish(block, 0, x_ref, w_ref, acc_ref, inv, cos, sin, rest_ref)
+        finish(block, 0, x_ref, w_ref, acc_ref, own, inv, cos, sin, rest_ref)
     else:
         rest_ref[...] = jnp.broadcast_to(inv, rest_ref.shape)
 
@@ -329,18 +350,20 @@
     return jnp.concatenate([ref[where] for ref in refs], axis=0)
 
 
-def early_body(block, cuts, *refs):
-    count = len(cuts)
-    x_ref, w_ref, acc_in_ref, inv_ref, cos_ref, sin_ref = refs[:6]
-    q_refs, kv_refs = refs[6 : 5 + count], refs[5 + count : 5 + 2 * count]
-    prev_refs = refs[5 + 2 * count : 4 + 3 * count]
-    q_ref, acc_ref, top_ref, sum_ref = refs[4 + 3 * count :]
-    rows = slice(*cuts[-1])
-    finish(block, 0, x_ref, w_ref, acc_in_ref, inv_ref[:, :1], cos_ref[rows], sin_ref[rows], q_ref)
+def early_body(block, rows, before, q_count, x_count, inv_count, kv_count, *refs):
+    w_ref, acc_in_ref, cos_ref, sin_ref = refs[:4]
+    refs = refs[4:]
+    x_refs, refs = refs[:x_count], refs[x_count:]
+    inv_refs, refs = refs[:inv_count], refs[inv_count:]
+    q_refs, refs = refs[:q_count], refs[q_count:]
+    kv_refs, prev_refs = refs[:kv_count], refs[kv_count : 2 * kv_count - 1]
+    q_ref, acc_ref, top_ref, sum_ref = refs[2 * kv_count - 1 :]
+    inv = joined(inv_refs)[:, :1]
+    cos, sin = cos_ref[slice(*rows)], sin_ref[slice(*rows)]
+    finish(block, 0, joined(x_refs), w_ref, acc_in_ref, slice(None), inv, cos, sin, q_ref)
     q_refs = (*q_refs, q_ref)
     has_prev = lax.axis_index("seq") > 0
-    before = cuts[-1][0]
-    shape = (before + cuts[-1][1], cuts[-1][1])
+    shape = (before + rows[1], rows[1])
     key = lax.broadcasted_iota(jnp.int32, shape, 0)
     query = lax.broadcasted_iota(jnp.int32, shape, 1)
     allowed = ((key < before) & has_prev) | ((key >= before) & (key - before <= query))
@@ -379,7 +402,7 @@
         out_ref[:, at_head[h]] = total.T.astype(BF16)
 
 
-def tuned(streams, lin_qkv, resid, w_out, w_qkv):
+def tuned(lin_qkv, resid, w_out, w_qkv):
     rows, _, width = lin_qkv.shape
     nheads = width // HD
     group = nheads // 2
@@ -388,8 +411,12 @@
     seq = lax.axis_index("seq")
     core = seq % 2
     shape = jax.ShapeDtypeStruct
-    edges = [rows * sum(streams[:i]) // sum(streams) for i in range(len(streams) + 1)]
-    cuts = list(zip(edges, edges[1:]))
+
+    def shared(shares):
+        edges = [rows * sum(shares[:i]) // sum(shares) for i in range(len(shares) + 1)]
+        return list(zip(edges, edges[1:]))
+
+    cuts, across, owns, ends, turns = (shared(x) for x in (FIRST, ACROSS, OWN, LAST, TURN))
     sizes = [b - a for a, b in cuts]
     last = len(cuts) - 1
 
@@ -451,68 +478,93 @@
         )
         got = [lax.ppermute(first_send, "head", PAIR)]
         *made, w_here = call(
-            functools.partial(mine_body, scale, cuts), (*lin_inputs, w_mine, resid, in_hbm(wqkv)),
+            functools.partial(mine_body, scale, cuts), (*lin_inputs, w_mine, resid, in_hbm(wqkv), first_send),
             (*halves[1:], *halves, pltpu.VMEM(wqkv.shape, BF16)),
-            [ON_CHIP] * 7 + [IN_HBM], (lin_scratch, pltpu.SemaphoreType.DMA((3 * full // width,))),
+            [ON_CHIP] * 7 + [IN_HBM, ANYWHERE], (lin_scratch, pltpu.SemaphoreType.DMA((3 * full // width,))),
             flops=2 * rows * width * full, moved=6 * width * full,
         )
         sends, mines = made[:last], made[last:]
         w_here = in_vmem(w_here)
 
-    def add(a, b):
-        return call(add_body, (a, b), shape(a.shape, BF16), vmem=4, moved=3 * a.size)
+    def added(lefts, rights, groups, target, after=()):
+        places = overlaps(groups, target)
+        ins = [x for i, _, _ in places for x in (lefts[i], rights[i])]
+        out = shape((target[1] - target[0], full // 2), BF16)
+        specs = [ON_CHIP] * len(ins) + [ANYWHERE] * len(after)
+        return call(functools.partial(add_body, places), (*ins, *after), out, specs, vmem=4, moved=3 * out.size)
 
     with jax.named_scope("mix"):
-        totals, rests = [], []
-        far = None
-        for i in range(last + 1):
-            if i > 0:
-                ready = sends[i - 1]
-                got.append(lax.ppermute(ready, "head", PAIR))
-        for i in range(last + 1):
-            partial = add(mines[i], got[i])
-            if i > 0:
-                pass
-                totals.append(add(held, far))
-            far = lax.ppermute(partial, "head", CROSS)
-            held = partial
-        totals.append(add(held, far))
-        rests = [lax.ppermute(total, "head", PAIR) for total in totals]
-
-    queries, kvs, prevs, accs = [], [], [], []
-    cost = dict(flops=rows * full * 3 * width, moved=3 * width * full)
+        got += [lax.ppermute(send, "head", PAIR) for send in sends]
+        sums, far = [], []
+        for i, group in enumerate(across):
+            part = added(mines, got, cuts, group, sums[-1:])
+            for j in {2: (1,)}.get(i, ()):
+                part, far[j] = lax.optimization_barrier((part, far[j]))
+            sums.append(part)
+            far.append(lax.ppermute(part, "head", CROSS))
+
+    def inside(group):
+        return [i for i, (a, b) in enumerate(ends) if group[0] <= a and b <= group[1]]
+
+    totals, rests, accs = [], [], []
+    queries, invs, kvs, prevs = [], [], [], []
+    ring = [(i, (i + 1) % lax.axis_size("seq")) for i in range(lax.axis_size("seq"))]
+
+    def turn(group):
+        members = inside(group)
+        (k, own, _), = overlaps(owns, group)
+        n = group[1] - group[0]
+        tail = k == len(owns) - 1
+        kv, other = call(
+            functools.partial(kv_body, block, group, own, len(members)),
+            (*(totals[i] for i in members), *(rests[i] for i in members), w_here, accs[k], cos2, sin2, accs[-1]),
+            (shape((2, n, width), BF16), shape((n, HD), F32) if tail else shape((n, width), BF16)),
+            [ON_CHIP] * (2 * len(members) + 4) + [ANYWHERE],
+        )
+        kvs.append(kv)
+        (invs if tail else queries).append(other)
+        prevs.append(lax.ppermute(kv, "seq", ring))
+
+    for k, group in enumerate(owns):
+        members = inside(group)
+        before = totals[-1:]
+        if k == len(owns) - 1:
+            with jax.named_scope("project"):
+                for early in turns:
+                    if early[1] <= owns[0][1]:
+                        turn(early)
+            before = kvs[-1:] and before
+        with jax.named_scope("mix"):
+            for i in members:
+                totals.append(added(sums, far, across, ends[i], before))
+            rests += [lax.ppermute(totals[i], "head", PAIR) for i in members]
+        with jax.named_scope("project"):
+            acc = shape((3, group[1] - group[0], width), F32)
+            if k < len(owns) - 1:
+                inputs = [totals[i] for i in members]
+                accs.append(call(functools.partial(first_body, block), (w_here, *inputs), acc))
+                continue
+            acc, hidden = call(
+                functools.partial(first_hidden_body, block, ends, len(members)), (w_here, *totals),
+                (acc, shape((rows, width), BF16)),
+            )
+            accs.append(acc)
     with jax.named_scope("project"):
-        for i in range(last):
-            acc = shape((3, sizes[i], width), F32)
-            accs.append(call(functools.partial(first_body, block), (totals[i], w_here), acc, **cost))
-        acc, hidden = call(
-            functools.partial(first_hidden_body, block, cuts), (totals[last], w_here, *totals[:last]),
-            (shape((3, sizes[last], width), F32), shape((rows, width), BF16)), **cost,
-        )
-        accs.append(acc)
-    for i in range(last + 1):
-        n = sizes[i]
-        with jax.named_scope("project"):
-            kv, other = call(
-                functools.partial(kv_body, block, cuts[i]),
-                (totals[i], rests[i], w_here, accs[i], cos2, sin2, hidden),
-                (shape((2, n, width), BF16), shape((n, width), BF16) if i < last else shape((n, HD), F32)),
-                [ON_CHIP] * 6 + [ANYWHERE], **cost,
-            )
-            kvs.append(kv)
-            queries.append(other)
-            prevs.append(lax.ppermute(kv, "seq", [(i, (i + 1) % 8) for i in range(8)]))
+        for group in turns[len(kvs) :]:
+            turn(group)
     with jax.named_scope("attend"):
-        inv = queries.pop()
         stat = shape((nheads, rows), F32)
+        tail = owns[-1]
+        members = [rests[i] for i in inside(tail)]
         query, acc, top, total = call(
-            functools.partial(early_body, block, cuts),
-            (rests[last], w_here, acc, inv, cos2, sin2, *queries, *kvs, *prevs[:last]),
-            (shape((sizes[last], width), BF16), shape((nheads, HD, rows), F32), stat, stat),
+            functools.partial(early_body, block, tail, turns[-1][0], len(queries), len(members), len(invs), len(kvs)),
+            (w_here, accs[-1], cos2, sin2, *members, *invs, *queries, *kvs, *prevs[:-1]),
+            (shape((tail[1] - tail[0], width), BF16), shape((nheads, HD, rows), F32), stat, stat),
             flops=8 * rows * rows * width, moved=12 * rows * width,
         )
+        queries.append(query)
         attended = call(
-            functools.partial(late_body, last + 1), (*queries, query, prevs[last], acc, top, total),
+            functools.partial(late_body, len(queries)), (*queries, prevs[-1], acc, top, total),
             shape((rows, width), BF16), flops=2 * rows * rows * width, moved=12 * rows * width,
         )
     return hidden, attended
@@ -521,7 +573,7 @@
 def solution(mesh):
     line = mesh.shape["seq"] == 8 and mesh.shape["head"] == 4
     return jax.shard_map(
-        functools.partial(tuned, STREAMS) if line else general,
+        tuned if line else general,
         mesh=mesh,
         in_specs=(P("seq", None, "head"), P("seq", "head"), P("head", None), P(None, None, "head")),
         out_specs=(P("seq", "head"), P("seq", "head")),

time: 104 us -> 101 us (0.971)
  waiting for transfers between devices: 32.8 us -> 25.7 us
  Pallas kernels: 29.4 us -> 34.9 us
  starting transfers between devices: 38.6 us -> 36.7 us
    ppermute x7 -> x10, waiting for transfers between devices: 25.6 us -> 18.2 us  [the longest x1 6.63 us: tuned(): got += [lax.ppermute(send, 'head', PAIR) for send in sends]]
    pallas_call x14 -> x18, Pallas kernels: 29.4 us -> 34.9 us  [call(): pl.pallas_call(body, in_specs=in_specs or [ON_CHIP] * len(ins), out_specs...]
    ppermute x7 -> x10, starting transfers between devices: 33.2 us -> 31.4 us  [the longest x3 25.1 us: tuned(): far.append(lax.ppermute(part, 'head', CROSS))]
  transfers between devices with their start and end apart: 13 -> 16, of which waited for: 9 -> 9; matrix products, arithmetic and copies ran while one was open for 1% -> 1% of each run, Pallas kernels for 24% -> 31%
where the time goes in v6:
time: 101 us; the launch traced here: 99.1 us
  starting transfers between devices  36.7 us (36%)
  Pallas kernels  34.9 us (35%)
  waiting for transfers between devices  25.7 us (25%)
    pallas_call x18, Pallas kernels, call(): pl.pallas_call(body, in_specs=in_specs or [ON_CHIP] * len(ins), out_specs...  34.9 us
    ppermute x3, starting transfers between devices, tuned(): far.append(lax.ppermute(part, 'head', CROSS))  25.1 us
    ppermute x1, waiting for transfers between devices, tuned(): got += [lax.ppermute(send, 'head', PAIR) for send in sends]  6.63 us
    ppermute x3, waiting for transfers between devices, tuned(): far.append(lax.ppermute(part, 'head', CROSS))  6.01 us
    ppermute x3, starting transfers between devices, tuned(): rests += [lax.ppermute(totals[i], 'head', PAIR) for i in members]  5.22 us
    ppermute x1, waiting for transfers between devices, tuned(): got = [lax.ppermute(first_send, 'head', PAIR)]  4 us
    ppermute x5, starting transfers between devices, swapped(): lax.ppermute(array, axis, [(i, i ^ bits) for i in range(lax.axis_size(axi...  3.7 us
    ppermute x5, waiting for transfers between devices, swapped(): lax.ppermute(array, axis, [(i, i ^ bits) for i in range(lax.axis_size(axi...  3.52 us
  transfers between devices with their start and end apart: 16, of which 9 were waited for; matrix products, arithmetic and copies ran while one was open for 1% of the time, Pallas kernels for 31%

profile of v6, /device:TPU:4, one launch (start us, length us, event | category | flops | bytes accessed | tf_op | source)
XLA Modules:
  0.0 99.1 jit_solution(13275068872930817941)
XLA Ops:
  0.6 1.7 %state.1 = (bf16[4,128,128]{2,1,0:T(8,128)(2,1)S(1)}, bf16[4,128,128]{2,1,0:T(8,128)(2,1)S(1)}) custom-call(bf16[3,256,1024]{2,1,0:T(8,128)(2,1)} %bitcast.2), custom_call_target="tpu_custom_call" | custom-call | tf_op jit(solution)/shard_map/state/pallas_call | solution.py:128
  2.4 0.1 collective-permute-start
  2.5 1.3 %collective-permute-done = bf16[4,128,128]{2,1,0:T(8,128)(2,1)S(1)} collective-permute-done((bf16[4,128,128]{2,1,0:T(8,128)(2,1)S(1)}, bf16[4,128,128]{2,1,0:T(8,128)(2,1)S(1)}, u32[]{:S(2)}, u32[]{:S(2)}) %collective-permute-start) | collective-permute-done | bytes 131104 | tf_op jit(solution)/shard_map/state/ppermute | solution.py:29
  3.8 1.6 %collective-permute-start.1 = (bf16[4,128,128]{2,1,0:T(8,128)(2,1)S(1)}, bf16[4,128,128]{2,1,0:T(8,128)(2,1)S(1)}, u32[]{:S(2)}, u32[]{:S(2)}) collective-permute-start(bf16[4,128,128]{2,1,0:T(8,128)(2,1)S(1)} %add_convert_fusion.1.after), channel_id=1, source_target_pairs={{0,8},{4,12},{8,0},{12,4},{16,24},{20,28},{24,16},{28,20},{1,9},{5... | collective-permute-start | bytes 393224 | tf_op jit(solution)/shard_map/state/ppermute | solution.py:29
  5.4 0.5 collective-permute-start.2
  5.9 1.5 %collective-permute-start.3 = (bf16[4,128,128]{2,1,0:T(8,128)(2,1)S(1)}, bf16[4,128,128]{2,1,0:T(8,128)(2,1)S(1)}, u32[]{:S(2)}, u32[]{:S(2)}) collective-permute-start(bf16[4,128,128]{2,1,0:T(8,128)(2,1)S(1)} %add_convert_fusion.1.after), channel_id=1, source_target_pairs={{0,24},{4,28},{8,16},{12,20},{16,8},{20,12},{24,0},{28,4},{1,25},{... | collective-permute-start | bytes 393224 | tf_op jit(solution)/shard_map/state/ppermute | solution.py:29
  7.4 0.5 fusion.1
  8.0 0.1 pad_maximum_fusion
  8.1 4.4 %intra.1 = (f32[256,1024]{1,0:T(8,128)S(1)}, bf16[256,1024]{1,0:T(8,128)(2,1)S(1)}, bf16[2,1024,1024]{2,1,0:T(8,128)(2,1)S(1)}, bf16[2,1024,1024]{2,1,0:T(8,128)(2,1)S(1)}) custom-call(bf16[3,256,1024]{2,1,0:T(8,128)(2,1)S(1)} %bitcast.3, bf16[4,128,128]{2,1,0:T(8,128)(2,1)S(1)} %add_convert_fusion.1.after, ...), custom_call_target="tpu_custom_call" | custom-call | tf_op jit(solution)/shard_map/intra/pallas_call | solution.py:128
  12.6 0.0 copy-start.1
  12.6 0.0 collective-permute-done.1
  12.6 0.9 collective-permute-done.2
  13.5 0.1 broadcast_select_fusion
  13.6 0.1 collective-permute-start.4
  13.7 1.3 %collective-permute-done.4.other_ref.refs_3_ = bf16[4,128,128]{2,1,0:T(8,128)(2,1)S(1)} collective-permute-done((bf16[4,128,128]{2,1,0:T(8,128)(2,1)S(1)}, bf16[4,128,128]{2,1,0:T(8,128)(2,1)S(1)}, u32[]{:S(2)}, u32[]{:S(2)}) %collective-permute-start.4) | collective-permute-done | bytes 131104 | tf_op jit(solution)/shard_map/prefix/ppermute | solution.py:29
  15.0 0.9 partials.2.refs_8_
  16.0 1.6 %collective-permute-start.5 = (bf16[128,2048]{1,0:T(8,128)(2,1)S(1)}, bf16[128,2048]{1,0:T(8,128)(2,1)S(1)}, u32[]{:S(2)}, u32[]{:S(2)}) collective-permute-start(bf16[128,2048]{1,0:T(8,128)(2,1)S(1)} %partials.2.refs_8_), channel_id=1, source_target_pairs={{0,1},{1,0},{2,3},{3,2},{4,5},{5,4},{6,7},{7,6},{8,9},{9,8},{10,11... | collective-permute-start | bytes 1572872 | tf_op jit(solution)/shard_map/partials/ppermute | solution.py:479
  17.6 8.7 %partials.3 = (bf16[128,2048]{1,0:T(8,128)(2,1)S(1)}, bf16[128,2048]{1,0:T(8,128)(2,1)S(1)}, bf16[128,2048]{1,0:T(8,128)(2,1)S(1)}, bf16[3,4096,1024]{2,1,0:T(8,128)(2,1)S(1)}) custom-call(bf16[256,1024]{1,0:T(8,128)(2,1)S(1)} %get-tuple-element.28.q_ref.refs_0_, f32[256,1024]{1,0:T(8,128)S(1)} %get-tuple-element.29.intra_ref.refs_1_, ...), custom_call_target="tpu_custom_call" | custom-call | tf_op jit(solution)/shard_map/partials/pallas_call | solution.py:128
  26.3 0.5 collective-permute-start.7
  26.8 4.0 %collective-permute-done.5.refs_1_ = bf16[128,2048]{1,0:T(8,128)(2,1)S(1)} collective-permute-done((bf16[128,2048]{1,0:T(8,128)(2,1)S(1)}, bf16[128,2048]{1,0:T(8,128)(2,1)S(1)}, u32[]{:S(2)}, u32[]{:S(2)}) %collective-permute-start.5) | collective-permute-done | bytes 524320 | tf_op jit(solution)/shard_map/partials/ppermute | solution.py:479
  30.8 0.1 mix.6.refs_0_.refs_2_
  30.9 3.7 %collective-permute-start.6 = (bf16[128,2048]{1,0:T(8,128)(2,1)S(1)}, bf16[128,2048]{1,0:T(8,128)(2,1)S(1)}, u32[]{:S(2)}, u32[]{:S(2)}) collective-permute-start(bf16[128,2048]{1,0:T(8,128)(2,1)S(1)} %mix.6.refs_0_.refs_2_), channel_id=1, source_target_pairs={{0,3},{3,0},{1,2},{2,1},{4,7},{7,4},{5,6},{6,5},{8,11},{11,8},{9,1... | collective-permute-start | bytes 1572872 | tf_op jit(solution)/shard_map/mix/ppermute | solution.py:504
  34.6 6.6 %collective-permute-done.7.refs_1_ = bf16[128,2048]{1,0:T(8,128)(2,1)S(1)} collective-permute-done((bf16[128,2048]{1,0:T(8,128)(2,1)S(1)}, bf16[128,2048]{1,0:T(8,128)(2,1)S(1)}, u32[]{:S(2)}, u32[]{:S(2)}) %collective-permute-start.7) | collective-permute-done | bytes 524320 | tf_op jit(solution)/shard_map/mix/ppermute | solution.py:497
  41.2 0.1 mix.8.refs_2_.refs_0_
  41.3 17.7 %collective-permute-start.8 = (bf16[64,2048]{1,0:T(8,128)(2,1)S(1)}, bf16[64,2048]{1,0:T(8,128)(2,1)S(1)}, u32[]{:S(2)}, u32[]{:S(2)}) collective-permute-start(bf16[64,2048]{1,0:T(8,128)(2,1)S(1)} %mix.8.refs_2_.refs_0_), channel_id=1, source_target_pairs={{0,3},{3,0},{1,2},{2,1},{4,7},{7,4},{5,6},{6,5},{8,11},{11,8},{9,1... | collective-permute-start | bytes 786440 | tf_op jit(solution)/shard_map/mix/ppermute | solution.py:504
  59.0 0.1 mix.7.refs_2_.refs_0_
  59.2 1.2 %collective-permute-start.10 = (bf16[128,2048]{1,0:T(8,128)(2,1)S(1)}, bf16[128,2048]{1,0:T(8,128)(2,1)S(1)}, u32[]{:S(2)}, u32[]{:S(2)}) collective-permute-start(bf16[128,2048]{1,0:T(8,128)(2,1)S(1)} %mix.7.refs_2_.refs_0_), channel_id=1, source_target_pairs={{0,1},{1,0},{2,3},{3,2},{4,5},{5,4},{6,7},{7,6},{8,9},{9,8},{10,11... | collective-permute-start | bytes 1572872 | tf_op jit(solution)/shard_map/mix/ppermute | solution.py:540
  60.3 0.1 mix.9.refs_0_
  60.4 6.0 %collective-permute-done.8.refs_1_ = bf16[64,2048]{1,0:T(8,128)(2,1)S(1)} collective-permute-done((bf16[64,2048]{1,0:T(8,128)(2,1)S(1)}, bf16[64,2048]{1,0:T(8,128)(2,1)S(1)}, u32[]{:S(2)}, u32[]{:S(2)}) %collective-permute-start.8) | collective-permute-done | bytes 262176 | tf_op jit(solution)/shard_map/mix/ppermute | solution.py:504
  66.4 3.7 %collective-permute-start.9 = (bf16[64,2048]{1,0:T(8,128)(2,1)S(1)}, bf16[64,2048]{1,0:T(8,128)(2,1)S(1)}, u32[]{:S(2)}, u32[]{:S(2)}) collective-permute-start(bf16[64,2048]{1,0:T(8,128)(2,1)S(1)} %mix.9.refs_0_), channel_id=1, source_target_pairs={{0,3},{3,0},{1,2},{2,1},{4,7},{7,4},{5,6},{6,5},{8,11},{11,8},{9,1... | collective-permute-start | bytes 786440 | tf_op jit(solution)/shard_map/mix/ppermute | solution.py:504
  70.1 0.1 mix.10.refs_2_.refs_1_.refs_0_
  70.2 3.4 %collective-permute-start.11 = (bf16[64,2048]{1,0:T(8,128)(2,1)S(1)}, bf16[64,2048]{1,0:T(8,128)(2,1)S(1)}, u32[]{:S(2)}, u32[]{:S(2)}) collective-permute-start(bf16[64,2048]{1,0:T(8,128)(2,1)S(1)} %mix.10.refs_2_.refs_1_.refs_0_), channel_id=1, source_target_pairs={{0,1},{1,0},{2,3},{3,2},{4,5},{5,4},{6,7},{7,6},{8,9},{9,8},{10,11... | collective-permute-start | bytes 786440 | tf_op jit(solution)/shard_map/mix/ppermute | solution.py:540
  73.6 2.3 %project.8.refs_6_.refs_3_ = f32[3,64,1024]{2,1,0:T(8,128)S(1)} custom-call(bf16[3,4096,1024]{2,1,0:T(8,128)(2,1)S(1)} %get-tuple-element.32.w_ref.refs_2_.refs_0_, bf16[64,2048]{1,0:T(8,128)(2,1)S(1)} %mix.10.refs_2_.refs_1_.refs_0_), custom_call_target="tpu_custom_call" | custom-call | tf_op jit(solution)/shard_map/project/pallas_call | solution.py:128
  76.0 1.8 %project.7.refs_3_ = f32[3,128,1024]{2,1,0:T(8,128)S(1)} custom-call(bf16[3,4096,1024]{2,1,0:T(8,128)(2,1)S(1)} %get-tuple-element.32.w_ref.refs_2_.refs_0_, bf16[128,2048]{1,0:T(8,128)(2,1)S(1)} %mix.7.refs_2_.refs_0_), custom_call_target="tpu_custom_call" | custom-call | tf_op jit(solution)/shard_map/project/pallas_call | solution.py:128
  77.8 2.1 %project.9 = (bf16[2,128,1024]{2,1,0:T(8,128)(2,1)S(1)}, bf16[128,1024]{1,0:T(8,128)(2,1)S(1)}) custom-call(bf16[128,2048]{1,0:T(8,128)(2,1)S(1)} %mix.7.refs_2_.refs_0_, bf16[128,2048]{1,0:T(8,128)(2,1)S(1)} %collective-permute-done.10.refs_1_, bf16[3,4096,1024]{2,1,0:T(8,128)(2,1)S(1)} %get-tuple-element.32.w_ref.refs_2_.refs_0_, ...), custom_call_target="tpu_custom_call" | custom-call | tf_op jit(solution)/shard_map/project/pallas_call | solution.py:128
  79.9 0.2 collective-permute-start.13
  80.1 0.1 mix.11.refs_2_.refs_0_
  80.2 0.6 collective-permute-start.12
  80.8 3.0 %project.6 = (f32[3,64,1024]{2,1,0:T(8,128)S(1)}, bf16[256,1024]{1,0:T(8,128)(2,1)}) custom-call(bf16[3,4096,1024]{2,1,0:T(8,128)(2,1)S(1)} %get-tuple-element.32.w_ref.refs_2_.refs_0_, bf16[128,2048]{1,0:T(8,128)(2,1)S(1)} %mix.7.refs_2_.refs_0_, bf16[64,2048]{1,0:T(8,128)(2,1)S(1)} %mix.10.refs_2_.refs_1_.refs_0_, bf16[64,2048]{1,0:T(8,128)(2,1)S(1)} %mix.11.refs_2_.refs_0_), custom_call_target="tpu_custom_call" | custom-call | tf_op jit(solution)/shard_map/project/pallas_call | solution.py:128
  83.8 2.4 %project.10 = (bf16[2,64,1024]{2,1,0:T(8,128)(2,1)S(1)}, bf16[64,1024]{1,0:T(8,128)(2,1)S(1)}) custom-call(bf16[64,2048]{1,0:T(8,128)(2,1)S(1)} %mix.10.refs_2_.refs_1_.refs_0_, bf16[64,2048]{1,0:T(8,128)(2,1)S(1)} %collective-permute-done.11.refs_1_, bf16[3,4096,1024]{2,1,0:T(8,128)(2,1)S(1)} %get-tuple-element.32.w_ref.refs_2_.refs_0_, ...), custom_call_target="tpu_custom_call" | custom-call | tf_op jit(solution)/shard_map/project/pallas_call | solution.py:128
  86.2 0.2 collective-permute-start.14
  86.4 2.7 %collective-permute-done.12.refs_1_.refs_4_ = bf16[64,2048]{1,0:T(8,128)(2,1)S(1)} collective-permute-done((bf16[64,2048]{1,0:T(8,128)(2,1)S(1)}, bf16[64,2048]{1,0:T(8,128)(2,1)S(1)}, u32[]{:S(2)}, u32[]{:S(2)}) %collective-permute-start.12) | collective-permute-done | bytes 262176 | tf_op jit(solution)/shard_map/mix/ppermute | solution.py:540
  89.2 1.6 %project.11 = (bf16[2,64,1024]{2,1,0:T(8,128)(2,1)S(1)}, f32[64,128]{1,0:T(8,128)S(1)}) custom-call(bf16[64,2048]{1,0:T(8,128)(2,1)S(1)} %mix.11.refs_2_.refs_0_, bf16[64,2048]{1,0:T(8,128)(2,1)S(1)} %collective-permute-done.12.refs_1_.refs_4_, bf16[3,4096,1024]{2,1,0:T(8,128)(2,1)S(1)} %get-tuple-element.32.w_ref.refs_2_.refs_0_, ...), custom_call_target="tpu_custom_call" | custom-call | tf_op jit(solution)/shard_map/project/pallas_call | solution.py:128
  90.8 0.1 collective-permute-start.15
  90.8 2.1 %collective-permute-done.14.refs_12_ = bf16[2,64,1024]{2,1,0:T(8,128)(2,1)S(1)} collective-permute-done((bf16[2,64,1024]{2,1,0:T(8,128)(2,1)S(1)}, bf16[2,64,1024]{2,1,0:T(8,128)(2,1)S(1)}, u32[]{:S(2)}, u32[]{:S(2)}) %collective-permute-start.14) | collective-permute-done | bytes 262176 | tf_op jit(solution)/shard_map/project/ppermute | solution.py:526
  93.0 3.9 %attend.2 = (bf16[64,1024]{1,0:T(8,128)(2,1)S(1)}, f32[8,128,256]{2,1,0:T(8,128)S(1)}, f32[8,256]{1,0:T(8,128)S(1)}, f32[8,256]{1,0:T(8,128)S(1)}) custom-call(bf16[3,4096,1024]{2,1,0:T(8,128)(2,1)S(1)} %get-tuple-element.32.w_ref.refs_2_.refs_0_, f32[3,64,1024]{2,1,0:T(8,128)S(1)} %get-tuple-element.40.refs_6_.refs_3_.refs_1_, ...), custom_call_target="tpu_custom_call" | custom-call | tf_op jit(solution)/shard_map/attend/pallas_call | solution.py:128
  96.8 0.7 collective-permute-done.15.refs_3_
  97.5 1.6 %attend.3 = bf16[256,1024]{1,0:T(8,128)(2,1)} custom-call(bf16[128,1024]{1,0:T(8,128)(2,1)S(1)} %get-tuple-element.39.refs_6_.refs_0_, bf16[64,1024]{1,0:T(8,128)(2,1)S(1)} %get-tuple-element.41.refs_7_.refs_1_, bf16[64,1024]{1,0:T(8,128)(2,1)S(1)} %get-tuple-element.46.refs_2_, bf16[2,64,1024]{2,1,0:T(8,128)(2,1)S(1)} %collective-permute-done.15.refs_3_, ...), custom_call_target="tpu_custom_call" | custom-call | tf_op jit(solution)/shard_map/attend/pallas_call | solution.py:128
  (13 shorter events, 0.1 us)
Async XLA Ops:
  0.6 7.5 %copy-start = (bf16[256,3,1024]{2,0,1:T(8,128)(2,1)S(1)}, bf16[256,3,1024]{2,0,1:T(8,128)(2,1)}, u32[]{:S(2)}) copy-start(bf16[256,3,1024]{2,0,1:T(8,128)(2,1)} %param.4) | copy-start | bytes 4718596
  2.4 1.4 %collective-permute-start = (bf16[4,128,128]{2,1,0:T(8,128)(2,1)S(1)}, bf16[4,128,128]{2,1,0:T(8,128)(2,1)S(1)}, u32[]{:S(2)}, u32[]{:S(2)}) collective-permute-start(bf16[4,128,128]{2,1,0:T(8,128)(2,1)S(1)} %get-tuple-element.27), channel_id=1, source_target_pairs={{0,4},{4,0},{8,12},{12,8},{16,20},{20,16},{24,28},{28,24},{1,5},{5... | collective-permute-start | bytes 393224 | tf_op jit(solution)/shard_map/state/ppermute | solution.py:29
  3.8 8.7 %collective-permute-start.1 = (bf16[4,128,128]{2,1,0:T(8,128)(2,1)S(1)}, bf16[4,128,128]{2,1,0:T(8,128)(2,1)S(1)}, u32[]{:S(2)}, u32[]{:S(2)}) collective-permute-start(bf16[4,128,128]{2,1,0:T(8,128)(2,1)S(1)} %add_convert_fusion.1.after), channel_id=1, source_target_pairs={{0,8},{4,12},{8,0},{12,4},{16,24},{20,28},{24,16},{28,20},{1,9},{5... | collective-permute-start | bytes 393224 | tf_op jit(solution)/shard_map/state/ppermute | solution.py:29
  5.4 8.1 %collective-permute-start.2 = (bf16[4,128,128]{2,1,0:T(8,128)(2,1)S(1)}, bf16[4,128,128]{2,1,0:T(8,128)(2,1)S(1)}, u32[]{:S(2)}, u32[]{:S(2)}) collective-permute-start(bf16[4,128,128]{2,1,0:T(8,128)(2,1)S(1)} %add_convert_fusion.1.after), channel_id=1, source_target_pairs={{0,16},{4,20},{8,24},{12,28},{16,0},{20,4},{24,8},{28,12},{1,17},{... | collective-permute-start | bytes 393224 | tf_op jit(solution)/shard_map/state/ppermute | solution.py:29
  5.9 7.6 %collective-permute-start.3 = (bf16[4,128,128]{2,1,0:T(8,128)(2,1)S(1)}, bf16[4,128,128]{2,1,0:T(8,128)(2,1)S(1)}, u32[]{:S(2)}, u32[]{:S(2)}) collective-permute-start(bf16[4,128,128]{2,1,0:T(8,128)(2,1)S(1)} %add_convert_fusion.1.after), channel_id=1, source_target_pairs={{0,24},{4,28},{8,16},{12,20},{16,8},{20,12},{24,0},{28,4},{1,25},{... | collective-permute-start | bytes 393224 | tf_op jit(solution)/shard_map/state/ppermute | solution.py:29
  12.6 5.1 %copy-start.1 = (bf16[256,1024]{1,0:T(8,128)(2,1)S(1)}, bf16[256,1024]{1,0:T(8,128)(2,1)}, u32[]{:S(2)}) copy-start(bf16[256,1024]{1,0:T(8,128)(2,1)} %refs_6_.1) | copy-start | bytes 1572868
  13.6 1.4 %collective-permute-start.4 = (bf16[4,128,128]{2,1,0:T(8,128)(2,1)S(1)}, bf16[4,128,128]{2,1,0:T(8,128)(2,1)S(1)}, u32[]{:S(2)}, u32[]{:S(2)}) collective-permute-start(bf16[4,128,128]{2,1,0:T(8,128)(2,1)S(1)} %get-tuple-element.50), channel_id=1, source_target_pairs={{0,4},{4,0},{8,12},{12,8},{16,20},{20,16},{24,28},{28,24},{1,5},{5... | collective-permute-start | bytes 393224 | tf_op jit(solution)/shard_map/prefix/ppermute | solution.py:29
  16.0 14.8 %collective-permute-start.5 = (bf16[128,2048]{1,0:T(8,128)(2,1)S(1)}, bf16[128,2048]{1,0:T(8,128)(2,1)S(1)}, u32[]{:S(2)}, u32[]{:S(2)}) collective-permute-start(bf16[128,2048]{1,0:T(8,128)(2,1)S(1)} %partials.2.refs_8_), channel_id=1, source_target_pairs={{0,1},{1,0},{2,3},{3,2},{4,5},{5,4},{6,7},{7,6},{8,9},{9,8},{10,11... | collective-permute-start | bytes 1572872 | tf_op jit(solution)/shard_map/partials/ppermute | solution.py:479
  26.3 15.0 %collective-permute-start.7 = (bf16[128,2048]{1,0:T(8,128)(2,1)S(1)}, bf16[128,2048]{1,0:T(8,128)(2,1)S(1)}, u32[]{:S(2)}, u32[]{:S(2)}) collective-permute-start(bf16[128,2048]{1,0:T(8,128)(2,1)S(1)} %get-tuple-element.35), channel_id=1, source_target_pairs={{0,1},{1,0},{2,3},{3,2},{4,5},{5,4},{6,7},{7,6},{8,9},{9,8},{10,11... | collective-permute-start | bytes 1572872 | tf_op jit(solution)/shard_map/mix/ppermute | solution.py:497
  30.9 28.1 %collective-permute-start.6 = (bf16[128,2048]{1,0:T(8,128)(2,1)S(1)}, bf16[128,2048]{1,0:T(8,128)(2,1)S(1)}, u32[]{:S(2)}, u32[]{:S(2)}) collective-permute-start(bf16[128,2048]{1,0:T(8,128)(2,1)S(1)} %mix.6.refs_0_.refs_2_), channel_id=1, source_target_pairs={{0,3},{3,0},{1,2},{2,1},{4,7},{7,4},{5,6},{6,5},{8,11},{11,8},{9,1... | collective-permute-start | bytes 1572872 | tf_op jit(solution)/shard_map/mix/ppermute | solution.py:504
  41.3 25.1 %collective-permute-start.8 = (bf16[64,2048]{1,0:T(8,128)(2,1)S(1)}, bf16[64,2048]{1,0:T(8,128)(2,1)S(1)}, u32[]{:S(2)}, u32[]{:S(2)}) collective-permute-start(bf16[64,2048]{1,0:T(8,128)(2,1)S(1)} %mix.8.refs_2_.refs_0_), channel_id=1, source_target_pairs={{0,3},{3,0},{1,2},{2,1},{4,7},{7,4},{5,6},{6,5},{8,11},{11,8},{9,1... | collective-permute-start | bytes 786440 | tf_op jit(solution)/shard_map/mix/ppermute | solution.py:504
  59.2 18.6 %collective-permute-start.10 = (bf16[128,2048]{1,0:T(8,128)(2,1)S(1)}, bf16[128,2048]{1,0:T(8,128)(2,1)S(1)}, u32[]{:S(2)}, u32[]{:S(2)}) collective-permute-start(bf16[128,2048]{1,0:T(8,128)(2,1)S(1)} %mix.7.refs_2_.refs_0_), channel_id=1, source_target_pairs={{0,1},{1,0},{2,3},{3,2},{4,5},{5,4},{6,7},{7,6},{8,9},{9,8},{10,11... | collective-permute-start | bytes 1572872 | tf_op jit(solution)/shard_map/mix/ppermute | solution.py:540
  66.4 13.7 %collective-permute-start.9 = (bf16[64,2048]{1,0:T(8,128)(2,1)S(1)}, bf16[64,2048]{1,0:T(8,128)(2,1)S(1)}, u32[]{:S(2)}, u32[]{:S(2)}) collective-permute-start(bf16[64,2048]{1,0:T(8,128)(2,1)S(1)} %mix.9.refs_0_), channel_id=1, source_target_pairs={{0,3},{3,0},{1,2},{2,1},{4,7},{7,4},{5,6},{6,5},{8,11},{11,8},{9,1... | collective-permute-start | bytes 786440 | tf_op jit(solution)/shard_map/mix/ppermute | solution.py:504
  70.2 13.6 %collective-permute-start.11 = (bf16[64,2048]{1,0:T(8,128)(2,1)S(1)}, bf16[64,2048]{1,0:T(8,128)(2,1)S(1)}, u32[]{:S(2)}, u32[]{:S(2)}) collective-permute-start(bf16[64,2048]{1,0:T(8,128)(2,1)S(1)} %mix.10.refs_2_.refs_1_.refs_0_), channel_id=1, source_target_pairs={{0,1},{1,0},{2,3},{3,2},{4,5},{5,4},{6,7},{7,6},{8,9},{9,8},{10,11... | collective-permute-start | bytes 786440 | tf_op jit(solution)/shard_map/mix/ppermute | solution.py:540
  79.9 13.1 %collective-permute-start.13 = (bf16[2,128,1024]{2,1,0:T(8,128)(2,1)S(1)}, bf16[2,128,1024]{2,1,0:T(8,128)(2,1)S(1)}, u32[]{:S(2)}, u32[]{:S(2)}) collective-permute-start(bf16[2,128,1024]{2,1,0:T(8,128)(2,1)S(1)} %get-tuple-element.43.refs_8_), channel_id=1, source_target_pairs={{0,4},{4,8},{8,12},{12,16},{16,20},{20,24},{24,28},{28,0},{1,5},{5... | collective-permute-start | bytes 1572872 | tf_op jit(solution)/shard_map/project/ppermute | solution.py:526
  80.2 9.0 %collective-permute-start.12 = (bf16[64,2048]{1,0:T(8,128)(2,1)S(1)}, bf16[64,2048]{1,0:T(8,128)(2,1)S(1)}, u32[]{:S(2)}, u32[]{:S(2)}) collective-permute-start(bf16[64,2048]{1,0:T(8,128)(2,1)S(1)} %mix.11.refs_2_.refs_0_), channel_id=1, source_target_pairs={{0,1},{1,0},{2,3},{3,2},{4,5},{5,4},{6,7},{7,6},{8,9},{9,8},{10,11... | collective-permute-start | bytes 786440 | tf_op jit(solution)/shard_map/mix/ppermute | solution.py:540
  86.2 6.7 %collective-permute-start.14 = (bf16[2,64,1024]{2,1,0:T(8,128)(2,1)S(1)}, bf16[2,64,1024]{2,1,0:T(8,128)(2,1)S(1)}, u32[]{:S(2)}, u32[]{:S(2)}) collective-permute-start(bf16[2,64,1024]{2,1,0:T(8,128)(2,1)S(1)} %get-tuple-element.44.refs_9_), channel_id=1, source_target_pairs={{0,4},{4,8},{8,12},{12,16},{16,20},{20,24},{24,28},{28,0},{1,5},{5... | collective-permute-start | bytes 786440 | tf_op jit(solution)/shard_map/project/ppermute | solution.py:526
  90.8 6.7 %collective-permute-start.15 = (bf16[2,64,1024]{2,1,0:T(8,128)(2,1)S(1)}, bf16[2,64,1024]{2,1,0:T(8,128)(2,1)S(1)}, u32[]{:S(2)}, u32[]{:S(2)}) collective-permute-start(bf16[2,64,1024]{2,1,0:T(8,128)(2,1)S(1)} %get-tuple-element.45.refs_10_), channel_id=1, source_target_pairs={{0,4},{4,8},{8,12},{12,16},{16,20},{20,24},{24,28},{28,0},{1,5},{5... | collective-permute-start | bytes 786440 | tf_op jit(solution)/shard_map/project/ppermute | solution.py:526

commit v7 on v6

--- a/solution.py
+++ b/solution.py
@@ -151,27 +151,22 @@
     return pltpu.with_memory_space_constraint(array, pltpu.VMEM)
 
 
-def state_body(qkv_ref, send_ref, keep_ref, k_ref, v_ref, sems):
+def state_body(other, qkv_ref, after, state_ref, k_ref, v_ref, sems):
     core = lax.axis_index("seq") % 2
-    count = send_ref.shape[0]
-    wide = k_ref.shape[2]
-    copies = []
-    for slot in range(2):
-        group = core if slot else 1 - core
-        pair = []
-        for plane, ref in ((1, k_ref), (2, v_ref)):
-            copy = pltpu.make_async_copy(
-                qkv_ref.at[plane, :, at(group * wide, wide)], ref.at[slot], sems.at[slot, plane - 1]
-            )
-            copy.start()
-            pair.append(copy)
-        copies.append(pair)
-    for slot, out in ((0, send_ref), (1, keep_ref)):
-        for copy in copies[slot]:
-            copy.wait()
-        for j in range(count):
-            head = slice(j * HD, (j + 1) * HD)
-            out[j] = dot_tn(k_ref[slot, :, head], v_ref[slot, :, head]).astype(BF16)
+    group = 1 - core if other else core
+    wide = k_ref.shape[1]
+    copies = start_all(
+        [
+            (qkv_ref.at[plane, :, at(group * wide, wide)], ref)
+            for plane, ref in ((1, k_ref), (2, v_ref))
+        ],
+        sems,
+    )
+    for copy in copies:
+        copy.wait()
+    for j in range(state_ref.shape[0]):
+        head = slice(j * HD, (j + 1) * HD)
+        state_ref[j] = dot_tn(k_ref[:, head], v_ref[:, head]).astype(BF16)
 
 
 def intra_body(qkv_ref, after, cos_ref, sin_ref, w_ref, o_ref, q_ref, w_other_ref, w_mine_ref, sems):
@@ -374,7 +369,7 @@
         logits = dot_nt(keys, stacked(q_refs, slice(None), head)) * SCORE
         logits = jnp.where(allowed, logits, NEG)
         top = jnp.max(logits, axis=0, keepdims=True)
-        expo = jnp.where(allowed, jnp.exp(logits - top), 0.0)
+        expo = jnp.exp(logits - top)
         top_ref[h : h + 1] = top
         sum_ref[h : h + 1] = jnp.sum(expo, axis=0, keepdims=True)
         acc_ref[h] = dot_tn(values, expo.astype(BF16))
@@ -392,7 +387,7 @@
     highest = jnp.concatenate([jnp.max(x, axis=0, keepdims=True) for x in logits], axis=0)
     top = jnp.maximum(top_ref[...], highest)
     fade = jnp.exp(top_ref[...] - top)
-    expo = [jnp.where(has_prev, jnp.exp(logits[h] - top[h : h + 1]), 0.0) for h in heads]
+    expo = [jnp.exp(logits[h] - top[h : h + 1]) for h in heads]
     sums = jnp.concatenate([jnp.sum(x, axis=0, keepdims=True) for x in expo], axis=0)
     inverse = 1.0 / (sum_ref[...] * fade + sums)
     fade = fade * inverse
@@ -432,15 +427,20 @@
 
     with jax.named_scope("state"):
         states = shape((group, HD, HD), BF16)
-        send, keep = call(
-            state_body, (in_hbm(qkv),), (states, states), [IN_HBM],
-            (
-                pltpu.VMEM((2, rows, width // 2), BF16),
-                pltpu.VMEM((2, rows, width // 2), BF16),
-                pltpu.SemaphoreType.DMA((2, 2)),
-            ),
-            flops=2 * rows * width * HD, moved=4 * rows * width,
-        )
+
+        def state(other, after):
+            return call(
+                functools.partial(state_body, other), (in_hbm(qkv), after), states, [IN_HBM, ANYWHERE],
+                (
+                    pltpu.VMEM((rows, width // 2), BF16),
+                    pltpu.VMEM((rows, width // 2), BF16),
+                    pltpu.SemaphoreType.DMA((2,)),
+                ),
+                flops=rows * width * HD, moved=2 * rows * width,
+            )
+
+        send = state(True, qkv)
+        keep = state(False, send)
         other = swapped(send, "seq", 1)
         chip_total = (keep.astype(F32) + other.astype(F32)).astype(BF16)
         by_x = swapped(chip_total, "seq", 2)

time: 101 us -> 101 us (level)
    pallas_call x18 -> x19, Pallas kernels: 34.9 us -> 35.9 us  [call(): pl.pallas_call(body, in_specs=in_specs or [ON_CHIP] * len(ins), out_specs...]
  transfers between devices with their start and end apart: 16 -> 16, of which waited for: 9 -> 8; matrix products, arithmetic and copies ran while one was open for 1% -> 1% of each run, Pallas kernels for 31% -> 32%
where the time goes in v7:
time: 101 us; the launch traced here: 99.1 us
  starting transfers between devices  36.7 us (36%)
  Pallas kernels  35.9 us (36%)
  waiting for transfers between devices  24.8 us (25%)
    pallas_call x19, Pallas kernels, call(): pl.pallas_call(body, in_specs=in_specs or [ON_CHIP] * len(ins), out_specs...  35.9 us
    ppermute x3, starting transfers between devices, tuned(): far.append(lax.ppermute(part, 'head', CROSS))  25.1 us
    ppermute x1, waiting for transfers between devices, tuned(): got += [lax.ppermute(send, 'head', PAIR) for send in sends]  6.63 us
    ppermute x3, waiting for transfers between devices, tuned(): far.append(lax.ppermute(part, 'head', CROSS))  6.01 us
    ppermute x3, starting transfers between devices, tuned(): rests += [lax.ppermute(totals[i], 'head', PAIR) for i in members]  5.22 us
    ppermute x1, waiting for transfers between devices, tuned(): got = [lax.ppermute(first_send, 'head', PAIR)]  4 us
    ppermute x5, starting transfers between devices, swapped(): lax.ppermute(array, axis, [(i, i ^ bits) for i in range(lax.axis_size(axi...  3.7 us
    ppermute x3, waiting for transfers between devices, turn(): prevs.append(lax.ppermute(kv, 'seq', ring))  2.86 us
  transfers between devices with their start and end apart: 16, of which 8 were waited for; matrix products, arithmetic and copies ran while one was open for 1% of the time, Pallas kernels for 32%

profile of v7, /device:TPU:4, one launch (start us, length us, event | category | flops | bytes accessed | tf_op | source)
XLA Modules:
  0.0 99.1 jit_solution(14960770899085099158)
XLA Ops:
  0.6 0.0 copy-start
  0.6 1.4 %state.2.after = bf16[4,128,128]{2,1,0:T(8,128)(2,1)S(1)} custom-call(bf16[3,256,1024]{2,1,0:T(8,128)(2,1)} %bitcast.2, bf16[3,256,1024]{2,1,0:T(8,128)(2,1)} %bitcast.3), custom_call_target="tpu_custom_call" | custom-call | tf_op jit(solution)/shard_map/state/pallas_call | solution.py:128
  2.1 0.1 collective-permute-start
  2.2 1.3 %state.3 = bf16[4,128,128]{2,1,0:T(8,128)(2,1)S(1)} custom-call(bf16[3,256,1024]{2,1,0:T(8,128)(2,1)} %bitcast.4, bf16[4,128,128]{2,1,0:T(8,128)(2,1)S(1)} %state.2.after), custom_call_target="tpu_custom_call" | custom-call | tf_op jit(solution)/shard_map/state/pallas_call | solution.py:128
  3.6 1.6 %collective-permute-start.1 = (bf16[4,128,128]{2,1,0:T(8,128)(2,1)S(1)}, bf16[4,128,128]{2,1,0:T(8,128)(2,1)S(1)}, u32[]{:S(2)}, u32[]{:S(2)}) collective-permute-start(bf16[4,128,128]{2,1,0:T(8,128)(2,1)S(1)} %add_convert_fusion.1.after), channel_id=1, source_target_pairs={{0,8},{4,12},{8,0},{12,4},{16,24},{20,28},{24,16},{28,20},{1,9},{5... | collective-permute-start | bytes 393224 | tf_op jit(solution)/shard_map/state/ppermute | solution.py:29
  5.2 0.5 collective-permute-start.2
  5.7 1.5 %collective-permute-start.3 = (bf16[4,128,128]{2,1,0:T(8,128)(2,1)S(1)}, bf16[4,128,128]{2,1,0:T(8,128)(2,1)S(1)}, u32[]{:S(2)}, u32[]{:S(2)}) collective-permute-start(bf16[4,128,128]{2,1,0:T(8,128)(2,1)S(1)} %add_convert_fusion.1.after), channel_id=1, source_target_pairs={{0,24},{4,28},{8,16},{12,20},{16,8},{20,12},{24,0},{28,4},{1,25},{... | collective-permute-start | bytes 393224 | tf_op jit(solution)/shard_map/state/ppermute | solution.py:29
  7.2 0.5 fusion.1
  7.7 0.1 pad_maximum_fusion
  7.9 4.4 %intra.1 = (f32[256,1024]{1,0:T(8,128)S(1)}, bf16[256,1024]{1,0:T(8,128)(2,1)S(1)}, bf16[2,1024,1024]{2,1,0:T(8,128)(2,1)S(1)}, bf16[2,1024,1024]{2,1,0:T(8,128)(2,1)S(1)}) custom-call(bf16[3,256,1024]{2,1,0:T(8,128)(2,1)S(1)} %bitcast.5, bf16[4,128,128]{2,1,0:T(8,128)(2,1)S(1)} %add_convert_fusion.1.after, ...), custom_call_target="tpu_custom_call" | custom-call | tf_op jit(solution)/shard_map/intra/pallas_call | solution.py:128
  12.3 0.0 copy-start.1
  12.3 1.2 %collective-permute-done.2 = bf16[4,128,128]{2,1,0:T(8,128)(2,1)S(1)} collective-permute-done((bf16[4,128,128]{2,1,0:T(8,128)(2,1)S(1)}, bf16[4,128,128]{2,1,0:T(8,128)(2,1)S(1)}, u32[]{:S(2)}, u32[]{:S(2)}) %collective-permute-start.2) | collective-permute-done | bytes 131104 | tf_op jit(solution)/shard_map/state/ppermute | solution.py:29
  13.6 0.1 broadcast_select_fusion
  13.7 0.1 collective-permute-start.4
  13.8 1.3 %collective-permute-done.4.other_ref.refs_3_ = bf16[4,128,128]{2,1,0:T(8,128)(2,1)S(1)} collective-permute-done((bf16[4,128,128]{2,1,0:T(8,128)(2,1)S(1)}, bf16[4,128,128]{2,1,0:T(8,128)(2,1)S(1)}, u32[]{:S(2)}, u32[]{:S(2)}) %collective-permute-start.4) | collective-permute-done | bytes 131104 | tf_op jit(solution)/shard_map/prefix/ppermute | solution.py:29
  15.1 0.9 partials.2.refs_8_
  16.1 1.6 %collective-permute-start.5 = (bf16[128,2048]{1,0:T(8,128)(2,1)S(1)}, bf16[128,2048]{1,0:T(8,128)(2,1)S(1)}, u32[]{:S(2)}, u32[]{:S(2)}) collective-permute-start(bf16[128,2048]{1,0:T(8,128)(2,1)S(1)} %partials.2.refs_8_), channel_id=1, source_target_pairs={{0,1},{1,0},{2,3},{3,2},{4,5},{5,4},{6,7},{7,6},{8,9},{9,8},{10,11... | collective-permute-start | bytes 1572872 | tf_op jit(solution)/shard_map/partials/ppermute | solution.py:479
  17.7 8.7 %partials.3 = (bf16[128,2048]{1,0:T(8,128)(2,1)S(1)}, bf16[128,2048]{1,0:T(8,128)(2,1)S(1)}, bf16[128,2048]{1,0:T(8,128)(2,1)S(1)}, bf16[3,4096,1024]{2,1,0:T(8,128)(2,1)S(1)}) custom-call(bf16[256,1024]{1,0:T(8,128)(2,1)S(1)} %get-tuple-element.24.q_ref.refs_0_, f32[256,1024]{1,0:T(8,128)S(1)} %get-tuple-element.25.intra_ref.refs_1_, ...), custom_call_target="tpu_custom_call" | custom-call | tf_op jit(solution)/shard_map/partials/pallas_call | solution.py:128
  26.4 0.5 collective-permute-start.7
  26.9 4.0 %collective-permute-done.5.refs_1_ = bf16[128,2048]{1,0:T(8,128)(2,1)S(1)} collective-permute-done((bf16[128,2048]{1,0:T(8,128)(2,1)S(1)}, bf16[128,2048]{1,0:T(8,128)(2,1)S(1)}, u32[]{:S(2)}, u32[]{:S(2)}) %collective-permute-start.5) | collective-permute-done | bytes 524320 | tf_op jit(solution)/shard_map/partials/ppermute | solution.py:479
  30.9 0.1 mix.6.refs_0_.refs_2_
  31.0 3.7 %collective-permute-start.6 = (bf16[128,2048]{1,0:T(8,128)(2,1)S(1)}, bf16[128,2048]{1,0:T(8,128)(2,1)S(1)}, u32[]{:S(2)}, u32[]{:S(2)}) collective-permute-start(bf16[128,2048]{1,0:T(8,128)(2,1)S(1)} %mix.6.refs_0_.refs_2_), channel_id=1, source_target_pairs={{0,3},{3,0},{1,2},{2,1},{4,7},{7,4},{5,6},{6,5},{8,11},{11,8},{9,1... | collective-permute-start | bytes 1572872 | tf_op jit(solution)/shard_map/mix/ppermute | solution.py:504
  34.7 6.6 %collective-permute-done.7.refs_1_ = bf16[128,2048]{1,0:T(8,128)(2,1)S(1)} collective-permute-done((bf16[128,2048]{1,0:T(8,128)(2,1)S(1)}, bf16[128,2048]{1,0:T(8,128)(2,1)S(1)}, u32[]{:S(2)}, u32[]{:S(2)}) %collective-permute-start.7) | collective-permute-done | bytes 524320 | tf_op jit(solution)/shard_map/mix/ppermute | solution.py:497
  41.3 0.1 mix.8.refs_2_.refs_0_
  41.4 17.7 %collective-permute-start.8 = (bf16[64,2048]{1,0:T(8,128)(2,1)S(1)}, bf16[64,2048]{1,0:T(8,128)(2,1)S(1)}, u32[]{:S(2)}, u32[]{:S(2)}) collective-permute-start(bf16[64,2048]{1,0:T(8,128)(2,1)S(1)} %mix.8.refs_2_.refs_0_), channel_id=1, source_target_pairs={{0,3},{3,0},{1,2},{2,1},{4,7},{7,4},{5,6},{6,5},{8,11},{11,8},{9,1... | collective-permute-start | bytes 786440 | tf_op jit(solution)/shard_map/mix/ppermute | solution.py:504
  59.1 0.1 mix.7.refs_2_.refs_0_
  59.3 1.2 %collective-permute-start.10 = (bf16[128,2048]{1,0:T(8,128)(2,1)S(1)}, bf16[128,2048]{1,0:T(8,128)(2,1)S(1)}, u32[]{:S(2)}, u32[]{:S(2)}) collective-permute-start(bf16[128,2048]{1,0:T(8,128)(2,1)S(1)} %mix.7.refs_2_.refs_0_), channel_id=1, source_target_pairs={{0,1},{1,0},{2,3},{3,2},{4,5},{5,4},{6,7},{7,6},{8,9},{9,8},{10,11... | collective-permute-start | bytes 1572872 | tf_op jit(solution)/shard_map/mix/ppermute | solution.py:540
  60.4 0.1 mix.9.refs_0_
  60.5 6.0 %collective-permute-done.8.refs_1_ = bf16[64,2048]{1,0:T(8,128)(2,1)S(1)} collective-permute-done((bf16[64,2048]{1,0:T(8,128)(2,1)S(1)}, bf16[64,2048]{1,0:T(8,128)(2,1)S(1)}, u32[]{:S(2)}, u32[]{:S(2)}) %collective-permute-start.8) | collective-permute-done | bytes 262176 | tf_op jit(solution)/shard_map/mix/ppermute | solution.py:504
  66.5 3.7 %collective-permute-start.9 = (bf16[64,2048]{1,0:T(8,128)(2,1)S(1)}, bf16[64,2048]{1,0:T(8,128)(2,1)S(1)}, u32[]{:S(2)}, u32[]{:S(2)}) collective-permute-start(bf16[64,2048]{1,0:T(8,128)(2,1)S(1)} %mix.9.refs_0_), channel_id=1, source_target_pairs={{0,3},{3,0},{1,2},{2,1},{4,7},{7,4},{5,6},{6,5},{8,11},{11,8},{9,1... | collective-permute-start | bytes 786440 | tf_op jit(solution)/shard_map/mix/ppermute | solution.py:504
  70.2 0.1 mix.10.refs_2_.refs_1_.refs_0_
  70.3 3.4 %collective-permute-start.11 = (bf16[64,2048]{1,0:T(8,128)(2,1)S(1)}, bf16[64,2048]{1,0:T(8,128)(2,1)S(1)}, u32[]{:S(2)}, u32[]{:S(2)}) collective-permute-start(bf16[64,2048]{1,0:T(8,128)(2,1)S(1)} %mix.10.refs_2_.refs_1_.refs_0_), channel_id=1, source_target_pairs={{0,1},{1,0},{2,3},{3,2},{4,5},{5,4},{6,7},{7,6},{8,9},{9,8},{10,11... | collective-permute-start | bytes 786440 | tf_op jit(solution)/shard_map/mix/ppermute | solution.py:540
  73.7 2.3 %project.8.refs_6_.refs_3_ = f32[3,64,1024]{2,1,0:T(8,128)S(1)} custom-call(bf16[3,4096,1024]{2,1,0:T(8,128)(2,1)S(1)} %get-tuple-element.28.w_ref.refs_2_.refs_0_, bf16[64,2048]{1,0:T(8,128)(2,1)S(1)} %mix.10.refs_2_.refs_1_.refs_0_), custom_call_target="tpu_custom_call" | custom-call | tf_op jit(solution)/shard_map/project/pallas_call | solution.py:128
  76.0 1.8 %project.7.refs_3_ = f32[3,128,1024]{2,1,0:T(8,128)S(1)} custom-call(bf16[3,4096,1024]{2,1,0:T(8,128)(2,1)S(1)} %get-tuple-element.28.w_ref.refs_2_.refs_0_, bf16[128,2048]{1,0:T(8,128)(2,1)S(1)} %mix.7.refs_2_.refs_0_), custom_call_target="tpu_custom_call" | custom-call | tf_op jit(solution)/shard_map/project/pallas_call | solution.py:128
  77.9 2.1 %project.9 = (bf16[2,128,1024]{2,1,0:T(8,128)(2,1)S(1)}, bf16[128,1024]{1,0:T(8,128)(2,1)S(1)}) custom-call(bf16[128,2048]{1,0:T(8,128)(2,1)S(1)} %mix.7.refs_2_.refs_0_, bf16[128,2048]{1,0:T(8,128)(2,1)S(1)} %collective-permute-done.10.refs_1_, bf16[3,4096,1024]{2,1,0:T(8,128)(2,1)S(1)} %get-tuple-element.28.w_ref.refs_2_.refs_0_, ...), custom_call_target="tpu_custom_call" | custom-call | tf_op jit(solution)/shard_map/project/pallas_call | solution.py:128
  80.0 0.2 collective-permute-start.13
  80.2 0.1 mix.11.refs_2_.refs_0_
  80.3 0.6 collective-permute-start.12
  80.9 3.0 %project.6 = (f32[3,64,1024]{2,1,0:T(8,128)S(1)}, bf16[256,1024]{1,0:T(8,128)(2,1)}) custom-call(bf16[3,4096,1024]{2,1,0:T(8,128)(2,1)S(1)} %get-tuple-element.28.w_ref.refs_2_.refs_0_, bf16[128,2048]{1,0:T(8,128)(2,1)S(1)} %mix.7.refs_2_.refs_0_, bf16[64,2048]{1,0:T(8,128)(2,1)S(1)} %mix.10.refs_2_.refs_1_.refs_0_, bf16[64,2048]{1,0:T(8,128)(2,1)S(1)} %mix.11.refs_2_.refs_0_), custom_call_target="tpu_custom_call" | custom-call | tf_op jit(solution)/shard_map/project/pallas_call | solution.py:128
  83.9 2.4 %project.10 = (bf16[2,64,1024]{2,1,0:T(8,128)(2,1)S(1)}, bf16[64,1024]{1,0:T(8,128)(2,1)S(1)}) custom-call(bf16[64,2048]{1,0:T(8,128)(2,1)S(1)} %mix.10.refs_2_.refs_1_.refs_0_, bf16[64,2048]{1,0:T(8,128)(2,1)S(1)} %collective-permute-done.11.refs_1_, bf16[3,4096,1024]{2,1,0:T(8,128)(2,1)S(1)} %get-tuple-element.28.w_ref.refs_2_.refs_0_, ...), custom_call_target="tpu_custom_call" | custom-call | tf_op jit(solution)/shard_map/project/pallas_call | solution.py:128
  86.3 0.2 collective-permute-start.14
  86.5 2.7 %collective-permute-done.12.refs_1_.refs_4_ = bf16[64,2048]{1,0:T(8,128)(2,1)S(1)} collective-permute-done((bf16[64,2048]{1,0:T(8,128)(2,1)S(1)}, bf16[64,2048]{1,0:T(8,128)(2,1)S(1)}, u32[]{:S(2)}, u32[]{:S(2)}) %collective-permute-start.12) | collective-permute-done | bytes 262176 | tf_op jit(solution)/shard_map/mix/ppermute | solution.py:540
  89.2 1.6 %project.11 = (bf16[2,64,1024]{2,1,0:T(8,128)(2,1)S(1)}, f32[64,128]{1,0:T(8,128)S(1)}) custom-call(bf16[64,2048]{1,0:T(8,128)(2,1)S(1)} %mix.11.refs_2_.refs_0_, bf16[64,2048]{1,0:T(8,128)(2,1)S(1)} %collective-permute-done.12.refs_1_.refs_4_, bf16[3,4096,1024]{2,1,0:T(8,128)(2,1)S(1)} %get-tuple-element.28.w_ref.refs_2_.refs_0_, ...), custom_call_target="tpu_custom_call" | custom-call | tf_op jit(solution)/shard_map/project/pallas_call | solution.py:128
  90.8 0.1 collective-permute-start.15
  90.9 2.2 %collective-permute-done.14.refs_12_ = bf16[2,64,1024]{2,1,0:T(8,128)(2,1)S(1)} collective-permute-done((bf16[2,64,1024]{2,1,0:T(8,128)(2,1)S(1)}, bf16[2,64,1024]{2,1,0:T(8,128)(2,1)S(1)}, u32[]{:S(2)}, u32[]{:S(2)}) %collective-permute-start.14) | collective-permute-done | bytes 262176 | tf_op jit(solution)/shard_map/project/ppermute | solution.py:526
  93.1 3.8 %attend.2 = (bf16[64,1024]{1,0:T(8,128)(2,1)S(1)}, f32[8,128,256]{2,1,0:T(8,128)S(1)}, f32[8,256]{1,0:T(8,128)S(1)}, f32[8,256]{1,0:T(8,128)S(1)}) custom-call(bf16[3,4096,1024]{2,1,0:T(8,128)(2,1)S(1)} %get-tuple-element.28.w_ref.refs_2_.refs_0_, f32[3,64,1024]{2,1,0:T(8,128)S(1)} %get-tuple-element.36.refs_6_.refs_3_.refs_1_, ...), custom_call_target="tpu_custom_call" | custom-call | tf_op jit(solution)/shard_map/attend/pallas_call | solution.py:128
  96.9 0.7 collective-permute-done.15.refs_3_
  97.6 1.6 %attend.3 = bf16[256,1024]{1,0:T(8,128)(2,1)} custom-call(bf16[128,1024]{1,0:T(8,128)(2,1)S(1)} %get-tuple-element.35.refs_6_.refs_0_, bf16[64,1024]{1,0:T(8,128)(2,1)S(1)} %get-tuple-element.37.refs_7_.refs_1_, bf16[64,1024]{1,0:T(8,128)(2,1)S(1)} %get-tuple-element.42.refs_2_, bf16[2,64,1024]{2,1,0:T(8,128)(2,1)S(1)} %collective-permute-done.15.refs_3_, ...), custom_call_target="tpu_custom_call" | custom-call | tf_op jit(solution)/shard_map/attend/pallas_call | solution.py:128
  (14 shorter events, 0.1 us)
Async XLA Ops:
  0.6 7.3 %copy-start = (bf16[256,3,1024]{2,0,1:T(8,128)(2,1)S(1)}, bf16[256,3,1024]{2,0,1:T(8,128)(2,1)}, u32[]{:S(2)}) copy-start(bf16[256,3,1024]{2,0,1:T(8,128)(2,1)} %param.4) | copy-start | bytes 4718596
  2.1 1.5 %collective-permute-start = (bf16[4,128,128]{2,1,0:T(8,128)(2,1)S(1)}, bf16[4,128,128]{2,1,0:T(8,128)(2,1)S(1)}, u32[]{:S(2)}, u32[]{:S(2)}) collective-permute-start(bf16[4,128,128]{2,1,0:T(8,128)(2,1)S(1)} %state.2.after), channel_id=1, source_target_pairs={{0,4},{4,0},{8,12},{12,8},{16,20},{20,16},{24,28},{28,24},{1,5},{5... | collective-permute-start | bytes 393224 | tf_op jit(solution)/shard_map/state/ppermute | solution.py:29
  3.6 8.7 %collective-permute-start.1 = (bf16[4,128,128]{2,1,0:T(8,128)(2,1)S(1)}, bf16[4,128,128]{2,1,0:T(8,128)(2,1)S(1)}, u32[]{:S(2)}, u32[]{:S(2)}) collective-permute-start(bf16[4,128,128]{2,1,0:T(8,128)(2,1)S(1)} %add_convert_fusion.1.after), channel_id=1, source_target_pairs={{0,8},{4,12},{8,0},{12,4},{16,24},{20,28},{24,16},{28,20},{1,9},{5... | collective-permute-start | bytes 393224 | tf_op jit(solution)/shard_map/state/ppermute | solution.py:29
  5.2 8.4 %collective-permute-start.2 = (bf16[4,128,128]{2,1,0:T(8,128)(2,1)S(1)}, bf16[4,128,128]{2,1,0:T(8,128)(2,1)S(1)}, u32[]{:S(2)}, u32[]{:S(2)}) collective-permute-start(bf16[4,128,128]{2,1,0:T(8,128)(2,1)S(1)} %add_convert_fusion.1.after), channel_id=1, source_target_pairs={{0,16},{4,20},{8,24},{12,28},{16,0},{20,4},{24,8},{28,12},{1,17},{... | collective-permute-start | bytes 393224 | tf_op jit(solution)/shard_map/state/ppermute | solution.py:29
  5.7 7.9 %collective-permute-start.3 = (bf16[4,128,128]{2,1,0:T(8,128)(2,1)S(1)}, bf16[4,128,128]{2,1,0:T(8,128)(2,1)S(1)}, u32[]{:S(2)}, u32[]{:S(2)}) collective-permute-start(bf16[4,128,128]{2,1,0:T(8,128)(2,1)S(1)} %add_convert_fusion.1.after), channel_id=1, source_target_pairs={{0,24},{4,28},{8,16},{12,20},{16,8},{20,12},{24,0},{28,4},{1,25},{... | collective-permute-start | bytes 393224 | tf_op jit(solution)/shard_map/state/ppermute | solution.py:29
  12.3 5.4 %copy-start.1 = (bf16[256,1024]{1,0:T(8,128)(2,1)S(1)}, bf16[256,1024]{1,0:T(8,128)(2,1)}, u32[]{:S(2)}) copy-start(bf16[256,1024]{1,0:T(8,128)(2,1)} %refs_6_.1) | copy-start | bytes 1572868
  13.7 1.4 %collective-permute-start.4 = (bf16[4,128,128]{2,1,0:T(8,128)(2,1)S(1)}, bf16[4,128,128]{2,1,0:T(8,128)(2,1)S(1)}, u32[]{:S(2)}, u32[]{:S(2)}) collective-permute-start(bf16[4,128,128]{2,1,0:T(8,128)(2,1)S(1)} %get-tuple-element.46), channel_id=1, source_target_pairs={{0,4},{4,0},{8,12},{12,8},{16,20},{20,16},{24,28},{28,24},{1,5},{5... | collective-permute-start | bytes 393224 | tf_op jit(solution)/shard_map/prefix/ppermute | solution.py:29
  16.1 14.8 %collective-permute-start.5 = (bf16[128,2048]{1,0:T(8,128)(2,1)S(1)}, bf16[128,2048]{1,0:T(8,128)(2,1)S(1)}, u32[]{:S(2)}, u32[]{:S(2)}) collective-permute-start(bf16[128,2048]{1,0:T(8,128)(2,1)S(1)} %partials.2.refs_8_), channel_id=1, source_target_pairs={{0,1},{1,0},{2,3},{3,2},{4,5},{5,4},{6,7},{7,6},{8,9},{9,8},{10,11... | collective-permute-start | bytes 1572872 | tf_op jit(solution)/shard_map/partials/ppermute | solution.py:479
  26.4 15.0 %collective-permute-start.7 = (bf16[128,2048]{1,0:T(8,128)(2,1)S(1)}, bf16[128,2048]{1,0:T(8,128)(2,1)S(1)}, u32[]{:S(2)}, u32[]{:S(2)}) collective-permute-start(bf16[128,2048]{1,0:T(8,128)(2,1)S(1)} %get-tuple-element.31), channel_id=1, source_target_pairs={{0,1},{1,0},{2,3},{3,2},{4,5},{5,4},{6,7},{7,6},{8,9},{9,8},{10,11... | collective-permute-start | bytes 1572872 | tf_op jit(solution)/shard_map/mix/ppermute | solution.py:497
  31.0 28.1 %collective-permute-start.6 = (bf16[128,2048]{1,0:T(8,128)(2,1)S(1)}, bf16[128,2048]{1,0:T(8,128)(2,1)S(1)}, u32[]{:S(2)}, u32[]{:S(2)}) collective-permute-start(bf16[128,2048]{1,0:T(8,128)(2,1)S(1)} %mix.6.refs_0_.refs_2_), channel_id=1, source_target_pairs={{0,3},{3,0},{1,2},{2,1},{4,7},{7,4},{5,6},{6,5},{8,11},{11,8},{9,1... | collective-permute-start | bytes 1572872 | tf_op jit(solution)/shard_map/mix/ppermute | solution.py:504
  41.4 25.1 %collective-permute-start.8 = (bf16[64,2048]{1,0:T(8,128)(2,1)S(1)}, bf16[64,2048]{1,0:T(8,128)(2,1)S(1)}, u32[]{:S(2)}, u32[]{:S(2)}) collective-permute-start(bf16[64,2048]{1,0:T(8,128)(2,1)S(1)} %mix.8.refs_2_.refs_0_), channel_id=1, source_target_pairs={{0,3},{3,0},{1,2},{2,1},{4,7},{7,4},{5,6},{6,5},{8,11},{11,8},{9,1... | collective-permute-start | bytes 786440 | tf_op jit(solution)/shard_map/mix/ppermute | solution.py:504
  59.3 18.6 %collective-permute-start.10 = (bf16[128,2048]{1,0:T(8,128)(2,1)S(1)}, bf16[128,2048]{1,0:T(8,128)(2,1)S(1)}, u32[]{:S(2)}, u32[]{:S(2)}) collective-permute-start(bf16[128,2048]{1,0:T(8,128)(2,1)S(1)} %mix.7.refs_2_.refs_0_), channel_id=1, source_target_pairs={{0,1},{1,0},{2,3},{3,2},{4,5},{5,4},{6,7},{7,6},{8,9},{9,8},{10,11... | collective-permute-start | bytes 1572872 | tf_op jit(solution)/shard_map/mix/ppermute | solution.py:540
  66.5 13.7 %collective-permute-start.9 = (bf16[64,2048]{1,0:T(8,128)(2,1)S(1)}, bf16[64,2048]{1,0:T(8,128)(2,1)S(1)}, u32[]{:S(2)}, u32[]{:S(2)}) collective-permute-start(bf16[64,2048]{1,0:T(8,128)(2,1)S(1)} %mix.9.refs_0_), channel_id=1, source_target_pairs={{0,3},{3,0},{1,2},{2,1},{4,7},{7,4},{5,6},{6,5},{8,11},{11,8},{9,1... | collective-permute-start | bytes 786440 | tf_op jit(solution)/shard_map/mix/ppermute | solution.py:504
  70.3 13.6 %collective-permute-start.11 = (bf16[64,2048]{1,0:T(8,128)(2,1)S(1)}, bf16[64,2048]{1,0:T(8,128)(2,1)S(1)}, u32[]{:S(2)}, u32[]{:S(2)}) collective-permute-start(bf16[64,2048]{1,0:T(8,128)(2,1)S(1)} %mix.10.refs_2_.refs_1_.refs_0_), channel_id=1, source_target_pairs={{0,1},{1,0},{2,3},{3,2},{4,5},{5,4},{6,7},{7,6},{8,9},{9,8},{10,11... | collective-permute-start | bytes 786440 | tf_op jit(solution)/shard_map/mix/ppermute | solution.py:540
  80.0 13.1 %collective-permute-start.13 = (bf16[2,128,1024]{2,1,0:T(8,128)(2,1)S(1)}, bf16[2,128,1024]{2,1,0:T(8,128)(2,1)S(1)}, u32[]{:S(2)}, u32[]{:S(2)}) collective-permute-start(bf16[2,128,1024]{2,1,0:T(8,128)(2,1)S(1)} %get-tuple-element.39.refs_8_), channel_id=1, source_target_pairs={{0,4},{4,8},{8,12},{12,16},{16,20},{20,24},{24,28},{28,0},{1,5},{5... | collective-permute-start | bytes 1572872 | tf_op jit(solution)/shard_map/project/ppermute | solution.py:526
  80.3 8.9 %collective-permute-start.12 = (bf16[64,2048]{1,0:T(8,128)(2,1)S(1)}, bf16[64,2048]{1,0:T(8,128)(2,1)S(1)}, u32[]{:S(2)}, u32[]{:S(2)}) collective-permute-start(bf16[64,2048]{1,0:T(8,128)(2,1)S(1)} %mix.11.refs_2_.refs_0_), channel_id=1, source_target_pairs={{0,1},{1,0},{2,3},{3,2},{4,5},{5,4},{6,7},{7,6},{8,9},{9,8},{10,11... | collective-permute-start | bytes 786440 | tf_op jit(solution)/shard_map/mix/ppermute | solution.py:540
  86.3 6.7 %collective-permute-start.14 = (bf16[2,64,1024]{2,1,0:T(8,128)(2,1)S(1)}, bf16[2,64,1024]{2,1,0:T(8,128)(2,1)S(1)}, u32[]{:S(2)}, u32[]{:S(2)}) collective-permute-start(bf16[2,64,1024]{2,1,0:T(8,128)(2,1)S(1)} %get-tuple-element.40.refs_9_), channel_id=1, source_target_pairs={{0,4},{4,8},{8,12},{12,16},{16,20},{20,24},{24,28},{28,0},{1,5},{5... | collective-permute-start | bytes 786440 | tf_op jit(solution)/shard_map/project/ppermute | solution.py:526
  90.8 6.7 %collective-permute-start.15 = (bf16[2,64,1024]{2,1,0:T(8,128)(2,1)S(1)}, bf16[2,64,1024]{2,1,0:T(8,128)(2,1)S(1)}, u32[]{:S(2)}, u32[]{:S(2)}) collective-permute-start(bf16[2,64,1024]{2,1,0:T(8,128)(2,1)S(1)} %get-tuple-element.41.refs_10_), channel_id=1, source_target_pairs={{0,4},{4,8},{8,12},{12,16},{16,20},{20,24},{24,28},{28,0},{1,5},{5... | collective-permute-start | bytes 786440 | tf_op jit(solution)/shard_map/project/ppermute | solution.py:526

commit v8 on v7

--- a/solution.py
+++ b/solution.py
@@ -298,13 +298,12 @@
             acc_ref[plane, :, to] = two_quarters(x, w_ref, plane, mine, to)
 
 
-def first_hidden_body(block, cuts, count, w_ref, *refs):
-    *total_refs, acc_ref, hidden_ref = refs
-    width = acc_ref.shape[2]
+def hidden_body(cuts, *refs):
+    *total_refs, hidden_ref = refs
+    width = hidden_ref.shape[1]
     own = at((lax.axis_index("head") // 2) * width, width)
     for (a, b), ref in zip(cuts, total_refs):
         hidden_ref[a:b] = ref[:, own]
-    first_body(block, w_ref, *total_refs[-count:], acc_ref)
 
 
 def finish(block, plane, x, w_ref, acc_ref, rows, inv, cos, sin, out_ref):
@@ -544,11 +543,9 @@
                 inputs = [totals[i] for i in members]
                 accs.append(call(functools.partial(first_body, block), (w_here, *inputs), acc))
                 continue
-            acc, hidden = call(
-                functools.partial(first_hidden_body, block, ends, len(members)), (w_here, *totals),
-                (acc, shape((rows, width), BF16)),
-            )
-            accs.append(acc)
+            inputs = [totals[i] for i in members]
+            accs.append(call(functools.partial(first_body, block), (w_here, *inputs), acc))
+            hidden = call(functools.partial(hidden_body, ends), totals, shape((rows, width), BF16))
     with jax.named_scope("project"):
         for group in turns[len(kvs) :]:
             turn(group)

time: 101 us -> 101 us (level)
    pallas_call x19 -> x20, Pallas kernels: 35.9 us -> 36 us  [call(): pl.pallas_call(body, in_specs=in_specs or [ON_CHIP] * len(ins), out_specs...]
where the time goes in v8:
time: 101 us; the launch traced here: 99.1 us
  starting transfers between devices  36.7 us (36%)
  Pallas kernels  36 us (36%)
  waiting for transfers between devices  24.6 us (24%)
    pallas_call x20, Pallas kernels, call(): pl.pallas_call(body, in_specs=in_specs or [ON_CHIP] * len(ins), out_specs...  36 us
    ppermute x3, starting transfers between devices, tuned(): far.append(lax.ppermute(part, 'head', CROSS))  25.1 us
    ppermute x1, waiting for transfers between devices, tuned(): got += [lax.ppermute(send, 'head', PAIR) for send in sends]  6.63 us
    ppermute x3, waiting for transfers between devices, tuned(): far.append(lax.ppermute(part, 'head', CROSS))  6.01 us
    ppermute x3, starting transfers between devices, tuned(): rests += [lax.ppermute(totals[i], 'head', PAIR) for i in members]  5.22 us
    ppermute x1, waiting for transfers between devices, tuned(): got = [lax.ppermute(first_send, 'head', PAIR)]  4 us
    ppermute x5, starting transfers between devices, swapped(): lax.ppermute(array, axis, [(i, i ^ bits) for i in range(lax.axis_size(axi...  3.7 us
    ppermute x3, waiting for transfers between devices, tuned(): rests += [lax.ppermute(totals[i], 'head', PAIR) for i in members]  3.4 us
  transfers between devices with their start and end apart: 16, of which 8 were waited for; matrix products, arithmetic and copies ran while one was open for 1% of the time, Pallas kernels for 32%

profile of v8, /device:TPU:4, one launch (start us, length us, event | category | flops | bytes accessed | tf_op | source)
XLA Modules:
  0.0 99.1 jit_solution(10899454253024049887)
XLA Ops:
  0.6 0.0 copy-start
  0.6 1.4 %state.2.after = bf16[4,128,128]{2,1,0:T(8,128)(2,1)S(1)} custom-call(bf16[3,256,1024]{2,1,0:T(8,128)(2,1)} %bitcast.2, bf16[3,256,1024]{2,1,0:T(8,128)(2,1)} %bitcast.3), custom_call_target="tpu_custom_call" | custom-call | tf_op jit(solution)/shard_map/state/pallas_call | solution.py:128
  2.1 0.1 collective-permute-start
  2.2 1.3 %state.3 = bf16[4,128,128]{2,1,0:T(8,128)(2,1)S(1)} custom-call(bf16[3,256,1024]{2,1,0:T(8,128)(2,1)} %bitcast.4, bf16[4,128,128]{2,1,0:T(8,128)(2,1)S(1)} %state.2.after), custom_call_target="tpu_custom_call" | custom-call | tf_op jit(solution)/shard_map/state/pallas_call | solution.py:128
  3.6 1.6 %collective-permute-start.1 = (bf16[4,128,128]{2,1,0:T(8,128)(2,1)S(1)}, bf16[4,128,128]{2,1,0:T(8,128)(2,1)S(1)}, u32[]{:S(2)}, u32[]{:S(2)}) collective-permute-start(bf16[4,128,128]{2,1,0:T(8,128)(2,1)S(1)} %add_convert_fusion.1.after), channel_id=1, source_target_pairs={{0,8},{4,12},{8,0},{12,4},{16,24},{20,28},{24,16},{28,20},{1,9},{5... | collective-permute-start | bytes 393224 | tf_op jit(solution)/shard_map/state/ppermute | solution.py:29
  5.2 0.5 collective-permute-start.2
  5.7 1.5 %collective-permute-start.3 = (bf16[4,128,128]{2,1,0:T(8,128)(2,1)S(1)}, bf16[4,128,128]{2,1,0:T(8,128)(2,1)S(1)}, u32[]{:S(2)}, u32[]{:S(2)}) collective-permute-start(bf16[4,128,128]{2,1,0:T(8,128)(2,1)S(1)} %add_convert_fusion.1.after), channel_id=1, source_target_pairs={{0,24},{4,28},{8,16},{12,20},{16,8},{20,12},{24,0},{28,4},{1,25},{... | collective-permute-start | bytes 393224 | tf_op jit(solution)/shard_map/state/ppermute | solution.py:29
  7.2 0.5 fusion.1
  7.7 0.1 pad_maximum_fusion
  7.9 4.4 %intra.1 = (f32[256,1024]{1,0:T(8,128)S(1)}, bf16[256,1024]{1,0:T(8,128)(2,1)S(1)}, bf16[2,1024,1024]{2,1,0:T(8,128)(2,1)S(1)}, bf16[2,1024,1024]{2,1,0:T(8,128)(2,1)S(1)}) custom-call(bf16[3,256,1024]{2,1,0:T(8,128)(2,1)S(1)} %bitcast.5, bf16[4,128,128]{2,1,0:T(8,128)(2,1)S(1)} %add_convert_fusion.1.after, ...), custom_call_target="tpu_custom_call" | custom-call | tf_op jit(solution)/shard_map/intra/pallas_call | solution.py:128
  12.3 1.2 %collective-permute-done.2 = bf16[4,128,128]{2,1,0:T(8,128)(2,1)S(1)} collective-permute-done((bf16[4,128,128]{2,1,0:T(8,128)(2,1)S(1)}, bf16[4,128,128]{2,1,0:T(8,128)(2,1)S(1)}, u32[]{:S(2)}, u32[]{:S(2)}) %collective-permute-start.2) | collective-permute-done | bytes 131104 | tf_op jit(solution)/shard_map/state/ppermute | solution.py:29
  13.6 0.1 broadcast_select_fusion
  13.7 0.1 collective-permute-start.4
  13.8 1.3 %collective-permute-done.4.other_ref.refs_3_ = bf16[4,128,128]{2,1,0:T(8,128)(2,1)S(1)} collective-permute-done((bf16[4,128,128]{2,1,0:T(8,128)(2,1)S(1)}, bf16[4,128,128]{2,1,0:T(8,128)(2,1)S(1)}, u32[]{:S(2)}, u32[]{:S(2)}) %collective-permute-start.4) | collective-permute-done | bytes 131104 | tf_op jit(solution)/shard_map/prefix/ppermute | solution.py:29
  15.1 0.9 partials.2.refs_8_
  16.1 1.6 %collective-permute-start.5 = (bf16[128,2048]{1,0:T(8,128)(2,1)S(1)}, bf16[128,2048]{1,0:T(8,128)(2,1)S(1)}, u32[]{:S(2)}, u32[]{:S(2)}) collective-permute-start(bf16[128,2048]{1,0:T(8,128)(2,1)S(1)} %partials.2.refs_8_), channel_id=1, source_target_pairs={{0,1},{1,0},{2,3},{3,2},{4,5},{5,4},{6,7},{7,6},{8,9},{9,8},{10,11... | collective-permute-start | bytes 1572872 | tf_op jit(solution)/shard_map/partials/ppermute | solution.py:478
  17.7 8.7 %partials.3 = (bf16[128,2048]{1,0:T(8,128)(2,1)S(1)}, bf16[128,2048]{1,0:T(8,128)(2,1)S(1)}, bf16[128,2048]{1,0:T(8,128)(2,1)S(1)}, bf16[3,4096,1024]{2,1,0:T(8,128)(2,1)S(1)}) custom-call(bf16[256,1024]{1,0:T(8,128)(2,1)S(1)} %get-tuple-element.22.q_ref.refs_0_, f32[256,1024]{1,0:T(8,128)S(1)} %get-tuple-element.23.intra_ref.refs_1_, ...), custom_call_target="tpu_custom_call" | custom-call | tf_op jit(solution)/shard_map/partials/pallas_call | solution.py:128
  26.4 0.5 collective-permute-start.7
  26.9 4.0 %collective-permute-done.5.refs_1_ = bf16[128,2048]{1,0:T(8,128)(2,1)S(1)} collective-permute-done((bf16[128,2048]{1,0:T(8,128)(2,1)S(1)}, bf16[128,2048]{1,0:T(8,128)(2,1)S(1)}, u32[]{:S(2)}, u32[]{:S(2)}) %collective-permute-start.5) | collective-permute-done | bytes 524320 | tf_op jit(solution)/shard_map/partials/ppermute | solution.py:478
  30.9 0.1 mix.6.refs_0_.refs_2_
  31.0 3.7 %collective-permute-start.6 = (bf16[128,2048]{1,0:T(8,128)(2,1)S(1)}, bf16[128,2048]{1,0:T(8,128)(2,1)S(1)}, u32[]{:S(2)}, u32[]{:S(2)}) collective-permute-start(bf16[128,2048]{1,0:T(8,128)(2,1)S(1)} %mix.6.refs_0_.refs_2_), channel_id=1, source_target_pairs={{0,3},{3,0},{1,2},{2,1},{4,7},{7,4},{5,6},{6,5},{8,11},{11,8},{9,1... | collective-permute-start | bytes 1572872 | tf_op jit(solution)/shard_map/mix/ppermute | solution.py:503
  34.7 6.6 %collective-permute-done.7.refs_1_ = bf16[128,2048]{1,0:T(8,128)(2,1)S(1)} collective-permute-done((bf16[128,2048]{1,0:T(8,128)(2,1)S(1)}, bf16[128,2048]{1,0:T(8,128)(2,1)S(1)}, u32[]{:S(2)}, u32[]{:S(2)}) %collective-permute-start.7) | collective-permute-done | bytes 524320 | tf_op jit(solution)/shard_map/mix/ppermute | solution.py:496
  41.3 0.1 mix.8.refs_2_.refs_0_
  41.4 17.7 %collective-permute-start.8 = (bf16[64,2048]{1,0:T(8,128)(2,1)S(1)}, bf16[64,2048]{1,0:T(8,128)(2,1)S(1)}, u32[]{:S(2)}, u32[]{:S(2)}) collective-permute-start(bf16[64,2048]{1,0:T(8,128)(2,1)S(1)} %mix.8.refs_2_.refs_0_), channel_id=1, source_target_pairs={{0,3},{3,0},{1,2},{2,1},{4,7},{7,4},{5,6},{6,5},{8,11},{11,8},{9,1... | collective-permute-start | bytes 786440 | tf_op jit(solution)/shard_map/mix/ppermute | solution.py:503
  59.1 0.1 mix.7.refs_2_.refs_0_
  59.3 1.2 %collective-permute-start.10 = (bf16[128,2048]{1,0:T(8,128)(2,1)S(1)}, bf16[128,2048]{1,0:T(8,128)(2,1)S(1)}, u32[]{:S(2)}, u32[]{:S(2)}) collective-permute-start(bf16[128,2048]{1,0:T(8,128)(2,1)S(1)} %mix.7.refs_2_.refs_0_), channel_id=1, source_target_pairs={{0,1},{1,0},{2,3},{3,2},{4,5},{5,4},{6,7},{7,6},{8,9},{9,8},{10,11... | collective-permute-start | bytes 1572872 | tf_op jit(solution)/shard_map/mix/ppermute | solution.py:539
  60.4 0.1 mix.9.refs_0_
  60.5 6.0 %collective-permute-done.8.refs_1_ = bf16[64,2048]{1,0:T(8,128)(2,1)S(1)} collective-permute-done((bf16[64,2048]{1,0:T(8,128)(2,1)S(1)}, bf16[64,2048]{1,0:T(8,128)(2,1)S(1)}, u32[]{:S(2)}, u32[]{:S(2)}) %collective-permute-start.8) | collective-permute-done | bytes 262176 | tf_op jit(solution)/shard_map/mix/ppermute | solution.py:503
  66.5 3.7 %collective-permute-start.9 = (bf16[64,2048]{1,0:T(8,128)(2,1)S(1)}, bf16[64,2048]{1,0:T(8,128)(2,1)S(1)}, u32[]{:S(2)}, u32[]{:S(2)}) collective-permute-start(bf16[64,2048]{1,0:T(8,128)(2,1)S(1)} %mix.9.refs_0_), channel_id=1, source_target_pairs={{0,3},{3,0},{1,2},{2,1},{4,7},{7,4},{5,6},{6,5},{8,11},{11,8},{9,1... | collective-permute-start | bytes 786440 | tf_op jit(solution)/shard_map/mix/ppermute | solution.py:503
  70.2 0.1 mix.10.refs_2_.refs_1_.refs_0_
  70.3 3.4 %collective-permute-start.11 = (bf16[64,2048]{1,0:T(8,128)(2,1)S(1)}, bf16[64,2048]{1,0:T(8,128)(2,1)S(1)}, u32[]{:S(2)}, u32[]{:S(2)}) collective-permute-start(bf16[64,2048]{1,0:T(8,128)(2,1)S(1)} %mix.10.refs_2_.refs_1_.refs_0_), channel_id=1, source_target_pairs={{0,1},{1,0},{2,3},{3,2},{4,5},{5,4},{6,7},{7,6},{8,9},{9,8},{10,11... | collective-permute-start | bytes 786440 | tf_op jit(solution)/shard_map/mix/ppermute | solution.py:539
  73.7 2.3 %project.9.refs_6_.refs_3_ = f32[3,64,1024]{2,1,0:T(8,128)S(1)} custom-call(bf16[3,4096,1024]{2,1,0:T(8,128)(2,1)S(1)} %get-tuple-element.31.w_ref.refs_2_.refs_0_, bf16[64,2048]{1,0:T(8,128)(2,1)S(1)} %mix.10.refs_2_.refs_1_.refs_0_), custom_call_target="tpu_custom_call" | custom-call | tf_op jit(solution)/shard_map/project/pallas_call | solution.py:128
  76.0 1.8 %project.8.refs_3_ = f32[3,128,1024]{2,1,0:T(8,128)S(1)} custom-call(bf16[3,4096,1024]{2,1,0:T(8,128)(2,1)S(1)} %get-tuple-element.31.w_ref.refs_2_.refs_0_, bf16[128,2048]{1,0:T(8,128)(2,1)S(1)} %mix.7.refs_2_.refs_0_), custom_call_target="tpu_custom_call" | custom-call | tf_op jit(solution)/shard_map/project/pallas_call | solution.py:128
  77.9 2.1 %project.10 = (bf16[2,128,1024]{2,1,0:T(8,128)(2,1)S(1)}, bf16[128,1024]{1,0:T(8,128)(2,1)S(1)}) custom-call(bf16[128,2048]{1,0:T(8,128)(2,1)S(1)} %mix.7.refs_2_.refs_0_, bf16[128,2048]{1,0:T(8,128)(2,1)S(1)} %collective-permute-done.10.refs_1_, bf16[3,4096,1024]{2,1,0:T(8,128)(2,1)S(1)} %get-tuple-element.31.w_ref.refs_2_.refs_0_, ...), custom_call_target="tpu_custom_call" | custom-call | tf_op jit(solution)/shard_map/project/pallas_call | solution.py:128
  80.0 0.2 collective-permute-start.13
  80.2 0.1 mix.11.refs_2_.refs_0_
  80.3 0.6 collective-permute-start.12
  80.9 2.3 %project.11.refs_6_.refs_3_.refs_1_ = f32[3,64,1024]{2,1,0:T(8,128)S(1)} custom-call(bf16[3,4096,1024]{2,1,0:T(8,128)(2,1)S(1)} %get-tuple-element.31.w_ref.refs_2_.refs_0_, bf16[64,2048]{1,0:T(8,128)(2,1)S(1)} %mix.11.refs_2_.refs_0_), custom_call_target="tpu_custom_call" | custom-call | tf_op jit(solution)/shard_map/project/pallas_call | solution.py:128
  83.2 2.4 %project.12 = (bf16[2,64,1024]{2,1,0:T(8,128)(2,1)S(1)}, bf16[64,1024]{1,0:T(8,128)(2,1)S(1)}) custom-call(bf16[64,2048]{1,0:T(8,128)(2,1)S(1)} %mix.10.refs_2_.refs_1_.refs_0_, bf16[64,2048]{1,0:T(8,128)(2,1)S(1)} %collective-permute-done.11.refs_1_, bf16[3,4096,1024]{2,1,0:T(8,128)(2,1)S(1)} %get-tuple-element.31.w_ref.refs_2_.refs_0_, ...), custom_call_target="tpu_custom_call" | custom-call | tf_op jit(solution)/shard_map/project/pallas_call | solution.py:128
  85.6 0.2 collective-permute-start.14
  85.8 3.4 %collective-permute-done.12.refs_1_.refs_4_ = bf16[64,2048]{1,0:T(8,128)(2,1)S(1)} collective-permute-done((bf16[64,2048]{1,0:T(8,128)(2,1)S(1)}, bf16[64,2048]{1,0:T(8,128)(2,1)S(1)}, u32[]{:S(2)}, u32[]{:S(2)}) %collective-permute-start.12) | collective-permute-done | bytes 262176 | tf_op jit(solution)/shard_map/mix/ppermute | solution.py:539
  89.2 1.6 %project.13 = (bf16[2,64,1024]{2,1,0:T(8,128)(2,1)S(1)}, f32[64,128]{1,0:T(8,128)S(1)}) custom-call(bf16[64,2048]{1,0:T(8,128)(2,1)S(1)} %mix.11.refs_2_.refs_0_, bf16[64,2048]{1,0:T(8,128)(2,1)S(1)} %collective-permute-done.12.refs_1_.refs_4_, bf16[3,4096,1024]{2,1,0:T(8,128)(2,1)S(1)} %get-tuple-element.31.w_ref.refs_2_.refs_0_, ...), custom_call_target="tpu_custom_call" | custom-call | tf_op jit(solution)/shard_map/project/pallas_call | solution.py:128
  90.8 0.1 collective-permute-start.15
  90.9 0.8 project.7
  91.7 0.8 collective-permute-done.14.refs_12_
  92.5 3.8 %attend.2 = (bf16[64,1024]{1,0:T(8,128)(2,1)S(1)}, f32[8,128,256]{2,1,0:T(8,128)S(1)}, f32[8,256]{1,0:T(8,128)S(1)}, f32[8,256]{1,0:T(8,128)S(1)}) custom-call(bf16[3,4096,1024]{2,1,0:T(8,128)(2,1)S(1)} %get-tuple-element.31.w_ref.refs_2_.refs_0_, f32[3,64,1024]{2,1,0:T(8,128)S(1)} %project.11.refs_6_.refs_3_.refs_1_, ...), custom_call_target="tpu_custom_call" | custom-call | tf_op jit(solution)/shard_map/attend/pallas_call | solution.py:128
  96.3 1.2 %collective-permute-done.15.refs_3_ = bf16[2,64,1024]{2,1,0:T(8,128)(2,1)S(1)} collective-permute-done((bf16[2,64,1024]{2,1,0:T(8,128)(2,1)S(1)}, bf16[2,64,1024]{2,1,0:T(8,128)(2,1)S(1)}, u32[]{:S(2)}, u32[]{:S(2)}) %collective-permute-start.15) | collective-permute-done | bytes 262176 | tf_op jit(solution)/shard_map/project/ppermute | solution.py:525
  97.6 1.6 %attend.3 = bf16[256,1024]{1,0:T(8,128)(2,1)} custom-call(bf16[128,1024]{1,0:T(8,128)(2,1)S(1)} %get-tuple-element.32.refs_6_.refs_0_, bf16[64,1024]{1,0:T(8,128)(2,1)S(1)} %get-tuple-element.33.refs_7_.refs_1_, bf16[64,1024]{1,0:T(8,128)(2,1)S(1)} %get-tuple-element.38.refs_2_, bf16[2,64,1024]{2,1,0:T(8,128)(2,1)S(1)} %collective-permute-done.15.refs_3_, ...), custom_call_target="tpu_custom_call" | custom-call | tf_op jit(solution)/shard_map/attend/pallas_call | solution.py:128
  (15 shorter events, 0.1 us)
Async XLA Ops:
  0.6 7.3 %copy-start = (bf16[256,3,1024]{2,0,1:T(8,128)(2,1)S(1)}, bf16[256,3,1024]{2,0,1:T(8,128)(2,1)}, u32[]{:S(2)}) copy-start(bf16[256,3,1024]{2,0,1:T(8,128)(2,1)} %param.4) | copy-start | bytes 4718596
  2.1 1.5 %collective-permute-start = (bf16[4,128,128]{2,1,0:T(8,128)(2,1)S(1)}, bf16[4,128,128]{2,1,0:T(8,128)(2,1)S(1)}, u32[]{:S(2)}, u32[]{:S(2)}) collective-permute-start(bf16[4,128,128]{2,1,0:T(8,128)(2,1)S(1)} %state.2.after), channel_id=1, source_target_pairs={{0,4},{4,0},{8,12},{12,8},{16,20},{20,16},{24,28},{28,24},{1,5},{5... | collective-permute-start | bytes 393224 | tf_op jit(solution)/shard_map/state/ppermute | solution.py:29
  3.6 8.7 %collective-permute-start.1 = (bf16[4,128,128]{2,1,0:T(8,128)(2,1)S(1)}, bf16[4,128,128]{2,1,0:T(8,128)(2,1)S(1)}, u32[]{:S(2)}, u32[]{:S(2)}) collective-permute-start(bf16[4,128,128]{2,1,0:T(8,128)(2,1)S(1)} %add_convert_fusion.1.after), channel_id=1, source_target_pairs={{0,8},{4,12},{8,0},{12,4},{16,24},{20,28},{24,16},{28,20},{1,9},{5... | collective-permute-start | bytes 393224 | tf_op jit(solution)/shard_map/state/ppermute | solution.py:29
  5.2 8.4 %collective-permute-start.2 = (bf16[4,128,128]{2,1,0:T(8,128)(2,1)S(1)}, bf16[4,128,128]{2,1,0:T(8,128)(2,1)S(1)}, u32[]{:S(2)}, u32[]{:S(2)}) collective-permute-start(bf16[4,128,128]{2,1,0:T(8,128)(2,1)S(1)} %add_convert_fusion.1.after), channel_id=1, source_target_pairs={{0,16},{4,20},{8,24},{12,28},{16,0},{20,4},{24,8},{28,12},{1,17},{... | collective-permute-start | bytes 393224 | tf_op jit(solution)/shard_map/state/ppermute | solution.py:29
  5.7 7.9 %collective-permute-start.3 = (bf16[4,128,128]{2,1,0:T(8,128)(2,1)S(1)}, bf16[4,128,128]{2,1,0:T(8,128)(2,1)S(1)}, u32[]{:S(2)}, u32[]{:S(2)}) collective-permute-start(bf16[4,128,128]{2,1,0:T(8,128)(2,1)S(1)} %add_convert_fusion.1.after), channel_id=1, source_target_pairs={{0,24},{4,28},{8,16},{12,20},{16,8},{20,12},{24,0},{28,4},{1,25},{... | collective-permute-start | bytes 393224 | tf_op jit(solution)/shard_map/state/ppermute | solution.py:29
  12.3 5.4 %copy-start.1 = (bf16[256,1024]{1,0:T(8,128)(2,1)S(1)}, bf16[256,1024]{1,0:T(8,128)(2,1)}, u32[]{:S(2)}) copy-start(bf16[256,1024]{1,0:T(8,128)(2,1)} %refs_6_.1) | copy-start | bytes 1572868
  13.7 1.4 %collective-permute-start.4 = (bf16[4,128,128]{2,1,0:T(8,128)(2,1)S(1)}, bf16[4,128,128]{2,1,0:T(8,128)(2,1)S(1)}, u32[]{:S(2)}, u32[]{:S(2)}) collective-permute-start(bf16[4,128,128]{2,1,0:T(8,128)(2,1)S(1)} %get-tuple-element.42), channel_id=1, source_target_pairs={{0,4},{4,0},{8,12},{12,8},{16,20},{20,16},{24,28},{28,24},{1,5},{5... | collective-permute-start | bytes 393224 | tf_op jit(solution)/shard_map/prefix/ppermute | solution.py:29
  16.1 14.8 %collective-permute-start.5 = (bf16[128,2048]{1,0:T(8,128)(2,1)S(1)}, bf16[128,2048]{1,0:T(8,128)(2,1)S(1)}, u32[]{:S(2)}, u32[]{:S(2)}) collective-permute-start(bf16[128,2048]{1,0:T(8,128)(2,1)S(1)} %partials.2.refs_8_), channel_id=1, source_target_pairs={{0,1},{1,0},{2,3},{3,2},{4,5},{5,4},{6,7},{7,6},{8,9},{9,8},{10,11... | collective-permute-start | bytes 1572872 | tf_op jit(solution)/shard_map/partials/ppermute | solution.py:478
  26.4 15.0 %collective-permute-start.7 = (bf16[128,2048]{1,0:T(8,128)(2,1)S(1)}, bf16[128,2048]{1,0:T(8,128)(2,1)S(1)}, u32[]{:S(2)}, u32[]{:S(2)}) collective-permute-start(bf16[128,2048]{1,0:T(8,128)(2,1)S(1)} %get-tuple-element.28), channel_id=1, source_target_pairs={{0,1},{1,0},{2,3},{3,2},{4,5},{5,4},{6,7},{7,6},{8,9},{9,8},{10,11... | collective-permute-start | bytes 1572872 | tf_op jit(solution)/shard_map/mix/ppermute | solution.py:496
  31.0 28.1 %collective-permute-start.6 = (bf16[128,2048]{1,0:T(8,128)(2,1)S(1)}, bf16[128,2048]{1,0:T(8,128)(2,1)S(1)}, u32[]{:S(2)}, u32[]{:S(2)}) collective-permute-start(bf16[128,2048]{1,0:T(8,128)(2,1)S(1)} %mix.6.refs_0_.refs_2_), channel_id=1, source_target_pairs={{0,3},{3,0},{1,2},{2,1},{4,7},{7,4},{5,6},{6,5},{8,11},{11,8},{9,1... | collective-permute-start | bytes 1572872 | tf_op jit(solution)/shard_map/mix/ppermute | solution.py:503
  41.4 25.1 %collective-permute-start.8 = (bf16[64,2048]{1,0:T(8,128)(2,1)S(1)}, bf16[64,2048]{1,0:T(8,128)(2,1)S(1)}, u32[]{:S(2)}, u32[]{:S(2)}) collective-permute-start(bf16[64,2048]{1,0:T(8,128)(2,1)S(1)} %mix.8.refs_2_.refs_0_), channel_id=1, source_target_pairs={{0,3},{3,0},{1,2},{2,1},{4,7},{7,4},{5,6},{6,5},{8,11},{11,8},{9,1... | collective-permute-start | bytes 786440 | tf_op jit(solution)/shard_map/mix/ppermute | solution.py:503
  59.3 18.6 %collective-permute-start.10 = (bf16[128,2048]{1,0:T(8,128)(2,1)S(1)}, bf16[128,2048]{1,0:T(8,128)(2,1)S(1)}, u32[]{:S(2)}, u32[]{:S(2)}) collective-permute-start(bf16[128,2048]{1,0:T(8,128)(2,1)S(1)} %mix.7.refs_2_.refs_0_), channel_id=1, source_target_pairs={{0,1},{1,0},{2,3},{3,2},{4,5},{5,4},{6,7},{7,6},{8,9},{9,8},{10,11... | collective-permute-start | bytes 1572872 | tf_op jit(solution)/shard_map/mix/ppermute | solution.py:539
  66.5 13.7 %collective-permute-start.9 = (bf16[64,2048]{1,0:T(8,128)(2,1)S(1)}, bf16[64,2048]{1,0:T(8,128)(2,1)S(1)}, u32[]{:S(2)}, u32[]{:S(2)}) collective-permute-start(bf16[64,2048]{1,0:T(8,128)(2,1)S(1)} %mix.9.refs_0_), channel_id=1, source_target_pairs={{0,3},{3,0},{1,2},{2,1},{4,7},{7,4},{5,6},{6,5},{8,11},{11,8},{9,1... | collective-permute-start | bytes 786440 | tf_op jit(solution)/shard_map/mix/ppermute | solution.py:503
  70.3 12.9 %collective-permute-start.11 = (bf16[64,2048]{1,0:T(8,128)(2,1)S(1)}, bf16[64,2048]{1,0:T(8,128)(2,1)S(1)}, u32[]{:S(2)}, u32[]{:S(2)}) collective-permute-start(bf16[64,2048]{1,0:T(8,128)(2,1)S(1)} %mix.10.refs_2_.refs_1_.refs_0_), channel_id=1, source_target_pairs={{0,1},{1,0},{2,3},{3,2},{4,5},{5,4},{6,7},{7,6},{8,9},{9,8},{10,11... | collective-permute-start | bytes 786440 | tf_op jit(solution)/shard_map/mix/ppermute | solution.py:539
  80.0 12.6 %collective-permute-start.13 = (bf16[2,128,1024]{2,1,0:T(8,128)(2,1)S(1)}, bf16[2,128,1024]{2,1,0:T(8,128)(2,1)S(1)}, u32[]{:S(2)}, u32[]{:S(2)}) collective-permute-start(bf16[2,128,1024]{2,1,0:T(8,128)(2,1)S(1)} %get-tuple-element.35.refs_8_), channel_id=1, source_target_pairs={{0,4},{4,8},{8,12},{12,16},{16,20},{20,24},{24,28},{28,0},{1,5},{5... | collective-permute-start | bytes 1572872 | tf_op jit(solution)/shard_map/project/ppermute | solution.py:525
  80.3 8.9 %collective-permute-start.12 = (bf16[64,2048]{1,0:T(8,128)(2,1)S(1)}, bf16[64,2048]{1,0:T(8,128)(2,1)S(1)}, u32[]{:S(2)}, u32[]{:S(2)}) collective-permute-start(bf16[64,2048]{1,0:T(8,128)(2,1)S(1)} %mix.11.refs_2_.refs_0_), channel_id=1, source_target_pairs={{0,1},{1,0},{2,3},{3,2},{4,5},{5,4},{6,7},{7,6},{8,9},{9,8},{10,11... | collective-permute-start | bytes 786440 | tf_op jit(solution)/shard_map/mix/ppermute | solution.py:539
  85.6 6.9 %collective-permute-start.14 = (bf16[2,64,1024]{2,1,0:T(8,128)(2,1)S(1)}, bf16[2,64,1024]{2,1,0:T(8,128)(2,1)S(1)}, u32[]{:S(2)}, u32[]{:S(2)}) collective-permute-start(bf16[2,64,1024]{2,1,0:T(8,128)(2,1)S(1)} %get-tuple-element.36.refs_9_), channel_id=1, source_target_pairs={{0,4},{4,8},{8,12},{12,16},{16,20},{20,24},{24,28},{28,0},{1,5},{5... | collective-permute-start | bytes 786440 | tf_op jit(solution)/shard_map/project/ppermute | solution.py:525
  90.8 6.7 %collective-permute-start.15 = (bf16[2,64,1024]{2,1,0:T(8,128)(2,1)S(1)}, bf16[2,64,1024]{2,1,0:T(8,128)(2,1)S(1)}, u32[]{:S(2)}, u32[]{:S(2)}) collective-permute-start(bf16[2,64,1024]{2,1,0:T(8,128)(2,1)S(1)} %get-tuple-element.37.refs_10_), channel_id=1, source_target_pairs={{0,4},{4,8},{8,12},{12,16},{16,20},{20,24},{24,28},{28,0},{1,5},{5... | collective-permute-start | bytes 786440 | tf_op jit(solution)/shard_map/project/ppermute | solution.py:525
